TPU v7x, 32 devices: a whole 2x2x4 slice. The times are simulated.
32 devices in a mesh: dp: 8 (over y, x, core), mp: 4 (over z).
Axes of the slice: x: 2, y: 2, z: 4, core: 2. Of those that a mesh axis runs over, the one named last changes fastest.
Arguments:
- layer_in: bfloat16 [32, 1024, 512], P('dp'), may hold values from -6 to 6
- doc_ids: int32 [32, 1024], P('dp'), may hold values from 0 to 3, never falling along the last dimension, each value on 1 to 512 neighbouring positions
- out_grad: float32 [32, 1024, 512], P('dp', 'mp'), may hold values from -13 to 13
- w_query: float32 [512, 512], P(None, 'mp'), may hold values from -0.25 to 0.25
- w_key: float32 [512, 512], P(None, 'mp'), may hold values from -0.25 to 0.25
- w_value: float32 [512, 512], P(None, 'mp'), may hold values from -0.25 to 0.25
- w_output: float32 [512, 512], P('mp')
- w_expand: float32 [2048, 512], P('mp'), may hold values from -0.25 to 0.25
- w_contract: float32 [2048, 512], P('mp'), may hold values from -0.125 to 0.125
- small_params: float32 [2562], replicated, may hold values from -2.5 to 2.5
- buffer_query: float32 [512, 512], P(None, 'mp')
- buffer_key: float32 [512, 512], P(None, 'mp')
- buffer_value: float32 [512, 512], P(None, 'mp')
- buffer_output: float32 [512, 512], P('mp')
- buffer_expand: float32 [2048, 512], P('mp')
- buffer_contract: float32 [2048, 512], P('mp')
- small_first: float32 [2562], replicated
- small_second: float32 [2562], replicated, as said below
Outputs:
- layer_out: float32 [32, 1024, 512], P('dp', 'mp')
- in_grad: float32 [32, 1024, 512], P('dp', 'mp')
- new_buffer_query: float32 [512, 512], P(None, 'mp')
- new_buffer_key: float32 [512, 512], P(None, 'mp')
- new_buffer_value: float32 [512, 512], P(None, 'mp')
- new_buffer_output: float32 [512, 512], P('mp')
- new_buffer_expand: float32 [2048, 512], P('mp')
- new_buffer_contract: float32 [2048, 512], P('mp')
- new_w_query: float32 [512, 512], P(None, 'mp')
- new_w_key: float32 [512, 512], P(None, 'mp')
- new_w_value: float32 [512, 512], P(None, 'mp')
- new_w_output: float32 [512, 512], P('mp')
- new_w_expand: float32 [2048, 512], P('mp')
- new_w_contract: float32 [2048, 512], P('mp')
- new_small_params: float32 [2562], replicated
- new_small_first: float32 [2562], replicated
- new_small_second: float32 [2562], replicated
Inputs may be any that keep to these rules, and one draw needn't show every extreme that they name: `doc_ids`: along each row the document numbers never fall; a document covers 1 to 512 positions, and one covers exactly 512. `small_second`: every entry is positive.
All inputs are finite; a program needn't handle non-finite values.
Results may differ from a plain program's by a relative error of at most 0.029.
Values may be sent and summed in bfloat16 or wider, within the bound.
No kernel may reach another device: no remote copies, remote signals or barrier semaphores. Data moves between devices by JAX's collectives and lax.ppermute only.
A program may use at most 192 MiB of HBM per device.

v0:
```python
import jax
import jax.numpy as jnp
from jax import lax
from jax.sharding import PartitionSpec as P

D = 512
HEAD_DIM = 64
FF = 2048
MICRO = 2
STEP = 10


newton_one = 3.4445
newton_two = -4.775
newton_three = 2.0315
muon_rates = (1.0, 1.0, 1.0, 5.0, 2.0, 1.0)
adam_rate = 0.25
mask_fill = -1e30
highest_precision = lax.Precision.HIGHEST


def shortened(x):
    return jax.tree.map(lambda a: a.astype(jnp.bfloat16) if a.dtype == jnp.float32 else a, x)


def gelu_tanh(values):
    return jax.nn.gelu(values, approximate=True)


def block_scores(query_blk, key_part, docs_query, docs_key, first_row):
    scores = jnp.einsum(
        "sqhd,skhd->shqk", query_blk, key_part, preferred_element_type=jnp.float32
    ) * HEAD_DIM ** (-0.5)
    rows_at = first_row + jnp.arange(query_blk.shape[1])
    cols_at = jnp.arange(key_part.shape[1])
    allowed = (rows_at[:, None] >= cols_at[None, :])[None] & (
        docs_query[:, :, None] == docs_key[:, None, :]
    )
    return jnp.where(allowed[:, None], scores, mask_fill)


def attend(query_all, key_all, value_all, documents, span_rows):
    block_outs = []
    log_sums = []
    for block_index in range(query_all.shape[1] // span_rows):
        row_start = block_index * span_rows
        finish = row_start + span_rows
        scores = block_scores(
            query_all[:, row_start:finish],
            key_all[:, :finish],
            documents[:, row_start:finish],
            documents[:, :finish],
            row_start,
        )
        row_peak = jnp.max(scores, axis=-1, keepdims=True)
        exponent = jnp.exp(scores - row_peak)
        row_total = jnp.sum(exponent, axis=-1, keepdims=True)
        prob_low = (exponent / row_total).astype(jnp.bfloat16)
        block_outs.append(
            jnp.einsum(
                "shqk,skhd->sqhd",
                prob_low,
                value_all[:, :finish],
                preferred_element_type=jnp.float32,
            ).astype(jnp.bfloat16)
        )
        log_sums.append(row_peak + jnp.log(row_total))
    return (jnp.concatenate(block_outs, 1), log_sums)


def attend_back(query_all, key_all, value_all, documents, span_rows, log_sums, heads_grad):
    query_grads = []
    key_grad = jnp.zeros(key_all.shape, jnp.float32)
    value_grad = jnp.zeros(value_all.shape, jnp.float32)
    scale = HEAD_DIM ** (-0.5)
    for block_index in range(query_all.shape[1] // span_rows):
        row_start = block_index * span_rows
        finish = row_start + span_rows
        query_blk = query_all[:, row_start:finish]
        scores = block_scores(
            query_blk,
            key_all[:, :finish],
            documents[:, row_start:finish],
            documents[:, :finish],
            row_start,
        )
        probs = jnp.exp(scores - log_sums[block_index])
        prob_low = probs.astype(jnp.bfloat16)
        grad_blk = heads_grad[:, row_start:finish]
        grad_probs = jnp.einsum(
            "sqhd,skhd->shqk", grad_blk, value_all[:, :finish], preferred_element_type=jnp.float32
        )
        row_delta = jnp.sum(probs * grad_probs, axis=-1, keepdims=True)
        grad_scores = (probs * (grad_probs - row_delta)).astype(jnp.bfloat16)
        query_grads.append(
            jnp.einsum(
                "shqk,skhd->sqhd",
                grad_scores,
                key_all[:, :finish],
                preferred_element_type=jnp.float32,
            )
            * scale
        )
        key_grad = key_grad.at[:, :finish].add(
            jnp.einsum(
                "shqk,sqhd->skhd", grad_scores, query_blk, preferred_element_type=jnp.float32
            )
            * scale
        )
        value_grad = value_grad.at[:, :finish].add(
            jnp.einsum("shqk,sqhd->skhd", prob_low, grad_blk, preferred_element_type=jnp.float32)
        )
    return (jnp.concatenate(query_grads, 1), key_grad, value_grad)


def gram_part(iterate, by_columns):
    if by_columns:
        return lax.dot_general(
            iterate,
            iterate,
            (((1,), (1,)), ((), ())),
            precision=highest_precision,
            preferred_element_type=jnp.float32,
        )
    return lax.dot_general(
        iterate,
        iterate,
        (((0,), (0,)), ((), ())),
        precision=highest_precision,
        preferred_element_type=jnp.float32,
    )


def newton_update(iterate, gram_sum, by_columns):
    square = jnp.dot(gram_sum, gram_sum, precision=highest_precision)
    polynomial = newton_two * gram_sum + newton_three * square
    if by_columns:
        applied = jnp.dot(polynomial, iterate, precision=highest_precision)
    else:
        applied = lax.dot_general(
            iterate,
            polynomial,
            (((1,), (1,)), ((), ())),
            precision=highest_precision,
            preferred_element_type=jnp.float32,
        )
    return newton_one * iterate + applied


def shards(
    layer_in,
    doc_ids,
    out_grad,
    w_query,
    w_key,
    w_value,
    w_output,
    w_expand,
    w_contract,
    small_params,
    buffer_query,
    buffer_key,
    buffer_value,
    buffer_output,
    buffer_expand,
    buffer_contract,
    small_first,
    small_second,
):
    group_count = lax.axis_size("mp")
    group_index = lax.axis_index("mp")
    seq_count, length, model_width = layer_in.shape
    per_micro = seq_count // MICRO
    token_span = length // group_count
    head_cols = w_query.shape[1]
    heads_here = head_cols // HEAD_DIM
    span_rows = min(512, length)
    expansion_bias = small_params[:FF]
    contraction_bias = small_params[FF : FF + D]
    alpha_attend = small_params[FF + D]
    alpha_ffn = small_params[FF + D + 1]
    query_key_value_weight = jnp.concatenate((w_query, w_key, w_value), 1).astype(jnp.bfloat16)
    row_local = (
        w_output.astype(jnp.bfloat16),
        w_expand.astype(jnp.bfloat16),
        w_contract.astype(jnp.bfloat16),
    )
    grad_qkv_weight = jnp.zeros((model_width, 3 * head_cols), jnp.float32)
    grad_output = jnp.zeros((D, D), jnp.float32)
    grad_expand = jnp.zeros((FF, D), jnp.float32)
    grad_contract = jnp.zeros((FF, D), jnp.float32)
    grad_bias_expand = jnp.zeros((FF,), jnp.float32)
    grad_bias_contract = jnp.zeros((D,), jnp.float32)
    grad_alpha_attend = jnp.zeros((), jnp.float32)
    grad_alpha_ffn = jnp.zeros((), jnp.float32)
    out_blocks = []
    grad_blocks = []
    for micro_index in range(MICRO):
        rows_from = micro_index * per_micro
        layer_inputs = layer_in[rows_from : rows_from + per_micro]
        documents = doc_ids[rows_from : rows_from + per_micro]
        upstream = out_grad[rows_from : rows_from + per_micro]
        query_key_value_rows = jnp.einsum(
            "orv,vx->orx", layer_inputs, query_key_value_weight, preferred_element_type=jnp.float32
        ).astype(jnp.bfloat16)
        qkv_split = query_key_value_rows.reshape(per_micro, length, 3, heads_here, HEAD_DIM)
        query_all = qkv_split[:, :, 0]
        key_all = qkv_split[:, :, 1]
        value_all = qkv_split[:, :, 2]
        head_outputs, log_sums = attend(query_all, key_all, value_all, documents, span_rows)
        heads_flat = head_outputs.reshape(per_micro, length, head_cols)
        heads_tok = lax.all_to_all(heads_flat, "mp", split_axis=1, concat_axis=2, tiled=True)
        row_now = (
            lax.all_gather(row_local[0], "mp", axis=0, tiled=True),
            lax.all_gather(row_local[1], "mp", axis=0, tiled=True),
            lax.all_gather(row_local[2], "mp", axis=0, tiled=True),
        )
        output_full, expand_full, contract_full = row_now
        attention_result = jnp.einsum(
            "std,de->ste", heads_tok, output_full, preferred_element_type=jnp.float32
        )
        local_in = lax.dynamic_slice_in_dim(
            layer_inputs, group_index * token_span, token_span, 1
        ).astype(jnp.float32)
        middle_activation = local_in + alpha_attend * attention_result
        middle_low = middle_activation.astype(jnp.bfloat16)
        preactivation = (
            jnp.einsum("std,fd->stf", middle_low, expand_full, preferred_element_type=jnp.float32)
            + expansion_bias
        )
        hidden_state, gelu_back = jax.vjp(gelu_tanh, preactivation)
        hidden_low = hidden_state.astype(jnp.bfloat16)
        residual_branch = (
            jnp.einsum("stf,fd->std", hidden_low, contract_full, preferred_element_type=jnp.float32)
            + contraction_bias
        )
        out_blocks.append(middle_activation + alpha_ffn * residual_branch)
        grad_alpha_ffn = grad_alpha_ffn + jnp.sum(upstream * residual_branch)
        branch_grad = (alpha_ffn * upstream).astype(jnp.bfloat16)
        grad_bias_contract = grad_bias_contract + jnp.sum(
            branch_grad, axis=(0, 1), dtype=jnp.float32
        )
        grad_contract = grad_contract + jnp.einsum(
            "stf,std->fd", hidden_low, branch_grad, preferred_element_type=jnp.float32
        )
        hidden_grad = jnp.einsum(
            "std,fd->stf", branch_grad, contract_full, preferred_element_type=jnp.float32
        )
        pre_grad = gelu_back(hidden_grad)[0].astype(jnp.bfloat16)
        grad_bias_expand = grad_bias_expand + jnp.sum(pre_grad, axis=(0, 1), dtype=jnp.float32)
        grad_expand = grad_expand + jnp.einsum(
            "stf,std->fd", pre_grad, middle_low, preferred_element_type=jnp.float32
        )
        middle_grad = upstream + jnp.einsum(
            "stf,fd->std", pre_grad, expand_full, preferred_element_type=jnp.float32
        )
        grad_alpha_attend = grad_alpha_attend + jnp.sum(middle_grad * attention_result)
        attend_grad = (alpha_attend * middle_grad).astype(jnp.bfloat16)
        grad_output = grad_output + jnp.einsum(
            "std,ste->de", heads_tok, attend_grad, preferred_element_type=jnp.float32
        )
        heads_grad_tok = jnp.einsum(
            "ste,de->std", attend_grad, output_full, preferred_element_type=jnp.float32
        ).astype(jnp.bfloat16)
        heads_grad = lax.all_to_all(heads_grad_tok, "mp", split_axis=2, concat_axis=1, tiled=True)
        heads_grad = heads_grad.reshape(per_micro, length, heads_here, HEAD_DIM)
        query_grad, key_grad, value_grad = attend_back(
            query_all, key_all, value_all, documents, span_rows, log_sums, heads_grad
        )
        query_key_value_gradient = (
            jnp.stack((query_grad, key_grad, value_grad), 2)
            .reshape(per_micro, length, 3 * head_cols)
            .astype(jnp.bfloat16)
        )
        grad_qkv_weight = grad_qkv_weight + jnp.einsum(
            "tmf,tmp->fp",
            layer_inputs,
            query_key_value_gradient,
            preferred_element_type=jnp.float32,
        )
        partial_grad = jnp.einsum(
            "nrj,yj->nry",
            query_key_value_gradient,
            query_key_value_weight,
            preferred_element_type=jnp.float32,
        )
        head_part = lax.psum_scatter(
            partial_grad.astype(jnp.bfloat16), "mp", scatter_dimension=1, tiled=True
        ).astype(jnp.float32)
        grad_blocks.append(middle_grad + head_part)
    layer_out = jnp.concatenate(out_blocks, 0)
    in_grad = jnp.concatenate(grad_blocks, 0)
    output_part, expand_part, contract_part = (
        lax.psum_scatter(
            grad_output.astype(jnp.bfloat16), "mp", scatter_dimension=0, tiled=True
        ).astype(jnp.float32),
        lax.psum_scatter(
            grad_expand.astype(jnp.bfloat16), "mp", scatter_dimension=0, tiled=True
        ).astype(jnp.float32),
        lax.psum_scatter(
            grad_contract.astype(jnp.bfloat16), "mp", scatter_dimension=0, tiled=True
        ).astype(jnp.float32),
    )
    matrix_grads = (
        lax.psum(grad_qkv_weight[:, :head_cols].astype(jnp.bfloat16), "dp").astype(jnp.float32),
        lax.psum(grad_qkv_weight[:, head_cols : 2 * head_cols].astype(jnp.bfloat16), "dp").astype(
            jnp.float32
        ),
        lax.psum(grad_qkv_weight[:, 2 * head_cols :].astype(jnp.bfloat16), "dp").astype(
            jnp.float32
        ),
        lax.psum(output_part.astype(jnp.bfloat16), "dp").astype(jnp.float32),
        lax.psum(expand_part.astype(jnp.bfloat16), "dp").astype(jnp.float32),
        lax.psum(contract_part.astype(jnp.bfloat16), "dp").astype(jnp.float32),
    )
    small_local = jnp.concatenate(
        (grad_bias_expand, grad_bias_contract, jnp.stack((grad_alpha_attend, grad_alpha_ffn)))
    )
    small_grad = lax.psum(small_local, ("dp", "mp"))
    first_new = 0.5 * small_first + 0.5 * small_grad
    second_new = 0.5 * small_second + 0.5 * small_grad * small_grad
    correction = 1.0 - 0.5**STEP
    small_new = small_params - adam_rate * (first_new / correction) / (
        jnp.sqrt(second_new / correction) + 1e-08
    )
    olds = (buffer_query, buffer_key, buffer_value, buffer_output, buffer_expand, buffer_contract)
    weights_old = (w_query, w_key, w_value, w_output, w_expand, w_contract)
    by_columns = (True, True, True, False, False, False)
    buffers = tuple(
        (0.5 * old_buffer + grad_matrix for old_buffer, grad_matrix in zip(olds, matrix_grads))
    )
    squares = lax.psum(tuple((jnp.sum(matrix * matrix) for matrix in buffers)), "mp")
    iterates = [
        matrix / (jnp.sqrt(square_sum) + 1e-07) for matrix, square_sum in zip(buffers, squares)
    ]
    for newton_step in range(5):
        gram_sums = jax.tree.map(
            lambda part: part.astype(jnp.float32),
            lax.psum(
                shortened(
                    tuple(
                        (
                            gram_part(iterate, column_flag)
                            for iterate, column_flag in zip(iterates, by_columns)
                        )
                    )
                ),
                "mp",
            ),
        )
        iterates = [
            newton_update(iterate, gram_sum, column_flag)
            for iterate, gram_sum, column_flag in zip(iterates, gram_sums, by_columns)
        ]
    new_weights = tuple(
        (
            weight - rate * iterate
            for weight, rate, iterate in zip(weights_old, muon_rates, iterates)
        )
    )
    return (layer_out, in_grad) + buffers + new_weights + (small_new, first_new, second_new)


def solution(mesh):
    in_specs = (
        P("dp", None, None),
        P("dp", None),
        P("dp", "mp", None),
        P(None, "mp"),
        P(None, "mp"),
        P(None, "mp"),
        P("mp", None),
        P("mp", None),
        P("mp", None),
        P(),
        P(None, "mp"),
        P(None, "mp"),
        P(None, "mp"),
        P("mp", None),
        P("mp", None),
        P("mp", None),
        P(),
        P(),
    )
    out_specs = (
        P("dp", "mp", None),
        P("dp", "mp", None),
        P(None, "mp"),
        P(None, "mp"),
        P(None, "mp"),
        P("mp", None),
        P("mp", None),
        P("mp", None),
        P(None, "mp"),
        P(None, "mp"),
        P(None, "mp"),
        P("mp", None),
        P("mp", None),
        P("mp", None),
        P(),
        P(),
        P(),
    )
    return jax.shard_map(shards, mesh=mesh, in_specs=in_specs, out_specs=out_specs, check_vma=False)
```

profile of v0, /device:TPU:0, one launch (start us, length us, event | category | flops | bytes accessed | tf_op | source)
XLA Modules:
  0.0 1201.7 jit_solution(14514732442061027347)
XLA Ops:
  30.9 6.3 all-to-all-start.1
  52.8 13.9 %all-to-all-done.1 = bf16[2,1024,128]{2,0,1:T(2,128)(2,1)S(1)} async-done(((bf16[2,1024,128]{2,0,1:T(2,128)(2,1)}), bf16[2,1024,128]{2,0,1:T(2,128)(2,1)S(1)}, u32[]{:S(2)}, u32[]{:S(2)}) %all-to-all-start.1) | async-done | bytes 524320 | tf_op jit(solution)/shard_map/all_to_all | solution.py:212
  70.8 37.5 %all_gather.12 = bf16[512,512]{1,0:T(8,128)(2,1)S(1)} all-gather(bf16[128,512]{1,0:T(8,128)(2,1)S(1)} %convert_element_type.381), channel_id=1, replica_groups=mesh['dp'=8,'mp'=4] {'mp'}, dimensions={0}, use_global_device_ids=true | all-gather | bytes 655360 | tf_op jit(solution)/shard_map/all_gather | solution.py:214
  108.3 4.5 fusion.208
  120.3 5.2 fusion.46
  128.8 4.6 fusion.110
  134.7 6.7 multiply_reduce_fusion.4
  157.1 4.5 fusion.206
  181.9 6.4 all-to-all-done.3
  201.9 17.9 %all-to-all-done.2 = bf16[2,256,512]{1,0,2:T(2,128)(2,1)S(1)} async-done(((bf16[2,256,512]{1,0,2:T(2,128)(2,1)}), bf16[2,256,512]{1,0,2:T(2,128)(2,1)S(1)}, u32[]{:S(2)}, u32[]{:S(2)}) %all-to-all-start.2) | async-done | bytes 524320 | tf_op jit(solution)/shard_map/all_to_all | solution.py:265
  222.4 4.9 multiply_reduce_fusion
  227.4 5.7 fusion.129
  233.1 4.4 multiply_convert_fusion
  263.0 16.3 %reduce-scatter.12.cloned.1.call-done = bf16[512,512]{1,0:T(8,128)(2,1)} async-done(((bf16[2048,512]{1,0:T(8,128)(2,1)}), bf16[512,512]{1,0:T(8,128)(2,1)}) %reduce-scatter.12.cloned.1.call-update) | async-done | bytes 524304 | tf_op jit(solution)/shard_map/reduce_scatter | solution.py:297
  280.8 62.8 %all-reduce.18.cloned.1.call-done = (bf16[512,128]{0,1:T(8,128)(2,1)}, bf16[512,128]{0,1:T(8,128)(2,1)}, bf16[512,128]{0,1:T(8,128)(2,1)}, bf16[128,512]{1,0:T(8...) async-done(((bf16[512,128]{0,1:T(8,128)(2,1)}, bf16[512,128]{0,1:T(8,128)(2,1)}, bf16[512,128]{0,1:T(8,128)(2,1)}, bf16[128,512]{1,0:T(8,128)(2,1)}, ...) | async-done | bytes 1572880 | tf_op jit(solution)/shard_map/psum | solution.py:305
  353.0 12.3 %all-reduce.4 = (f32[]{:T(128)}, f32[]{:T(128)}, f32[]{:T(128)}, f32[]{:T(128)}, f32[]{:T(128)}, /*index=5*/f32[]{:T(128)}) all-reduce(f32[]{:T(128)} %get-tuple-element.257, f32[]{:T(128)} %get-tuple-element.318, f32[]{:T(128)} %get-tuple-element.253, f32[]{:T(128)} %get-tuple-element.251, ...), channel_id=1, replica_groups=mesh['dp'=8,'mp'=4] {'mp'}, use_global_device_ids=true, to_apply=%region_24.25 | all-reduce | flops 6 | bytes 48 | tf_op jit(solution)/shard_map/psum | solution.py:332
  384.1 119.1 %all-reduce.28.cloned.1.call-done = (bf16[512,512]{1,0:T(8,128)(2,1)}, bf16[512,512]{1,0:T(8,128)(2,1)}, bf16[512,512]{1,0:T(8,128)(2,1)}, bf16[512,512]{1,0:T(8...) async-done(((bf16[512,512]{1,0:T(8,128)(2,1)}, bf16[512,512]{1,0:T(8,128)(2,1)}, bf16[512,512]{1,0:T(8,128)(2,1)}, bf16[512,512]{1,0:T(8,128)(2,1)}, ...) | async-done | bytes 3145744 | tf_op jit(solution)/shard_map/psum | solution.py:339
  530.3 121.8 %all-reduce.26.cloned.1.call-done = (bf16[512,512]{1,0:T(8,128)(2,1)}, bf16[512,512]{1,0:T(8,128)(2,1)}, bf16[512,512]{1,0:T(8,128)(2,1)}, bf16[512,512]{1,0:T(8...) async-done(((bf16[512,512]{1,0:T(8,128)(2,1)}, bf16[512,512]{1,0:T(8,128)(2,1)}, bf16[512,512]{1,0:T(8,128)(2,1)}, bf16[512,512]{1,0:T(8,128)(2,1)}, ...) | async-done | bytes 3145744 | tf_op jit(solution)/shard_map/psum | solution.py:339
  678.0 121.8 %all-reduce.24.cloned.1.call-done = (bf16[512,512]{1,0:T(8,128)(2,1)}, bf16[512,512]{1,0:T(8,128)(2,1)}, bf16[512,512]{1,0:T(8,128)(2,1)}, bf16[512,512]{1,0:T(8...) async-done(((bf16[512,512]{1,0:T(8,128)(2,1)}, bf16[512,512]{1,0:T(8,128)(2,1)}, bf16[512,512]{1,0:T(8,128)(2,1)}, bf16[512,512]{1,0:T(8,128)(2,1)}, ...) | async-done | bytes 3145744 | tf_op jit(solution)/shard_map/psum | solution.py:339
  834.6 113.0 %all-reduce.22.cloned.1.call-done = (bf16[512,512]{1,0:T(8,128)(2,1)}, bf16[512,512]{1,0:T(8,128)(2,1)}, bf16[512,512]{1,0:T(8,128)(2,1)}, bf16[512,512]{1,0:T(8...) async-done(((bf16[512,512]{1,0:T(8,128)(2,1)}, bf16[512,512]{1,0:T(8,128)(2,1)}, bf16[512,512]{1,0:T(8,128)(2,1)}, bf16[512,512]{1,0:T(8,128)(2,1)}, ...) | async-done | bytes 3145744 | tf_op jit(solution)/shard_map/psum | solution.py:339
  983.2 9.9 reduce-scatter.8.cloned.1.call-done
  996.7 42.0 %reduce-scatter.6.cloned.1.call-done = bf16[2,256,512]{2,1,0:T(8,128)(2,1)} async-done(((bf16[2,1024,512]{2,1,0:T(8,128)(2,1)}), bf16[2,256,512]{2,1,0:T(8,128)(2,1)}) %reduce-scatter.6.cloned.1.call-update) | async-done | bytes 524304 | tf_op jit(solution)/shard_map/reduce_scatter | solution.py:287
  1043.2 44.3 %psum.343 = f32[2562]{0:T(1024)S(1)} all-reduce(f32[2562]{0:T(1024)S(1)} %concatenate.50), channel_id=1, replica_groups=mesh['dp'=8,'mp'=4] {'dp','mp'}, use_global_device_ids=true, to_apply=%region_73.74 | all-reduce | flops 2562 | bytes 20496 | tf_op jit(solution)/shard_map/psum | solution.py:319
  1091.2 73.6 %all-reduce.20.cloned.1.call-done = (bf16[512,512]{1,0:T(8,128)(2,1)}, bf16[512,512]{1,0:T(8,128)(2,1)}, bf16[512,512]{1,0:T(8,128)(2,1)}, bf16[512,512]{1,0:T(8...) async-done(((bf16[512,512]{1,0:T(8,128)(2,1)}, bf16[512,512]{1,0:T(8,128)(2,1)}, bf16[512,512]{1,0:T(8,128)(2,1)}, bf16[512,512]{1,0:T(8,128)(2,1)}, ...) | async-done | bytes 3145744 | tf_op jit(solution)/shard_map/psum | solution.py:339
  (507 shorter events, 318.8 us)
Async XLA Ops:
  7.2 113.1 %all-gather.3.cloned.1.call-start = ((), (), s32[]{:S(2)}) async-start(), calls=%async_computation.9 | async-start | bytes 2621440 | tf_op jit(solution)/shard_map/all_gather | solution.py:215
  30.9 35.7 %all-to-all-start.1 = ((bf16[2,1024,128]{2,0,1:T(2,128)(2,1)}), bf16[2,1024,128]{2,0,1:T(2,128)(2,1)S(1)}, u32[]{:S(2)}, u32[]{:S(2)}) async-start(bf16[2,1024,128]{2,0,1:T(2,128)(2,1)} %copy.166), calls=%async_computation.1 | async-start | bytes 1048576 | tf_op jit(solution)/shard_map/all_to_all | solution.py:212
  37.3 91.5 %all-gather.5.cloned.1.call-start = ((), (), s32[]{:S(2)}) async-start(), calls=%async_computation.10 | async-start | bytes 2621440 | tf_op jit(solution)/shard_map/all_gather | solution.py:216
  66.6 46.8 %all-to-all-start = ((bf16[2,1024,128]{2,0,1:T(2,128)(2,1)}), bf16[2,1024,128]{2,0,1:T(2,128)(2,1)S(1)}, u32[]{:S(2)}, u32[]{:S(2)}) async-start(bf16[2,1024,128]{2,0,1:T(2,128)(2,1)} %copy.160), calls=%async_computation | async-start | bytes 1048576 | tf_op jit(solution)/shard_map/all_to_all | solution.py:212
  70.1 192.9 %reduce-scatter.10.cloned.1.call-start = ((), (), s32[]{:S(2)}) async-start(), calls=%async_computation.13 | async-start | bytes 655360 | tf_op jit(solution)/shard_map/reduce_scatter | solution.py:294
  157.0 106.0 %reduce-scatter.14.cloned.1.call-start = ((), (), s32[]{:S(2)}) async-start(), calls=%async_computation.15 | async-start | bytes 2621440 | tf_op jit(solution)/shard_map/reduce_scatter | solution.py:300
  171.6 16.7 %all-to-all-start.3 = ((bf16[2,256,512]{1,0,2:T(2,128)(2,1)}), bf16[2,256,512]{1,0,2:T(2,128)(2,1)}, u32[]{:S(2)}, u32[]{:S(2)}) async-start(bf16[2,256,512]{1,0,2:T(2,128)(2,1)} %copy.176), calls=%async_computation.4 | async-start | bytes 1048576 | tf_op jit(solution)/shard_map/all_to_all | solution.py:265
  176.0 103.4 %reduce-scatter.12.cloned.1.call-start = ((), (), s32[]{:S(2)}) async-start(), calls=%async_computation.14 | async-start | bytes 2621440 | tf_op jit(solution)/shard_map/reduce_scatter | solution.py:297
  188.3 31.5 %all-to-all-start.2 = ((bf16[2,256,512]{1,0,2:T(2,128)(2,1)}), bf16[2,256,512]{1,0,2:T(2,128)(2,1)S(1)}, u32[]{:S(2)}, u32[]{:S(2)}) async-start(bf16[2,256,512]{1,0,2:T(2,128)(2,1)} %copy.168), calls=%async_computation.2 | async-start | bytes 1048576 | tf_op jit(solution)/shard_map/all_to_all | solution.py:265
  191.8 151.8 %all-reduce.18.cloned.1.call-start = ((), (), s32[]{:S(2)}) async-start(), calls=%async_computation.16 | async-start | bytes 3145728 | tf_op jit(solution)/shard_map/psum | solution.py:305
  279.4 223.9 %all-reduce.28.cloned.1.call-start = ((), (), s32[]{:S(2)}) async-start(), calls=%async_computation.21 | async-start | bytes 6291456 | tf_op jit(solution)/shard_map/psum | solution.py:339
  345.2 160.0 %copy-start.75 = (f32[512,128]{0,1:T(8,128)}, f32[512,128]{0,1:T(8,128)S(1)}, u32[]{:S(2)}) copy-start(f32[512,128]{0,1:T(8,128)S(1)} %get-tuple-element.258) | copy-start | bytes 786436
  349.3 159.4 %copy-start.77 = (f32[512,128]{0,1:T(8,128)}, f32[512,128]{0,1:T(8,128)S(1)}, u32[]{:S(2)}) copy-start(f32[512,128]{0,1:T(8,128)S(1)} %get-tuple-element.319) | copy-start | bytes 786436
  349.3 163.0 %copy-start.78 = (f32[512,128]{0,1:T(8,128)}, f32[512,128]{0,1:T(8,128)S(1)}, u32[]{:S(2)}) copy-start(f32[512,128]{0,1:T(8,128)S(1)} %get-tuple-element.254) | copy-start | bytes 786436
  383.9 268.3 %all-reduce.26.cloned.1.call-start = ((), (), s32[]{:S(2)}) async-start(), calls=%async_computation.20 | async-start | bytes 6291456 | tf_op jit(solution)/shard_map/psum | solution.py:339
  530.3 269.5 %all-reduce.24.cloned.1.call-start = ((), (), s32[]{:S(2)}) async-start(), calls=%async_computation.19 | async-start | bytes 6291456 | tf_op jit(solution)/shard_map/psum | solution.py:339
  675.3 126.4 %copy-start.45 = (f32[512,128]{0,1:T(8,128)S(1)}, f32[512,128]{0,1:T(8,128)}, u32[]{:S(2)}) copy-start(f32[512,128]{0,1:T(8,128)} %copy-done.44) | copy-start | bytes 786436
  678.0 127.3 %copy-start.47 = (f32[512,128]{0,1:T(8,128)S(1)}, f32[512,128]{0,1:T(8,128)}, u32[]{:S(2)}) copy-start(f32[512,128]{0,1:T(8,128)} %copy-done.46) | copy-start | bytes 786436
  678.0 269.6 %all-reduce.22.cloned.1.call-start = ((), (), s32[]{:S(2)}) async-start(), calls=%async_computation.18 | async-start | bytes 6291456 | tf_op jit(solution)/shard_map/psum | solution.py:339
  825.7 167.5 %reduce-scatter.8.cloned.1.call-start = ((), (), s32[]{:S(2)}) async-start(), calls=%async_computation.12 | async-start | bytes 2621440 | tf_op jit(solution)/shard_map/reduce_scatter | solution.py:287
  829.8 208.8 %reduce-scatter.6.cloned.1.call-start = ((), (), s32[]{:S(2)}) async-start(), calls=%async_computation.11 | async-start | bytes 2621440 | tf_op jit(solution)/shard_map/reduce_scatter | solution.py:287
  834.1 118.9 %copy-start.39 = (f32[512,128]{0,1:T(8,128)S(1)}, f32[512,128]{0,1:T(8,128)}, u32[]{:S(2)}) copy-start(f32[512,128]{0,1:T(8,128)} %copy-done.38) | copy-start | bytes 786436
  834.1 330.7 %all-reduce.20.cloned.1.call-start = ((), (), s32[]{:S(2)}) async-start(), calls=%async_computation.17 | async-start | bytes 6291456 | tf_op jit(solution)/shard_map/psum | solution.py:339
  1041.8 124.9 %copy-start.29 = (f32[512,128]{0,1:T(8,128)S(1)}, f32[512,128]{0,1:T(8,128)}, u32[]{:S(2)}) copy-start(f32[512,128]{0,1:T(8,128)} %copy-done.28) | copy-start | bytes 786436
  (126 other events, 1402.7 us)
Sparse Core Ops, SparseCore 0:
  10.2 59.6 all-gather.2
  72.0 53.5 all-gather.4
  157.2 21.7 reduce-scatter.9
  181.1 50.5 reduce-scatter.13
  234.5 44.7 reduce-scatter.11
  283.7 59.8 all-reduce.17
  384.0 119.1 all-reduce.27
  530.4 121.7 all-reduce.25
  678.1 121.6 all-reduce.23
  825.8 121.7 all-reduce.21
  950.5 42.6 reduce-scatter.7
  995.3 43.2 reduce-scatter.5
  1041.7 123.0 all-reduce.19
where the time goes:
time: 1210 us; the launch traced here: 1200 us
  waiting for transfers between devices  719 us (59%)
  matrix products  258 us (21%)
  blocking collectives  94 us (8%)
  local copies, waits for them, and re-layouts  46.1 us (4%)
  other arithmetic  43 us (4%)
  between operations  23.3 us (2%)
  starting transfers between devices  18.9 us (2%)
    psum x5, waiting for transfers between devices, shards(): lax.psum(shortened(tuple((gram_part(iterate, column_flag) for iterate, co...  549 us
    psum x1, waiting for transfers between devices, shards(): lax.psum(grad_qkv_weight[:, :head_cols].astype(jnp.bfloat16), 'dp')  62.8 us
    reduce_scatter x2, waiting for transfers between devices, shards(): lax.psum_scatter(partial_grad.astype(jnp.bfloat16), 'mp', scatter_dimensi...  51.9 us
    psum x1, blocking collectives, shards(): small_grad = lax.psum(small_local, ('dp', 'mp'))  44.3 us
    dot_general x15, matrix products, gram_part(): lax.dot_general(iterate, iterate, (((0,), (0,)), ((), ())), precision=hig...  38.7 us
    all_gather x1, blocking collectives, shards(): lax.all_gather(row_local[0], 'mp', axis=0, tiled=True)  37.5 us
    dot_general x15, matrix products, newton_update(): lax.dot_general(iterate, polynomial, (((1,), (1,)), ((), ())), precision=...  28.2 us
    dot_general x15, matrix products, gram_part(): lax.dot_general(iterate, iterate, (((1,), (1,)), ((), ())), precision=hig...  27.8 us
  transfers between devices with their start and end apart: 17, of which 12 were waited for; matrix products, arithmetic and copies ran while one was open for 15% of the time, Pallas kernels for 0%

commit v1 on v0

--- a/solution.py
+++ b/solution.py
@@ -1,6 +1,10 @@
+import functools
+
 import jax
 import jax.numpy as jnp
 from jax import lax
+from jax.experimental import pallas as pl
+from jax.experimental.pallas import tpu as pltpu
 from jax.sharding import PartitionSpec as P
 
 D = 512
@@ -147,7 +151,7 @@
     return newton_one * iterate + applied
 
 
-def shards(
+def general_shards(
     layer_in,
     doc_ids,
     out_grad,
@@ -361,6 +365,422 @@
     return (layer_out, in_grad) + buffers + new_weights + (small_new, first_new, second_new)
 
 
+max_doc = 512
+q_rows = 256
+f32 = jnp.float32
+bf16 = jnp.bfloat16
+nt = (((1,), (1,)), ((), ()))
+nn = (((1,), (0,)), ((), ()))
+tn = (((0,), (0,)), ((), ()))
+
+
+def mm(a, b, dims):
+    return lax.dot_general(a, b, dims, preferred_element_type=f32)
+
+
+def swap(x, axis, mask):
+    size = lax.axis_size(axis)
+    return lax.ppermute(x, axis, [(a, a ^ mask) for a in range(size)])
+
+
+def reorder(x, index, axis):
+    parts = [
+        lax.dynamic_slice_in_dim(x, slot ^ index, 1, axis) for slot in range(x.shape[axis])
+    ]
+    return jnp.concatenate(parts, axis)
+
+
+def pick(x, index):
+    return lax.dynamic_index_in_dim(x, index, 0, keepdims=False)
+
+
+def gather_rows(piece):
+    planes = lax.axis_size("mp")
+    chips = lax.axis_size("dp") // 2
+    slots = jnp.stack([piece] + [swap(piece, "mp", k) for k in range(1, planes)])
+    slots = jnp.stack([slots] + [swap(slots, "dp", 2 * m) for m in range(1, chips)], 1)
+    return jnp.stack([slots, swap(slots, "dp", 1)], 2)
+
+
+def window(first_row):
+    return max(0, first_row + 1 - max_doc) // 128 * 128
+
+
+def forward_kernel(last_ref, q_ref, k_ref, v_ref, o_ref):
+    length = q_ref.shape[0]
+    lane = lax.broadcasted_iota(jnp.int32, (q_rows, 128), 1)
+    for first in range(0, length, q_rows):
+        low, high = window(first), first + q_rows
+        row = first + lax.broadcasted_iota(jnp.int32, (q_rows, high - low), 0)
+        col = low + lax.broadcasted_iota(jnp.int32, (q_rows, high - low), 1)
+        allowed = (col <= row) & (row <= last_ref[:, low:high])
+        query = q_ref[first:high, :] * jnp.asarray(HEAD_DIM**-0.5, bf16)
+        halves = []
+        for half in range(2):
+            mine = (lane >= HEAD_DIM * half) & (lane < HEAD_DIM * (half + 1))
+            scores = mm(jnp.where(mine, query, jnp.zeros_like(query)), k_ref[low:high, :], nt)
+            scores = jnp.where(allowed, scores, mask_fill)
+            weight = jnp.exp(scores - jnp.max(scores, axis=1, keepdims=True))
+            total = jnp.sum(weight, axis=1, keepdims=True)
+            halves.append(mm((weight * (1.0 / total)).astype(bf16), v_ref[low:high, :], nn))
+        o_ref[first:high, :] = jnp.where(lane < HEAD_DIM, halves[0], halves[1]).astype(bf16)
+
+
+def backward_kernel(start_ref, q_ref, k_ref, v_ref, g_ref, out_ref, dk_ref, dv_ref):
+    length = q_ref.shape[0]
+    lane = lax.broadcasted_iota(jnp.int32, (q_rows, 128), 1)
+    dk_ref[...] = jnp.zeros_like(dk_ref)
+    dv_ref[...] = jnp.zeros_like(dv_ref)
+    key_t = k_ref[...].astype(f32).T.astype(bf16)
+    for first in range(0, length, q_rows):
+        low, high = window(first), first + q_rows
+        col = low + lax.broadcasted_iota(jnp.int32, (high - low, q_rows), 0)
+        row = first + lax.broadcasted_iota(jnp.int32, (high - low, q_rows), 1)
+        allowed = (col <= row) & (col >= start_ref[:, first:high])
+        query = q_ref[first:high, :] * jnp.asarray(HEAD_DIM**-0.5, bf16)
+        grad = g_ref[first:high, :]
+        key = k_ref[low:high, :]
+        value = v_ref[low:high, :]
+        dk = dk_ref[low:high, :]
+        dv = dv_ref[low:high, :]
+        dq = []
+        for half in range(2):
+            mine = (lane >= HEAD_DIM * half) & (lane < HEAD_DIM * (half + 1))
+            q_half = jnp.where(mine, query, jnp.zeros_like(query))
+            g_half = jnp.where(mine, grad, jnp.zeros_like(grad))
+            scores = jnp.where(allowed, mm(key, q_half, nt), mask_fill)
+            weight = jnp.exp(scores - jnp.max(scores, axis=0, keepdims=True))
+            probs = weight * (1.0 / jnp.sum(weight, axis=0, keepdims=True))
+            g_probs = mm(value, g_half, nt)
+            delta = jnp.sum(probs * g_probs, axis=0, keepdims=True)
+            g_scores = (probs * (g_probs - delta)).astype(bf16)
+            dv = dv + mm(probs.astype(bf16), g_half, nn)
+            dk = dk + mm(g_scores, q_half, nn)
+            dq.append(mm(key_t[HEAD_DIM * half : HEAD_DIM * (half + 1), low:high], g_scores, nn))
+        dk_ref[low:high, :] = dk
+        dv_ref[low:high, :] = dv
+        dq = jnp.concatenate(dq, 0) * HEAD_DIM**-0.5
+        out_ref[0, first:high, :] = dq.T.astype(bf16)
+    out_ref[1] = dk_ref[...].astype(bf16)
+    out_ref[2] = dv_ref[...].astype(bf16)
+
+
+def attention(qkv, last):
+    length, width = qkv.shape[0], qkv.shape[1] // 3
+    pairs = width // 128
+    part = lambda which: pl.BlockSpec((length, 128), lambda h: (0, which * pairs + h))
+    return pl.pallas_call(
+        forward_kernel,
+        grid=(pairs,),
+        in_specs=[pl.BlockSpec((1, length), lambda h: (0, 0)), part(0), part(1), part(2)],
+        out_specs=pl.BlockSpec((length, 128), lambda h: (0, h)),
+        out_shape=jax.ShapeDtypeStruct((length, width), bf16),
+        compiler_params=pltpu.CompilerParams(vmem_limit_bytes=48 << 20),
+        cost_estimate=pl.CostEstimate(
+            flops=2 * length * 768 * 512 * pairs, bytes_accessed=8 * length * width, transcendentals=0
+        ),
+        name="attention_forward",
+    )(last, qkv, qkv, qkv)
+
+
+def attention_back(qkv, start, grad):
+    length, width = grad.shape
+    pairs = width // 128
+    part = lambda which: pl.BlockSpec((length, 128), lambda h: (0, which * pairs + h))
+    return pl.pallas_call(
+        backward_kernel,
+        grid=(pairs,),
+        in_specs=[
+            pl.BlockSpec((1, length), lambda h: (0, 0)),
+            part(0),
+            part(1),
+            part(2),
+            pl.BlockSpec((length, 128), lambda h: (0, h)),
+        ],
+        out_specs=pl.BlockSpec((3, length, 128), lambda h: (0, 0, h)),
+        out_shape=jax.ShapeDtypeStruct((3, length, width), bf16),
+        scratch_shapes=[pltpu.VMEM((length, 128), f32), pltpu.VMEM((length, 128), f32)],
+        compiler_params=pltpu.CompilerParams(vmem_limit_bytes=48 << 20),
+        cost_estimate=pl.CostEstimate(
+            flops=5 * length * 768 * 512 * pairs, bytes_accessed=14 * length * width, transcendentals=0
+        ),
+        name="attention_backward",
+    )(start, qkv, qkv, qkv, grad)
+
+
+def newton_kernel(rows_ref, out_ref, x_ref, low_ref):
+    dim = x_ref.shape[0]
+    cols = x_ref.shape[1]
+    chunk = min(cols, 512)
+    total = jnp.zeros((1, 1), f32)
+    for at in range(0, cols, chunk):
+        part = rows_ref[at : at + chunk, :].astype(f32)
+        total = total + jnp.sum(jnp.sum(part * part, axis=0, keepdims=True), axis=1, keepdims=True)
+    inverse = 1.0 / (jnp.sqrt(total) + 1e-07)
+    for at in range(0, cols, chunk):
+        part = rows_ref[at : at + chunk, :].astype(f32).T * inverse
+        x_ref[:, at : at + chunk] = part
+        low_ref[:, at : at + chunk] = part.astype(bf16)
+    diagonal = lax.broadcasted_iota(jnp.int32, (dim, dim), 0) == lax.broadcasted_iota(
+        jnp.int32, (dim, dim), 1
+    )
+
+    def step(limit):
+        gram = jnp.zeros((dim, dim), f32)
+        for at in range(0, cols, chunk):
+            part = low_ref[:, at : at + chunk]
+            gram = gram + mm(part, part, nt)
+        trace = jnp.sum(
+            jnp.sum(jnp.where(diagonal, gram, 0.0), axis=0, keepdims=True), axis=1, keepdims=True
+        )
+        shift = trace * (1.0 / dim)
+        rest = jnp.where(diagonal, gram - shift, gram)
+        rest_low = rest.astype(bf16)
+        poly = (newton_two + 2.0 * newton_three * shift) * rest + newton_three * mm(
+            rest_low, rest_low, nn
+        )
+        poly = poly.astype(bf16)
+        scale = newton_one + newton_two * shift + newton_three * shift * shift
+        for at in range(0, limit, chunk):
+            part = scale * x_ref[:, at : at + chunk] + mm(poly, low_ref[:, at : at + chunk], nn)
+            x_ref[:, at : at + chunk] = part
+            low_ref[:, at : at + chunk] = part.astype(bf16)
+
+    @pl.loop(0, 4)
+    def _(_):
+        step(cols)
+
+    kept = out_ref.shape[0]
+    step(kept)
+    for at in range(0, kept, chunk):
+        out_ref[at : at + chunk, :] = x_ref[:, at : at + chunk].T.astype(bf16)
+
+
+def newton(rows, kept):
+    cols, dim = rows.shape
+    return pl.pallas_call(
+        newton_kernel,
+        in_specs=[pl.BlockSpec(memory_space=pltpu.VMEM)],
+        out_specs=pl.BlockSpec(memory_space=pltpu.VMEM),
+        out_shape=jax.ShapeDtypeStruct((kept, dim), bf16),
+        scratch_shapes=[pltpu.VMEM((dim, cols), f32), pltpu.VMEM((dim, cols), bf16)],
+        compiler_params=pltpu.CompilerParams(vmem_limit_bytes=48 << 20),
+        cost_estimate=pl.CostEstimate(
+            flops=10 * dim * dim * (2 * cols + dim), bytes_accessed=4 * cols * dim, transcendentals=0
+        ),
+        name="newton",
+    )(rows)
+
+
+def shards(
+    layer_in,
+    doc_ids,
+    out_grad,
+    w_query,
+    w_key,
+    w_value,
+    w_output,
+    w_expand,
+    w_contract,
+    small_params,
+    buffer_query,
+    buffer_key,
+    buffer_value,
+    buffer_output,
+    buffer_expand,
+    buffer_contract,
+    small_first,
+    small_second,
+):
+    planes = lax.axis_size("mp")
+    spots = lax.axis_size("dp")
+    chips = spots // 2
+    plane = lax.axis_index("mp")
+    spot = lax.axis_index("dp")
+    core = spot % 2
+    length = layer_in.shape[1]
+    token_span = length // planes
+    head_cols = w_query.shape[1]
+    hidden_rows = w_expand.shape[0]
+    qkv_span = head_cols // spots
+    hid_span = hidden_rows // spots
+    to_planes = range(1, planes)
+    to_chips = range(1, chips)
+
+    columns = lambda w: lax.dynamic_slice_in_dim(w, spot * qkv_span, qkv_span, 1).T
+    rows = lambda w, span: lax.dynamic_slice_in_dim(w, spot * span, span, 0)
+    qkv_piece = jnp.concatenate([columns(w).astype(bf16) for w in (w_query, w_key, w_value)])
+    rest_piece = jnp.concatenate(
+        [
+            rows(w_output, qkv_span).astype(bf16),
+            rows(w_expand, hid_span).astype(bf16),
+            rows(w_contract, hid_span).astype(bf16),
+        ]
+    )
+    qkv_slots = gather_rows(qkv_piece).reshape(planes, spots, 3, qkv_span, D)
+    qkv_weight = qkv_slots.transpose(2, 0, 1, 3, 4).reshape(3 * planes * head_cols, D)
+    rest_slots = gather_rows(rest_piece).reshape(planes * spots, qkv_span + 2 * hid_span, D)
+    output_full = rest_slots[:, :qkv_span].reshape(planes * head_cols, D)
+    expand_full = rest_slots[:, qkv_span : qkv_span + hid_span].reshape(planes * hidden_rows, D)
+    contract_full = rest_slots[:, qkv_span + hid_span :].reshape(planes * hidden_rows, D)
+
+    def to_slots(bias):
+        shaped = bias.reshape(planes, spots, hid_span)
+        return reorder(reorder(shaped, plane, 0), spot, 1).reshape(-1)
+
+    expansion_bias = to_slots(small_params[:FF])
+    contraction_bias = small_params[FF : FF + D]
+    alpha_attend = small_params[FF + D]
+    alpha_ffn = small_params[FF + D + 1]
+
+    inputs = pick(layer_in, plane)
+    documents = pick(doc_ids, plane)
+    last = (
+        jnp.sum(documents[None, :] <= documents[:, None], axis=1, dtype=jnp.int32)[None, :] - 1
+    )
+    start = jnp.sum(documents[None, :] < documents[:, None], axis=1, dtype=jnp.int32)[None, :]
+    grad_low = out_grad.astype(bf16)
+    upstream = jnp.stack(
+        [pick(grad_low, plane)] + [swap(pick(grad_low, plane ^ k), "mp", k) for k in to_planes]
+    )
+    upstream = reorder(upstream, plane, 0).reshape(length, D).astype(f32)
+
+    qkv = mm(inputs, qkv_weight, nt).astype(bf16)
+    heads = attention(qkv, last)
+    attended = mm(heads, output_full, nn)
+    middle = inputs.astype(f32) + alpha_attend * attended
+    middle_low = middle.astype(bf16)
+    pre = mm(middle_low, expand_full, nt) + expansion_bias
+    hidden, gelu_back = jax.vjp(gelu_tanh, pre)
+    hidden_low = hidden.astype(bf16)
+    branch = mm(hidden_low, contract_full, nn) + contraction_bias
+    layer_out = middle + alpha_ffn * branch
+
+    def to_positions(whole):
+        blocks = whole.astype(bf16).reshape(planes, token_span, D)
+        got = jnp.stack(
+            [pick(blocks, plane)] + [swap(pick(blocks, plane ^ k), "mp", k) for k in to_planes]
+        )
+        return reorder(got, plane, 0).astype(f32)
+
+    layer_out = to_positions(layer_out)
+
+    grad_alpha_ffn = jnp.sum(upstream * branch)
+    branch_grad = (alpha_ffn * upstream).astype(bf16)
+    grad_bias_contract = jnp.sum(branch_grad, axis=0, dtype=f32)
+    grad_contract = mm(hidden_low, branch_grad, tn)
+    hidden_grad = mm(branch_grad, contract_full, nt)
+    pre_grad = gelu_back(hidden_grad)[0].astype(bf16)
+    grad_bias_expand = to_slots(jnp.sum(pre_grad, axis=0, dtype=f32))
+    grad_expand = mm(pre_grad, middle_low, tn)
+    middle_grad = upstream + mm(pre_grad, expand_full, nn)
+    grad_alpha_attend = jnp.sum(middle_grad * attended)
+    attend_grad = (alpha_attend * middle_grad).astype(bf16)
+    grad_output = mm(heads, attend_grad, tn)
+    heads_grad = mm(attend_grad, output_full, nt).astype(bf16)
+
+    ffn_shape = (planes, chips, 2, hid_span, D)
+    is_zero = core == 0
+    grad_expand = grad_expand.astype(bf16)
+    grad_contract = grad_contract.astype(bf16)
+    kept = jnp.where(is_zero, grad_expand, grad_contract).reshape(ffn_shape)
+    given = jnp.where(is_zero, grad_contract, grad_expand).reshape(ffn_shape)
+    ffn_sum = (kept.astype(f32) + jnp.flip(swap(given, "dp", 1), 2).astype(f32)).astype(bf16)
+    got = [swap(ffn_sum[:, m], "dp", 2 * m) for m in to_chips]
+    ffn_sum = ffn_sum[:, 0].astype(f32)
+    for block in got:
+        ffn_sum = ffn_sum + block.astype(f32)
+    ffn_sum = ffn_sum.astype(bf16)
+    got = [swap(ffn_sum[k], "mp", k) for k in to_planes]
+    ffn_sum = ffn_sum[0].astype(f32)
+    for block in got:
+        ffn_sum = ffn_sum + block.astype(f32)
+    ffn_buffer = jnp.where(is_zero, buffer_expand, buffer_contract)
+    ffn_buffer = jnp.stack(
+        [
+            lax.dynamic_slice_in_dim(ffn_buffer, (spot ^ c) * hid_span, hid_span, 0)
+            for c in range(2)
+        ]
+    )
+    ffn_piece = (0.5 * ffn_buffer + ffn_sum).astype(bf16)
+    ffn_rows = jnp.stack([ffn_piece] + [swap(ffn_piece, "mp", k) for k in to_planes])
+    ffn_rows = jnp.stack([ffn_rows] + [swap(ffn_rows, "dp", 2 * m) for m in to_chips], 1)
+
+    qkv_grad = attention_back(qkv, start, heads_grad)
+    weight_three = qkv_weight.reshape(3, D, D)
+    in_grad = middle_grad
+    for which in range(3):
+        in_grad = in_grad + mm(qkv_grad[which], weight_three[which], nn)
+    grads = [mm(qkv_grad[which], inputs, tn).astype(bf16) for which in range(3)]
+    grads.append(grad_output.astype(bf16))
+    grads = jnp.stack(grads).reshape(4, planes, chips, 2, qkv_span, D)
+    total = grads[:, :, :, 0].astype(f32) + swap(grads[:, :, :, 1], "dp", 1).astype(f32)
+    total = total.astype(bf16)
+    got = [swap(total[:, :, m], "dp", 2 * m) for m in to_chips]
+    total = total[:, :, 0].astype(f32)
+    for block in got:
+        total = total + block.astype(f32)
+    old = jnp.stack(
+        [columns(w) for w in (buffer_query, buffer_key, buffer_value)]
+        + [rows(buffer_output, qkv_span)]
+    )
+    total = jnp.concatenate([total[:, :1] + 0.5 * old[:, None], total[:, 1:]], 1)
+    total = reorder(total, plane, 1)
+    sent = total.astype(bf16)
+    got = [swap(pick(sent, plane ^ k), "mp", k) for k in to_planes]
+    total = pick(total, plane)
+    for block in got:
+        total = total + block.astype(f32)
+    total = total.astype(bf16)
+    att_rows = jnp.stack([total] + [swap(total, "dp", 2 * m) for m in to_chips], 1)
+    att_rows = jnp.stack([att_rows, swap(att_rows, "dp", 1)], 2)
+    att_rows = att_rows.reshape(D, D)
+
+    in_grad = to_positions(in_grad)
+
+    ffn_rows = ffn_rows.reshape(planes * hidden_rows, D)
+    ffn_step = newton(ffn_rows, hidden_rows)
+
+    def spread_ffn(mine):
+        mine = reorder(mine.reshape(spots, hid_span, D), spot, 0).reshape(hidden_rows, D)
+        other = swap(mine, "dp", 1)
+        expand = jnp.where(is_zero, mine, other).astype(f32)
+        contract = jnp.where(is_zero, other, mine).astype(f32)
+        return expand, contract
+
+    new_buffer_expand, new_buffer_contract = spread_ffn(ffn_rows[:hidden_rows])
+    step_expand, step_contract = spread_ffn(ffn_step)
+
+    def spread_att(whole):
+        blocks = whole.reshape(planes, spots, qkv_span, D)
+        got = jnp.stack(
+            [pick(blocks, plane)] + [swap(pick(blocks, plane ^ k), "mp", k) for k in to_planes]
+        )
+        got = reorder(reorder(got, plane, 0), spot, 1).reshape(planes, head_cols, D).astype(f32)
+        return got[0].T, got[1].T, got[2].T, got[3]
+
+    att_buffers = spread_att(att_rows)
+    att_steps = spread_att(newton(att_rows, D))
+
+    small_local = jnp.concatenate(
+        (grad_bias_expand, grad_bias_contract, jnp.stack((grad_alpha_attend, grad_alpha_ffn)))
+    )
+    small_grad = lax.psum(small_local, ("dp", "mp"))
+    first_new = 0.5 * small_first + 0.5 * small_grad
+    second_new = 0.5 * small_second + 0.5 * small_grad * small_grad
+    correction = 1.0 - 0.5**STEP
+    small_new = small_params - adam_rate * (first_new / correction) / (
+        jnp.sqrt(second_new / correction) + 1e-08
+    )
+    buffers = att_buffers + (new_buffer_expand, new_buffer_contract)
+    steps = att_steps + (step_expand, step_contract)
+    weights_old = (w_query, w_key, w_value, w_output, w_expand, w_contract)
+    new_weights = tuple(
+        weight - rate * step for weight, rate, step in zip(weights_old, muon_rates, steps)
+    )
+    return (layer_out, in_grad) + buffers + new_weights + (small_new, first_new, second_new)
+
+
 def solution(mesh):
     in_specs = (
         P("dp", None, None),
@@ -401,4 +821,5 @@
         P(),
         P(),
     )
-    return jax.shard_map(shards, mesh=mesh, in_specs=in_specs, out_specs=out_specs, check_vma=False)
+    whole = mesh.shape["mp"] == 4 and mesh.shape["dp"] == 8
+    return jax.shard_map(shards if whole else general_shards, mesh=mesh, in_specs=in_specs, out_specs=out_specs, check_vma=False)

time: 1210 us -> 431 us (0.36)
  waiting for transfers between devices: 719 us -> 126 us
  matrix products: 258 us -> 51 us
  Pallas kernels: 0 us -> 63.3 us
  blocking collectives: 94 us -> 39.1 us
  starting transfers between devices: 18.9 us -> 70.9 us
  between operations: 23.3 us -> 2.28 us
    psum x6 -> x0, waiting for transfers between devices: 612 us -> none  [the longest x5 549 us: shards(): lax.psum(shortened(tuple((gram_part(iterate, column_flag) for iterate, co...]
    dot_general x138 -> x16, matrix products: 258 us -> 51 us  [mm(): return lax.dot_general(a, b, dims, preferred_element_type=f32)]
    ppermute x0 -> x55, waiting for transfers between devices: none -> 126 us  [swap(): return lax.ppermute(x, axis, [(a, a ^ mask) for a in range(size)])]
    ppermute x0 -> x55, starting transfers between devices: none -> 70.9 us  [swap(): return lax.ppermute(x, axis, [(a, a ^ mask) for a in range(size)])]
    reduce_scatter x5 -> x0, waiting for transfers between devices: 68.2 us -> none  [the longest x2 51.9 us: shards(): lax.psum_scatter(partial_grad.astype(jnp.bfloat16), 'mp', scatter_dimensi...]
    pallas_call x0 -> x4, Pallas kernels: none -> 63.3 us  [the longest x1 25.1 us: attention_back(): pl.pallas_call(backward_kernel, grid=(pairs,), in_specs=[pl.BlockSpec((1,...]
    all_to_all x4 -> x0, waiting for transfers between devices: 38.2 us -> none  [the longest x2 24.3 us: shards(): lax.all_to_all(heads_grad_tok, 'mp', split_axis=2, concat_axis=1, tiled=T...]
    all_gather x1 -> x0, blocking collectives: 37.5 us -> none  [shards(): lax.all_gather(row_local[0], 'mp', axis=0, tiled=True)]
  transfers between devices with their start and end apart: 17 -> 55, of which waited for: 12 -> 26; matrix products, arithmetic and copies ran while one was open for 15% -> 17% of each run, Pallas kernels for 0% -> 6%
where the time goes in v1:
time: 431 us; the launch traced here: 427 us
  waiting for transfers between devices  126 us (29%)
  starting transfers between devices  70.9 us (16%)
  Pallas kernels  63.3 us (15%)
  matrix products  51 us (12%)
  local copies, waits for them, and re-layouts  39.8 us (9%)
  blocking collectives  39.1 us (9%)
  other arithmetic  34.4 us (8%)
    ppermute x55, waiting for transfers between devices, swap(): return lax.ppermute(x, axis, [(a, a ^ mask) for a in range(size)])  126 us
    ppermute x55, starting transfers between devices, swap(): return lax.ppermute(x, axis, [(a, a ^ mask) for a in range(size)])  70.9 us
    dot_general x16, matrix products, mm(): return lax.dot_general(a, b, dims, preferred_element_type=f32)  51 us
    psum x1, blocking collectives, shards(): small_grad = lax.psum(small_local, ('dp', 'mp'))  39.1 us
    pallas_call x1, Pallas kernels, attention_back(): pl.pallas_call(backward_kernel, grid=(pairs,), in_specs=[pl.BlockSpec((1,...  25.1 us
    pallas_call x2, Pallas kernels, newton(): pl.pallas_call(newton_kernel, in_specs=[pl.BlockSpec(memory_space=pltpu.V...  21.7 us
    pallas_call x1, Pallas kernels, attention(): pl.pallas_call(forward_kernel, grid=(pairs,), in_specs=[pl.BlockSpec((1,...  16.5 us
    unnamed x133, local copies, waits for them, and re-layouts  15.7 us
  transfers between devices with their start and end apart: 55, of which 26 were waited for; matrix products, arithmetic and copies ran while one was open for 17% of the time, Pallas kernels for 6%

profile of v1, /device:TPU:0, one launch (start us, length us, event | category | flops | bytes accessed | tf_op | source)
XLA Modules:
  0.0 426.6 jit_solution(16975658499922718126)
XLA Ops:
  32.5 9.5 %collective-permute-done.10 = bf16[4,144,512]{2,1,0:T(8,128)(2,1)} collective-permute-done((bf16[4,144,512]{2,1,0:T(8,128)(2,1)}, bf16[4,144,512]{2,1,0:T(8,128)(2,1)}, u32[]{:S(2)}, u32[]{:S(2)}) %collective-permute-start.10) | collective-permute-done | bytes 589856 | tf_op jit(solution)/shard_map/ppermute | solution.py:383
  44.1 9.4 %collective-permute-done.11 = bf16[4,144,512]{2,1,0:T(8,128)(2,1)} collective-permute-done((bf16[4,144,512]{2,1,0:T(8,128)(2,1)}, bf16[4,144,512]{2,1,0:T(8,128)(2,1)}, u32[]{:S(2)}, u32[]{:S(2)}) %collective-permute-start.11) | collective-permute-done | bytes 589856 | tf_op jit(solution)/shard_map/ppermute | solution.py:383
  80.3 6.5 %collective-permute-done.18 = bf16[256,512]{1,0:T(8,128)(2,1)} collective-permute-done((bf16[256,512]{1,0:T(8,128)(2,1)}, bf16[256,512]{1,0:T(8,128)(2,1)}, u32[]{:S(2)}, u32[]{:S(2)}) %collective-permute-start.18) | collective-permute-done | bytes 262176 | tf_op jit(solution)/shard_map/ppermute | solution.py:383
  95.6 16.5 %attention_forward.1 = bf16[1024,512]{1,0:T(8,128)(2,1)S(1)} custom-call(s32[1,1024]{1,0:T(1,128)S(1)} %bitcast.312, bf16[1024,1536]{1,0:T(8,128)(2,1)S(1)} %convolution_convert_fusion.q_ref.k_ref.v_ref, bf16[1024,1536]{1,0:T(8,128)(2,1)S(1)} %convolution_convert_fusion.q_ref.k_ref.v_ref, bf16[1024,1536]{1,0:T(8,128)(2,1)S(1)} %convolution_convert_fusion.q_ref.k_ref.v_ref), custom_call_target="tpu_custom_call" | custom-call | flops 3221225472 | bytes 4194304 | tf_op jit(solution)/shard_map/attention_forward/pallas_call | solution.py:472
  114.7 4.0 fusion.12
  118.7 5.5 %multiply_convert_fusion = (bf16[1024,2048]{1,0:T(8,128)(2,1)}, f32[1024,2048]{1,0:T(8,128)S(1)}) fusion(f32[2048]{0:T(1024)S(1)} %add.288, bf16[1024,512]{1,0:T(8,128)(2,1)S(1)} %get-tuple-element.199, bf16[2048,512]{1,0:T(8,128)(2,1)S(1)} %bitcast.336), kind=kOutput, calls=%fused_computation.10 | convolution fusion | flops 2168455168 | bytes 15736832 | tf_op jit(solution)/shard_map/dot_general | solution.py:378
  124.2 9.1 %convert_reduce_fusion = (f32[2048]{0:T(1024)}, bf16[1024,2048]{1,0:T(8,128)(2,1)S(1)}) fusion(f32[1024,2048]{1,0:T(8,128)S(1)} %get-tuple-element.202, f32[2048]{0:T(1024)S(1)} %add.288, bf16[1024,512]{1,0:T(8,128)(2,1)S(1)} %bitcast.341, bf16[2048,512]{1,0:T(8,128)(2,1)S(1)} %bitcast.334), kind=kOutput, calls=%fused_computation.9 | convolution fusion | flops 2195716096 | bytes 15745024 | tf_op jit(solution)/shard_map/dot_general | solution.py:378
  143.1 25.1 %attention_backward.1 = bf16[3,1024,512]{2,1,0:T(8,128)(2,1)S(1)} custom-call(s32[1,1024]{1,0:T(1,128)S(1)} %bitcast.313, bf16[1024,1536]{1,0:T(8,128)(2,1)} %copy-done.2, bf16[1024,1536]{1,0:T(8,128)(2,1)} %copy-done.2, bf16[1024,1536]{1,0:T(8,128)(2,1)} %copy-done.2, bf16[1024,512]{1,0:T(8,128)(2,1)S(1)} %convolution_convert_fusion.3.g_ref), custom_call_target="tpu_custom_call" | custom-call | flops 8053063680 | bytes 7340032 | tf_op jit(solution)/shard_map/attention_backward/pallas_call | solution.py:490
  184.4 6.2 %collective-permute-start.20 = (bf16[256,512]{1,0:T(8,128)(2,1)S(1)}, bf16[256,512]{1,0:T(8,128)(2,1)S(1)}, u32[]{:S(2)}, u32[]{:S(2)}) collective-permute-start(bf16[256,512]{1,0:T(8,128)(2,1)S(1)} %get-tuple-element.109), channel_id=1, source_target_pairs={{0,1},{1,0},{2,3},{3,2},{4,5},{5,4},{6,7},{7,6},{8,9},{9,8},{10,11... | collective-permute-start | bytes 786440 | tf_op jit(solution)/shard_map/ppermute | solution.py:383
  193.1 7.1 %fusion.11 = (f32[]{:T(128)}, bf16[1024,512]{1,0:T(8,128)(2,1)S(1)}, f32[]{:T(128)}, bf16[1024,512]{1,0:T(8,128)(2,1)}) fusion(f32[512]{0:T(512)S(1)} %slice-done.1, bf16[1,256,512]{2,1,0:T(8,128)(2,1)S(1)} %copy-done.7, bf16[1,256,512]{2,1,0:T(8,128)(2,1)S(1)} %copy-done.9, bf16[1,256,512]{2,1,0:T(8,128)(2,1)S(1)} %copy-done.11, ...), kind=kOutput, calls=%fused_computation.30 | convolution fusion | flops 2156396544 | bytes 14682132 | tf_op jit(solution)/shard_map/dot_general | solution.py:378
  201.6 39.1 %psum.7 = f32[2562]{0:T(1024)S(1)} all-reduce(f32[2562]{0:T(1024)S(1)} %concatenate.79), channel_id=1, replica_groups=mesh['dp'=8,'mp'=4] {'dp','mp'}, use_global_device_ids=true, to_apply=%region_6.7 | all-reduce | flops 2562 | bytes 20496 | tf_op jit(solution)/shard_map/psum | solution.py:768
  240.7 5.6 %broadcast_select_fusion = (bf16[2048,512]{1,0:T(8,128)(2,1)S(1)}, bf16[2048,512]{1,0:T(8,128)(2,1)S(1)}) fusion(bf16[2048,512]{1,0:T(8,128)(2,1)} %convolution_convert_fusion.2, pred[]{:T(512)S(6)} %eq.5, bf16[1024,2048]{1,0:T(8,128)(2,1)} %get-tuple-element.201, bf16[1024,512]{1,0:T(8,128)(2,1)} %get-tuple-element.92), kind=kOutput, calls=%fused_computation.37 | convolution fusion | flops 2150629376 | bytes 11534337 | tf_op jit(solution)/shard_map/dot_general | solution.py:378
  265.9 6.5 %collective-permute-done.27 = bf16[4,16,512]{2,1,0:T(8,128)(2,1)S(1)} collective-permute-done((bf16[4,16,512]{2,1,0:T(8,128)(2,1)S(1)}, bf16[4,16,512]{2,1,0:T(8,128)(2,1)S(1)}, u32[]{:S(2)}, u32[]{:S(2)}) %collective-permute-start.27) | collective-permute-done | bytes 65568 | tf_op jit(solution)/shard_map/ppermute | solution.py:383
  274.0 9.2 %collective-permute-done.28 = bf16[4,16,512]{2,1,0:T(8,128)(2,1)S(1)} collective-permute-done((bf16[4,16,512]{2,1,0:T(8,128)(2,1)S(1)}, bf16[4,16,512]{2,1,0:T(8,128)(2,1)S(1)}, u32[]{:S(2)}, u32[]{:S(2)}) %collective-permute-start.28) | collective-permute-done | bytes 65568 | tf_op jit(solution)/shard_map/ppermute | solution.py:383
  292.5 7.0 %newton.2 = bf16[512,512]{1,0:T(8,128)(2,1)S(1)} custom-call(bf16[512,512]{1,0:T(8,128)(2,1)S(1)} %bitcast.301), custom_call_target="tpu_custom_call" | custom-call | flops 4026531840 | bytes 1048576 | tf_op jit(solution)/shard_map/newton/pallas_call | solution.py:561
  307.7 6.1 %collective-permute-done.52 = bf16[8,16,512]{2,1,0:T(8,128)(2,1)S(1)} collective-permute-done((bf16[8,16,512]{2,1,0:T(8,128)(2,1)S(1)}, bf16[8,16,512]{2,1,0:T(8,128)(2,1)S(1)}, u32[]{:S(2)}, u32[]{:S(2)}) %collective-permute-start.52) | collective-permute-done | bytes 131104 | tf_op jit(solution)/shard_map/ppermute | solution.py:383
  315.7 9.3 %collective-permute-done.35 = bf16[8,16,512]{2,1,0:T(8,128)(2,1)S(1)} collective-permute-done((bf16[8,16,512]{2,1,0:T(8,128)(2,1)S(1)}, bf16[8,16,512]{2,1,0:T(8,128)(2,1)S(1)}, u32[]{:S(2)}, u32[]{:S(2)}) %collective-permute-start.35) | collective-permute-done | bytes 131104 | tf_op jit(solution)/shard_map/ppermute | solution.py:383
  330.7 11.2 %collective-permute-done.38 = bf16[4,2,64,512]{3,2,1,0:T(8,128)(2,1)S(1)} collective-permute-done((bf16[4,2,64,512]{3,2,1,0:T(8,128)(2,1)S(1)}, bf16[4,2,64,512]{3,2,1,0:T(8,128)(2,1)S(1)}, u32[]{:S(2)}, u32[]{:S(2)}) %collective-permute-start.38) | collective-permute-done | bytes 524320 | tf_op jit(solution)/shard_map/ppermute | solution.py:383
  342.0 10.1 %collective-permute-done.39 = bf16[4,2,64,512]{3,2,1,0:T(8,128)(2,1)S(1)} collective-permute-done((bf16[4,2,64,512]{3,2,1,0:T(8,128)(2,1)S(1)}, bf16[4,2,64,512]{3,2,1,0:T(8,128)(2,1)S(1)}, u32[]{:S(2)}, u32[]{:S(2)}) %collective-permute-start.39) | collective-permute-done | bytes 524320 | tf_op jit(solution)/shard_map/ppermute | solution.py:383
  359.8 7.0 %collective-permute-done.42 = bf16[2,64,512]{2,1,0:T(8,128)(2,1)S(1)} collective-permute-done((bf16[2,64,512]{2,1,0:T(8,128)(2,1)S(1)}, bf16[2,64,512]{2,1,0:T(8,128)(2,1)S(1)}, u32[]{:S(2)}, u32[]{:S(2)}) %collective-permute-start.42) | collective-permute-done | bytes 131104 | tf_op jit(solution)/shard_map/ppermute | solution.py:383
  373.2 7.3 %collective-permute-done.45 = bf16[2,64,512]{2,1,0:T(8,128)(2,1)S(1)} collective-permute-done((bf16[2,64,512]{2,1,0:T(8,128)(2,1)S(1)}, bf16[2,64,512]{2,1,0:T(8,128)(2,1)S(1)}, u32[]{:S(2)}, u32[]{:S(2)}) %collective-permute-start.45) | collective-permute-done | bytes 131104 | tf_op jit(solution)/shard_map/ppermute | solution.py:383
  390.1 5.5 %collective-permute-done.47 = bf16[4,2,64,512]{3,2,1,0:T(8,128)(2,1)} collective-permute-done((bf16[4,2,64,512]{3,2,1,0:T(8,128)(2,1)S(1)}, bf16[4,2,64,512]{3,2,1,0:T(8,128)(2,1)}, u32[]{:S(2)}, u32[]{:S(2)}) %collective-permute-start.47) | collective-permute-done | bytes 524320 | tf_op jit(solution)/shard_map/ppermute | solution.py:383
  395.6 8.0 %collective-permute-done.48 = bf16[4,2,64,512]{3,2,1,0:T(8,128)(2,1)} collective-permute-done((bf16[4,2,64,512]{3,2,1,0:T(8,128)(2,1)S(1)}, bf16[4,2,64,512]{3,2,1,0:T(8,128)(2,1)}, u32[]{:S(2)}, u32[]{:S(2)}) %collective-permute-start.48) | collective-permute-done | bytes 524320 | tf_op jit(solution)/shard_map/ppermute | solution.py:383
  406.2 14.7 %newton.3 = bf16[512,512]{1,0:T(8,128)(2,1)S(1)} custom-call(bf16[2048,512]{1,0:T(8,128)(2,1)S(1)} %bitcast.300), custom_call_target="tpu_custom_call" | custom-call | flops 12079595520 | bytes 4194304 | tf_op jit(solution)/shard_map/newton/pallas_call | solution.py:561
  (343 shorter events, 178.9 us)
Async XLA Ops:
  3.3 20.1 %collective-permute-start.7 = (bf16[144,512]{1,0:T(8,128)(2,1)}, bf16[144,512]{1,0:T(8,128)(2,1)}, u32[]{:S(2)}, u32[]{:S(2)}) collective-permute-start(bf16[144,512]{1,0:T(8,128)(2,1)} %get-tuple-element.170), channel_id=1, source_target_pairs={{0,1},{1,0},{2,3},{3,2},{4,5},{5,4},{6,7},{7,6},{8,9},{9,8},{10,11... | collective-permute-start | bytes 442376 | tf_op jit(solution)/shard_map/ppermute | solution.py:383
  6.3 17.0 %collective-permute-start.8 = (bf16[144,512]{1,0:T(8,128)(2,1)}, bf16[144,512]{1,0:T(8,128)(2,1)}, u32[]{:S(2)}, u32[]{:S(2)}) collective-permute-start(bf16[144,512]{1,0:T(8,128)(2,1)} %get-tuple-element.170), channel_id=1, source_target_pairs={{0,2},{1,3},{2,0},{3,1},{4,6},{5,7},{6,4},{7,5},{8,10},{9,11},{10,... | collective-permute-start | bytes 442376 | tf_op jit(solution)/shard_map/ppermute | solution.py:383
  13.1 45.2 %collective-permute-start.2 = (bf16[48,512]{1,0:T(8,128)(2,1)}, bf16[48,512]{1,0:T(8,128)(2,1)}, u32[]{:S(2)}, u32[]{:S(2)}) collective-permute-start(bf16[48,512]{1,0:T(8,128)(2,1)} %get-tuple-element.172), channel_id=1, source_target_pairs={{0,3},{1,2},{2,1},{3,0},{4,7},{5,6},{6,5},{7,4},{8,11},{9,10},{10,... | collective-permute-start | bytes 147464 | tf_op jit(solution)/shard_map/ppermute | solution.py:383
  16.9 41.4 %collective-permute-start = (bf16[48,512]{1,0:T(8,128)(2,1)}, bf16[48,512]{1,0:T(8,128)(2,1)}, u32[]{:S(2)}, u32[]{:S(2)}) collective-permute-start(bf16[48,512]{1,0:T(8,128)(2,1)} %get-tuple-element.172), channel_id=1, source_target_pairs={{0,1},{1,0},{2,3},{3,2},{4,5},{5,4},{6,7},{7,6},{8,9},{9,8},{10,11... | collective-permute-start | bytes 147464 | tf_op jit(solution)/shard_map/ppermute | solution.py:383
  26.9 26.6 %collective-permute-start.11 = (bf16[4,144,512]{2,1,0:T(8,128)(2,1)}, bf16[4,144,512]{2,1,0:T(8,128)(2,1)}, u32[]{:S(2)}, u32[]{:S(2)}) collective-permute-start(bf16[4,144,512]{2,1,0:T(8,128)(2,1)} %get-tuple-element.129), channel_id=1, source_target_pairs={{0,16},{4,20},{8,24},{12,28},{16,0},{20,4},{24,8},{28,12},{1,17},{... | collective-permute-start | bytes 1769480 | tf_op jit(solution)/shard_map/ppermute | solution.py:383
  28.4 26.8 %collective-permute-start.12 = (bf16[4,144,512]{2,1,0:T(8,128)(2,1)}, bf16[4,144,512]{2,1,0:T(8,128)(2,1)}, u32[]{:S(2)}, u32[]{:S(2)}) collective-permute-start(bf16[4,144,512]{2,1,0:T(8,128)(2,1)} %get-tuple-element.129), channel_id=1, source_target_pairs={{0,24},{4,28},{8,16},{12,20},{16,8},{20,12},{24,0},{28,4},{1,25},{... | collective-permute-start | bytes 1769480 | tf_op jit(solution)/shard_map/ppermute | solution.py:383
  53.5 26.8 %collective-permute-start.17 = (bf16[256,512]{1,0:T(8,128)(2,1)}, bf16[256,512]{1,0:T(8,128)(2,1)}, u32[]{:S(2)}, u32[]{:S(2)}) collective-permute-start(bf16[256,512]{1,0:T(8,128)(2,1)} %get-tuple-element.117), channel_id=1, source_target_pairs={{0,1},{1,0},{2,3},{3,2},{4,5},{5,4},{6,7},{7,6},{8,9},{9,8},{10,11... | collective-permute-start | bytes 786440 | tf_op jit(solution)/shard_map/ppermute | solution.py:383
  58.3 53.9 %collective-permute-start.13 = (bf16[4,4,144,512]{3,2,1,0:T(8,128)(2,1)}, bf16[4,4,144,512]{3,2,1,0:T(8,128)(2,1)}, u32[]{:S(2)}, u32[]{:S(2)}) collective-permute-start(bf16[4,4,144,512]{3,2,1,0:T(8,128)(2,1)} %get-tuple-element.80), channel_id=1, source_target_pairs={{0,4},{4,0},{8,12},{12,8},{16,20},{20,16},{24,28},{28,24},{1,5},{5... | collective-permute-start | bytes 7077896 | tf_op jit(solution)/shard_map/ppermute | solution.py:383
  66.9 19.8 %collective-permute-start.18 = (bf16[256,512]{1,0:T(8,128)(2,1)}, bf16[256,512]{1,0:T(8,128)(2,1)}, u32[]{:S(2)}, u32[]{:S(2)}) collective-permute-start(bf16[256,512]{1,0:T(8,128)(2,1)} %get-tuple-element.116), channel_id=1, source_target_pairs={{0,2},{1,3},{2,0},{3,1},{4,6},{5,7},{6,4},{7,5},{8,10},{9,11},{10,... | collective-permute-start | bytes 786440 | tf_op jit(solution)/shard_map/ppermute | solution.py:383
  72.7 17.2 %collective-permute-start.6 = (bf16[4,4,48,512]{3,2,1,0:T(8,128)(2,1)}, bf16[4,4,48,512]{3,2,1,0:T(8,128)(2,1)}, u32[]{:S(2)}, u32[]{:S(2)}) collective-permute-start(bf16[4,4,48,512]{3,2,1,0:T(8,128)(2,1)} %get-tuple-element.127), channel_id=1, source_target_pairs={{0,4},{4,0},{8,12},{12,8},{16,20},{20,16},{24,28},{28,24},{1,5},{5... | collective-permute-start | bytes 2359304 | tf_op jit(solution)/shard_map/ppermute | solution.py:383
  181.0 65.3 %collective-permute-start.23 = (bf16[4,4,4,16,512]{4,3,1,0,2:T(8,128)(2,1)}, bf16[4,4,4,16,512]{4,3,1,0,2:T(8,128)(2,1)}, u32[]{:S(2)}, u32[]{:S(2)}) collective-permute-start(bf16[4,4,4,16,512]{4,3,1,0,2:T(8,128)(2,1)} %bitcast.299), channel_id=1, source_target_pairs={{0,4},{4,0},{8,12},{12,8},{16,20},{20,16},{24,28},{28,24},{1,5},{5... | collective-permute-start | bytes 3145736 | tf_op jit(solution)/shard_map/ppermute | solution.py:383
  184.4 67.6 %collective-permute-start.20 = (bf16[256,512]{1,0:T(8,128)(2,1)S(1)}, bf16[256,512]{1,0:T(8,128)(2,1)S(1)}, u32[]{:S(2)}, u32[]{:S(2)}) collective-permute-start(bf16[256,512]{1,0:T(8,128)(2,1)S(1)} %get-tuple-element.109), channel_id=1, source_target_pairs={{0,1},{1,0},{2,3},{3,2},{4,5},{5,4},{6,7},{7,6},{8,9},{9,8},{10,11... | collective-permute-start | bytes 786440 | tf_op jit(solution)/shard_map/ppermute | solution.py:383
  190.6 62.4 %collective-permute-start.21 = (bf16[256,512]{1,0:T(8,128)(2,1)S(1)}, bf16[256,512]{1,0:T(8,128)(2,1)}, u32[]{:S(2)}, u32[]{:S(2)}) collective-permute-start(bf16[256,512]{1,0:T(8,128)(2,1)S(1)} %get-tuple-element.108), channel_id=1, source_target_pairs={{0,2},{1,3},{2,0},{3,1},{4,6},{5,7},{6,4},{7,5},{8,10},{9,11},{10,... | collective-permute-start | bytes 786440 | tf_op jit(solution)/shard_map/ppermute | solution.py:383
  190.7 63.4 %collective-permute-start.22 = (bf16[256,512]{1,0:T(8,128)(2,1)S(1)}, bf16[256,512]{1,0:T(8,128)(2,1)}, u32[]{:S(2)}, u32[]{:S(2)}) collective-permute-start(bf16[256,512]{1,0:T(8,128)(2,1)S(1)} %get-tuple-element.107), channel_id=1, source_target_pairs={{0,3},{1,2},{2,1},{3,0},{4,7},{5,6},{6,5},{7,4},{8,11},{9,10},{10,... | collective-permute-start | bytes 786440 | tf_op jit(solution)/shard_map/ppermute | solution.py:383
  253.1 31.9 %collective-permute-start.14 = (bf16[256,512]{1,0:T(8,128)(2,1)S(1)}, bf16[256,512]{1,0:T(8,128)(2,1)S(1)}, u32[]{:S(2)}, u32[]{:S(2)}) collective-permute-start(bf16[256,512]{1,0:T(8,128)(2,1)S(1)} %get-tuple-element.125), channel_id=1, source_target_pairs={{0,1},{1,0},{2,3},{3,2},{4,5},{5,4},{6,7},{7,6},{8,9},{9,8},{10,11... | collective-permute-start | bytes 786440 | tf_op jit(solution)/shard_map/ppermute | solution.py:383
  254.1 31.4 %collective-permute-start.15 = (bf16[256,512]{1,0:T(8,128)(2,1)S(1)}, bf16[256,512]{1,0:T(8,128)(2,1)S(1)}, u32[]{:S(2)}, u32[]{:S(2)}) collective-permute-start(bf16[256,512]{1,0:T(8,128)(2,1)S(1)} %get-tuple-element.124), channel_id=1, source_target_pairs={{0,2},{1,3},{2,0},{3,1},{4,6},{5,7},{6,4},{7,5},{8,10},{9,11},{10,... | collective-permute-start | bytes 786440 | tf_op jit(solution)/shard_map/ppermute | solution.py:383
  257.7 29.1 %collective-permute-start.16 = (bf16[256,512]{1,0:T(8,128)(2,1)S(1)}, bf16[256,512]{1,0:T(8,128)(2,1)S(1)}, u32[]{:S(2)}, u32[]{:S(2)}) collective-permute-start(bf16[256,512]{1,0:T(8,128)(2,1)S(1)} %get-tuple-element.123), channel_id=1, source_target_pairs={{0,3},{1,2},{2,1},{3,0},{4,7},{5,6},{6,5},{7,4},{8,11},{9,10},{10,... | collective-permute-start | bytes 786440 | tf_op jit(solution)/shard_map/ppermute | solution.py:383
  264.7 18.5 %collective-permute-start.28 = (bf16[4,16,512]{2,1,0:T(8,128)(2,1)S(1)}, bf16[4,16,512]{2,1,0:T(8,128)(2,1)S(1)}, u32[]{:S(2)}, u32[]{:S(2)}) collective-permute-start(bf16[4,16,512]{2,1,0:T(8,128)(2,1)S(1)} %get-tuple-element.166), channel_id=1, source_target_pairs={{0,2},{1,3},{2,0},{3,1},{4,6},{5,7},{6,4},{7,5},{8,10},{9,11},{10,... | collective-permute-start | bytes 196616 | tf_op jit(solution)/shard_map/ppermute | solution.py:383
  283.2 42.8 %collective-permute-start.37 = (bf16[4,4,2,64,512]{4,3,2,0,1:T(8,128)(2,1)S(1)}, bf16[4,4,2,64,512]{4,3,2,0,1:T(8,128)(2,1)S(1)}, u32[]{:S(2)}, u32[]{:S(2)}) collective-permute-start(bf16[4,4,2,64,512]{4,3,2,0,1:T(8,128)(2,1)S(1)} %copy.143), channel_id=1, source_target_pairs={{0,4},{4,0},{8,12},{12,8},{16,20},{20,16},{24,28},{28,24},{1,5},{5... | collective-permute-start | bytes 6291464 | tf_op jit(solution)/shard_map/ppermute | solution.py:383
  307.3 17.8 %collective-permute-start.35 = (bf16[8,16,512]{2,1,0:T(8,128)(2,1)S(1)}, bf16[8,16,512]{2,1,0:T(8,128)(2,1)S(1)}, u32[]{:S(2)}, u32[]{:S(2)}) collective-permute-start(bf16[8,16,512]{2,1,0:T(8,128)(2,1)S(1)} %get-tuple-element.156), channel_id=1, source_target_pairs={{0,2},{1,3},{2,0},{3,1},{4,6},{5,7},{6,4},{7,5},{8,10},{9,11},{10,... | collective-permute-start | bytes 393224 | tf_op jit(solution)/shard_map/ppermute | solution.py:383
  328.6 23.4 %collective-permute-start.39 = (bf16[4,2,64,512]{3,2,1,0:T(8,128)(2,1)S(1)}, bf16[4,2,64,512]{3,2,1,0:T(8,128)(2,1)S(1)}, u32[]{:S(2)}, u32[]{:S(2)}) collective-permute-start(bf16[4,2,64,512]{3,2,1,0:T(8,128)(2,1)S(1)} %get-tuple-element.86), channel_id=1, source_target_pairs={{0,16},{4,20},{8,24},{12,28},{16,0},{20,4},{24,8},{28,12},{1,17},{... | collective-permute-start | bytes 1572872 | tf_op jit(solution)/shard_map/ppermute | solution.py:383
  329.0 23.1 %collective-permute-start.40 = (bf16[4,2,64,512]{3,2,1,0:T(8,128)(2,1)S(1)}, bf16[4,2,64,512]{3,2,1,0:T(8,128)(2,1)S(1)}, u32[]{:S(2)}, u32[]{:S(2)}) collective-permute-start(bf16[4,2,64,512]{3,2,1,0:T(8,128)(2,1)S(1)} %get-tuple-element.85), channel_id=1, source_target_pairs={{0,24},{4,28},{8,16},{12,20},{16,8},{20,12},{24,0},{28,4},{1,25},{... | collective-permute-start | bytes 1572872 | tf_op jit(solution)/shard_map/ppermute | solution.py:383
  380.9 22.6 %collective-permute-start.48 = (bf16[4,2,64,512]{3,2,1,0:T(8,128)(2,1)S(1)}, bf16[4,2,64,512]{3,2,1,0:T(8,128)(2,1)}, u32[]{:S(2)}, u32[]{:S(2)}) collective-permute-start(bf16[4,2,64,512]{3,2,1,0:T(8,128)(2,1)S(1)} %get-tuple-element.142), channel_id=1, source_target_pairs={{0,16},{4,20},{8,24},{12,28},{16,0},{20,4},{24,8},{28,12},{1,17},{... | collective-permute-start | bytes 1572872 | tf_op jit(solution)/shard_map/ppermute | solution.py:383
  382.6 21.9 %collective-permute-start.49 = (bf16[4,2,64,512]{3,2,1,0:T(8,128)(2,1)S(1)}, bf16[4,2,64,512]{3,2,1,0:T(8,128)(2,1)}, u32[]{:S(2)}, u32[]{:S(2)}) collective-permute-start(bf16[4,2,64,512]{3,2,1,0:T(8,128)(2,1)S(1)} %get-tuple-element.142), channel_id=1, source_target_pairs={{0,24},{4,28},{8,16},{12,20},{16,8},{20,12},{24,0},{28,4},{1,25},{... | collective-permute-start | bytes 1572872 | tf_op jit(solution)/shard_map/ppermute | solution.py:383
  (79 other events, 706.1 us)

commit v2 on v0

--- a/solution.py
+++ b/solution.py
@@ -1,6 +1,10 @@
+import functools
+
 import jax
 import jax.numpy as jnp
 from jax import lax
+from jax.experimental import pallas as pl
+from jax.experimental.pallas import tpu as pltpu
 from jax.sharding import PartitionSpec as P
 
 D = 512
@@ -147,7 +151,7 @@
     return newton_one * iterate + applied
 
 
-def shards(
+def general_shards(
     layer_in,
     doc_ids,
     out_grad,
@@ -361,6 +365,950 @@
     return (layer_out, in_grad) + buffers + new_weights + (small_new, first_new, second_new)
 
 
+max_doc = 512
+q_rows = 256
+f32 = jnp.float32
+bf16 = jnp.bfloat16
+nt = (((1,), (1,)), ((), ()))
+nn = (((1,), (0,)), ((), ()))
+tn = (((0,), (0,)), ((), ()))
+gelu_root = 0.7978845608028654
+gelu_cube = 0.044715
+
+
+def mm(a, b, dims):
+    return lax.dot_general(a, b, dims, preferred_element_type=f32)
+
+
+def swap(x, axis, mask):
+    size = lax.axis_size(axis)
+    return lax.ppermute(x, axis, [(a, a ^ mask) for a in range(size)])
+
+
+def reorder(x, index, axis):
+    parts = [
+        lax.dynamic_slice_in_dim(x, slot ^ index, 1, axis) for slot in range(x.shape[axis])
+    ]
+    return jnp.concatenate(parts, axis)
+
+
+def pick(x, index):
+    return lax.dynamic_index_in_dim(x, index, 0, keepdims=False)
+
+
+def like(shape, dtype):
+    return jax.ShapeDtypeStruct(shape, dtype)
+
+
+whole = pl.BlockSpec(memory_space=pltpu.VMEM)
+
+
+def run(kernel, place, args, outs, name, grid=(1,), in_specs=None, out_specs=None, scratch=(), flops=0):
+    moved = sum(a.size * a.dtype.itemsize for a in args)
+    moved += sum(o.size * jnp.dtype(o.dtype).itemsize for o in outs)
+    return pl.pallas_call(
+        kernel,
+        grid_spec=pltpu.PrefetchScalarGridSpec(
+            num_scalar_prefetch=1,
+            grid=grid,
+            in_specs=in_specs or [whole] * len(args),
+            out_specs=out_specs or [whole] * len(outs),
+            scratch_shapes=list(scratch),
+        ),
+        out_shape=list(outs),
+        compiler_params=pltpu.CompilerParams(vmem_limit_bytes=56 << 20),
+        cost_estimate=pl.CostEstimate(flops=flops, bytes_accessed=moved, transcendentals=0),
+        name=name,
+    )(place, *args)
+
+
+def weight_pieces_kernel(place, q, k, v, o, e, c, qkv_out, rest_out, turned):
+    span = o.shape[0]
+    at = pl.multiple_of(place[1] * span, span)
+    for which, ref in enumerate((q, k, v)):
+        turned[...] = ref[...].T
+        qkv_out[which * span : (which + 1) * span, :] = turned[pl.ds(at, span), :].astype(bf16)
+    hid = e.shape[0]
+    rest_out[:span, :] = o[...].astype(bf16)
+    rest_out[span : span + hid, :] = e[...].astype(bf16)
+    rest_out[span + hid :, :] = c[...].astype(bf16)
+
+
+def buffer_pieces_kernel(place, q, k, v, o, e, c, att_out, ffn_out, turned):
+    span = o.shape[0]
+    at = pl.multiple_of(place[1] * span, span)
+    for which, ref in enumerate((q, k, v)):
+        turned[...] = ref[...].T
+        att_out[which] = 0.5 * turned[pl.ds(at, span), :]
+    att_out[3] = 0.5 * o[...]
+    ffn_out[0] = 0.5 * c[...]
+    ffn_out[1] = 0.5 * e[...]
+
+
+def pieces(kernel, place, arrays, outs, name):
+    q, k, v, o, e, c = arrays
+    spots = lax.axis_size("dp")
+    span, hid = o.shape[0] // spots, e.shape[0] // spots
+    row = lambda size: pl.BlockSpec((size, D), lambda g, place: (place[1], 0))
+    return run(
+        kernel,
+        place,
+        arrays,
+        outs,
+        name,
+        in_specs=[whole, whole, whole, row(span), row(hid), row(hid)],
+        scratch=[pltpu.VMEM((q.shape[1], D), f32)],
+    )
+
+
+def split_positions_kernel(place, *refs):
+    count = len(refs) // 2
+    for u in range(count):
+        refs[count + u][...] = refs[u][0].astype(bf16)
+
+
+def split_positions(x, place):
+    planes, span, width = x.shape
+    block = lambda u: pl.BlockSpec((1, span, width), lambda g, place: (place[0] ^ u, 0, 0))
+    return run(
+        split_positions_kernel,
+        place,
+        [x] * planes,
+        [like((span, width), bf16)] * planes,
+        "split_positions",
+        in_specs=[block(u) for u in range(planes)],
+    )
+
+
+def join_positions_kernel(place, *refs):
+    out = refs[-1]
+    for u, ref in enumerate(refs[:-1]):
+        out[place[0] ^ u] = ref[...].astype(f32)
+
+
+def join_positions(parts, place):
+    span, width = parts[0].shape
+    return run(
+        join_positions_kernel,
+        place,
+        parts,
+        [like((len(parts), span, width), f32)],
+        "join_positions",
+    )[0]
+
+
+def window(first_row):
+    return max(0, first_row + 1 - max_doc) // 128 * 128
+
+
+def pair_weights(halves, which, span):
+    return jnp.concatenate([half[0, which * span : (which + 1) * span, :] for half in halves], 0)
+
+
+def interleave(own, other):
+    return [half for pair in zip(own, other) for half in pair]
+
+
+def forward_kernel(place, last_ref, in_ref, *refs):
+    halves, (qkv_ref, o_ref) = refs[:-2], refs[-2:]
+    length = in_ref.shape[0]
+    span = halves[0].shape[1] // 3
+    for which in range(3):
+        weight = pair_weights(halves, which, span)
+        qkv_ref[which] = mm(in_ref[...], weight, nt).astype(bf16)
+    lane = lax.broadcasted_iota(jnp.int32, (q_rows, 128), 1)
+    for first in range(0, length, q_rows):
+        low, high = window(first), first + q_rows
+        row = first + lax.broadcasted_iota(jnp.int32, (q_rows, high - low), 0)
+        col = low + lax.broadcasted_iota(jnp.int32, (q_rows, high - low), 1)
+        allowed = (col <= row) & (row <= last_ref[:, low:high])
+        query = qkv_ref[0, first:high, :] * jnp.asarray(HEAD_DIM**-0.5, bf16)
+        halves = []
+        for half in range(2):
+            mine = (lane >= HEAD_DIM * half) & (lane < HEAD_DIM * (half + 1))
+            scores = mm(jnp.where(mine, query, jnp.zeros_like(query)), qkv_ref[1, low:high, :], nt)
+            scores = jnp.where(allowed, scores, mask_fill)
+            weight = jnp.exp(scores - jnp.max(scores, axis=1, keepdims=True))
+            total = jnp.sum(weight, axis=1, keepdims=True)
+            halves.append(mm((weight * (1.0 / total)).astype(bf16), qkv_ref[2, low:high, :], nn))
+        o_ref[first:high, :] = jnp.where(lane < HEAD_DIM, halves[0], halves[1]).astype(bf16)
+
+
+def attention(place, last, inputs, halves):
+    length = inputs.shape[0]
+    planes, rows, _ = halves[0].shape
+    half = pl.BlockSpec((1, rows, D), lambda h, place: (h, 0, 0))
+    return run(
+        forward_kernel,
+        place,
+        [last, inputs, *halves],
+        [like((3, length, D), bf16), like((length, D), bf16)],
+        "attention_forward",
+        grid=(planes,),
+        in_specs=[whole, whole] + [half] * len(halves),
+        out_specs=[
+            pl.BlockSpec((3, length, 128), lambda h, place: (0, 0, h)),
+            pl.BlockSpec((length, 128), lambda h, place: (0, h)),
+        ],
+        flops=8 * length * D * D + 2 * length * 768 * 512 * planes,
+    )
+
+
+def backward_kernel(is_last, spots, place, start_ref, in_ref, qkv_ref, g_ref, gout_ref, gmid_ref, *rest):
+    halves, rest = rest[:spots], rest[spots:]
+    ins, (keep_ref, give_ref, dk_ref, dv_ref, dq_ref, acc_ref) = rest[:-6], rest[-6:]
+    length = in_ref.shape[0]
+    span = halves[0].shape[1] // 3
+    chips = spots // 2
+    step = pl.program_id(0)
+    lane = lax.broadcasted_iota(jnp.int32, (q_rows, 128), 1)
+    dk_ref[...] = jnp.zeros_like(dk_ref)
+    dv_ref[...] = jnp.zeros_like(dv_ref)
+    key_t = qkv_ref[1].astype(f32).T.astype(bf16)
+    for first in range(0, length, q_rows):
+        low, high = window(first), first + q_rows
+        col = low + lax.broadcasted_iota(jnp.int32, (high - low, q_rows), 0)
+        row = first + lax.broadcasted_iota(jnp.int32, (high - low, q_rows), 1)
+        allowed = (col <= row) & (col >= start_ref[:, first:high])
+        query = qkv_ref[0, first:high, :] * jnp.asarray(HEAD_DIM**-0.5, bf16)
+        grad = g_ref[first:high, :]
+        key = qkv_ref[1, low:high, :]
+        value = qkv_ref[2, low:high, :]
+        dk = dk_ref[low:high, :]
+        dv = dv_ref[low:high, :]
+        dq = []
+        for half in range(2):
+            mine = (lane >= HEAD_DIM * half) & (lane < HEAD_DIM * (half + 1))
+            q_half = jnp.where(mine, query, jnp.zeros_like(query))
+            g_half = jnp.where(mine, grad, jnp.zeros_like(grad))
+            scores = jnp.where(allowed, mm(key, q_half, nt), mask_fill)
+            weight = jnp.exp(scores - jnp.max(scores, axis=0, keepdims=True))
+            probs = weight * (1.0 / jnp.sum(weight, axis=0, keepdims=True))
+            g_probs = mm(value, g_half, nt)
+            delta = jnp.sum(probs * g_probs, axis=0, keepdims=True)
+            g_scores = (probs * (g_probs - delta)).astype(bf16)
+            dv = dv + mm(probs.astype(bf16), g_half, nn)
+            dk = dk + mm(g_scores, q_half, nn)
+            dq.append(mm(key_t[HEAD_DIM * half : HEAD_DIM * (half + 1), low:high], g_scores, nn))
+        dk_ref[low:high, :] = dk
+        dv_ref[low:high, :] = dv
+        dq = jnp.concatenate(dq, 0) * HEAD_DIM**-0.5
+        dq_ref[first:high, :] = dq.T.astype(bf16)
+    grads = (dq_ref[...], dk_ref[...].astype(bf16), dv_ref[...].astype(bf16))
+
+    @pl.when(step == 0)
+    def _():
+        acc_ref[...] = gmid_ref[...]
+
+    for which, grad in enumerate(grads):
+        acc_ref[...] += mm(grad, pair_weights(halves, which, span), nn)
+    for which in range(4):
+        if which < 3:
+            rows = mm(grads[which], in_ref[...], tn).astype(bf16)
+        else:
+            rows = gout_ref[...]
+        for m in range(chips):
+            for c, ref in enumerate((keep_ref, give_ref)):
+                at = (2 * m + c) * span
+                ref[m, 0, which * span : (which + 1) * span, :] = rows[at : at + span, :]
+
+    @pl.when(step == pl.num_programs(0) - 1)
+    def _():
+        if not is_last:
+            ins[0][...] = acc_ref[...]
+            return
+        rows = ins[0].shape[0]
+        for u, ref in enumerate(ins):
+            at = pl.multiple_of((place[0] ^ u) * rows, rows)
+            ref[...] = acc_ref[pl.ds(at, rows), :].astype(bf16)
+
+
+def attention_back(
+    place, start, inputs, halves, qkv, heads_grad, grad_output, so_far, first, count, is_last
+):
+    length = inputs.shape[0]
+    planes, rows, _ = halves[0].shape
+    spots = len(halves)
+    chips = spots // 2
+    span = rows // 3
+    half = pl.BlockSpec((1, rows, D), lambda h, place: (first + h, 0, 0))
+    out_half = pl.BlockSpec((chips, 1, 4 * span, D), lambda h, place: (0, h, 0, 0))
+    outs = [like((length // planes, D), bf16)] * planes if is_last else [like((length, D), f32)]
+    out = run(
+        functools.partial(backward_kernel, is_last, spots),
+        place,
+        [start, inputs, qkv, heads_grad, grad_output, so_far, *halves],
+        outs + [like((chips, count, 4 * span, D), bf16)] * 2,
+        "attention_backward",
+        grid=(count,),
+        in_specs=[
+            whole,
+            whole,
+            pl.BlockSpec((3, length, 128), lambda h, place: (0, 0, first + h)),
+            pl.BlockSpec((length, 128), lambda h, place: (0, first + h)),
+            pl.BlockSpec((128, D), lambda h, place: (first + h, 0)),
+            whole,
+        ]
+        + [half] * spots,
+        out_specs=[whole] * len(outs) + [out_half] * 2,
+        scratch=[
+            pltpu.VMEM((length, 128), f32),
+            pltpu.VMEM((length, 128), f32),
+            pltpu.VMEM((length, 128), bf16),
+            pltpu.VMEM((length, D), f32),
+        ],
+        flops=(12 * length * D * D + 5 * length * 768 * 512 * planes) * count // planes,
+    )
+    return out[:-2], out[-2], out[-1]
+
+
+def ffn_kernel(planes, spots, place, *refs):
+    alphas, in_ref, heads_ref = refs[:3]
+    ups = refs[3 : 3 + planes]
+    halves = refs[3 + planes : 3 + planes + spots]
+    bias_ref, bout_ref = refs[3 + planes + spots : 5 + planes + spots]
+    outs = refs[5 + planes + spots :]
+    lays = outs[:planes]
+    g_ref, gout_ref, gheads_ref, gmid_ref, gbin_ref, gbout_ref, galpha_ref = outs[
+        planes : planes + 7
+    ]
+    attended, middle, mid_low, g_low, up, branch, o_low, lay, weights = outs[planes + 7 :]
+    chips = spots // 2
+    length = in_ref.shape[0]
+    block = length // planes
+    hid = g_ref.shape[3] // planes
+    span = halves[0].shape[1] - 2 * hid
+    core, chip = pl.program_id(0), pl.program_id(1)
+    alpha_att, alpha_ffn = alphas[0], alphas[1]
+    tiles = [slice(at, at + 256) for at in range(0, length, 256)]
+
+    @pl.when((core == 0) & (chip == 0))
+    def _():
+        for k in range(planes):
+            for at, half in enumerate(halves):
+                m, c = at // 2, at % 2
+                row = (k * spots + at) * span
+                o_low[row : row + span, :] = half[k, :span, :]
+                row = span
+                for which in range(2):
+                    weights[c, m, which, k * hid : (k + 1) * hid, :] = half[k, row : row + hid, :]
+                    row += hid
+        for u in range(planes):
+            at = pl.multiple_of((place[0] ^ u) * block, block)
+            up[pl.ds(at, block), :] = ups[u][...]
+        total = jnp.zeros((1, D), f32)
+        for t in tiles:
+            found = mm(heads_ref[t, :], o_low[...], nn)
+            attended[t, :] = found
+            mid = in_ref[t, :].astype(f32) + alpha_att * found
+            middle[t, :] = mid
+            mid_low[t, :] = mid.astype(bf16)
+            upstream = up[t, :].astype(f32)
+            grad = (alpha_ffn * upstream).astype(bf16)
+            g_low[t, :] = grad
+            total = total + jnp.sum(grad.astype(f32), axis=0, keepdims=True)
+            branch[t, :] = jnp.zeros((256, D), f32)
+            gmid_ref[t, :] = upstream
+        gbout_ref[...] = total
+
+    expand = weights[core, chip, 0]
+    contract = weights[core, chip, 1]
+    bias = bias_ref[0, 0]
+    gc = jnp.zeros((planes * hid, D), f32)
+    ge = jnp.zeros((planes * hid, D), f32)
+    gb = jnp.zeros((1, planes * hid), f32)
+    for t in tiles:
+        mid = mid_low[t, :]
+        grad = g_low[t, :]
+        pre = mm(mid, expand, nt) + bias
+        square = pre * pre
+        tanh = jnp.tanh(gelu_root * pre * (1.0 + gelu_cube * square))
+        half = 0.5 * (1.0 + tanh)
+        hidden = (pre * half).astype(bf16)
+        slope = half + (0.5 * gelu_root) * pre * (1.0 - tanh * tanh) * (
+            1.0 + (3.0 * gelu_cube) * square
+        )
+        branch[t, :] += mm(hidden, contract, nn)
+        g_pre = (mm(grad, contract, nt) * slope).astype(bf16)
+        gmid_ref[t, :] += mm(g_pre, expand, nn)
+        gc = gc + mm(hidden, grad, tn)
+        ge = ge + mm(g_pre, mid, tn)
+        gb = gb + jnp.sum(g_pre.astype(f32), axis=0, keepdims=True)
+    g_ref[0, 0, 0] = gc.astype(bf16)
+    g_ref[0, 0, 1] = ge.astype(bf16)
+    gbin_ref[0, 0] = gb
+
+    @pl.when((core == 1) & (chip == chips - 1))
+    def _():
+        sum_ffn = jnp.zeros((1, D), f32)
+        sum_att = jnp.zeros((1, D), f32)
+        gout = jnp.zeros((D, D), f32)
+        for t in tiles:
+            final = branch[t, :] + bout_ref[...]
+            lay[t, :] = middle[t, :] + alpha_ffn * final
+            sum_ffn = sum_ffn + jnp.sum(up[t, :].astype(f32) * final, axis=0, keepdims=True)
+            gm = gmid_ref[t, :]
+            sum_att = sum_att + jnp.sum(gm * attended[t, :], axis=0, keepdims=True)
+            g_att = (alpha_att * gm).astype(bf16)
+            gout = gout + mm(heads_ref[t, :], g_att, tn)
+            gheads_ref[t, :] = mm(g_att, o_low[...], nt).astype(bf16)
+        gout_ref[...] = gout.astype(bf16)
+        galpha_ref[0:1, :] = sum_att
+        galpha_ref[1:2, :] = sum_ffn
+        for u, ref in enumerate(lays):
+            at = pl.multiple_of((place[0] ^ u) * block, block)
+            ref[...] = lay[pl.ds(at, block), :].astype(bf16)
+
+
+def feed_forward(place, alphas, inputs, heads, ups, halves, bias, bout):
+    length = inputs.shape[0]
+    planes = len(ups)
+    spots = len(halves)
+    chips = spots // 2
+    hid = bias.shape[-1]
+    step = lambda *tail: pl.BlockSpec((1, 1) + tail, lambda c, m, place: (c, m) + (0,) * len(tail))
+    out = run(
+        functools.partial(ffn_kernel, planes, spots),
+        place,
+        [alphas, inputs, heads, *ups, *halves, bias, bout],
+        [like((length // planes, D), bf16)] * planes
+        + [
+            like((2, chips, 2, hid, D), bf16),
+            like((D, D), bf16),
+            like((length, D), bf16),
+            like((length, D), f32),
+            like((2, chips, 1, hid), f32),
+            like((1, D), f32),
+            like((2, D), f32),
+        ],
+        "feed_forward",
+        grid=(2, chips),
+        in_specs=[pl.BlockSpec(memory_space=pltpu.SMEM)]
+        + [whole] * (2 + planes + spots)
+        + [step(1, hid), whole],
+        out_specs=[whole] * planes
+        + [step(2, hid, D), whole, whole, whole, step(1, hid), whole, whole],
+        scratch=[
+            pltpu.VMEM((length, D), f32),
+            pltpu.VMEM((length, D), f32),
+            pltpu.VMEM((length, D), bf16),
+            pltpu.VMEM((length, D), bf16),
+            pltpu.VMEM((length, D), bf16),
+            pltpu.VMEM((length, D), f32),
+            pltpu.VMEM((D, D), bf16),
+            pltpu.VMEM((length, D), f32),
+            pltpu.VMEM((2, chips, 2, hid, D), bf16),
+        ],
+        flops=12 * length * D * 2 * chips * hid,
+    )
+    return out[:planes], out[planes:]
+
+
+def sum_kernel(count, place, *refs):
+    ins, outs = refs[:count], refs[count:]
+    rows = outs[0].shape[0]
+    for at, out in enumerate(outs):
+        span = slice(at * rows, (at + 1) * rows)
+        total = ins[0][span, :].astype(f32)
+        for ref in ins[1:]:
+            total = total + ref[span, :].astype(f32)
+        out[...] = total.astype(out.dtype)
+
+
+def sum_parts(place, ins, parts, name):
+    rows = ins[0].shape[0] // parts
+    return run(
+        functools.partial(sum_kernel, len(ins)),
+        place,
+        ins,
+        [like((rows, ins[0].shape[1]), bf16)] * parts,
+        name,
+    )
+
+
+def small_write(out, total):
+    at = out.shape[0] - 2 * total.shape[0]
+    high = total.astype(bf16)
+    out[at : at + total.shape[0], :] = high
+    out[at + total.shape[0] :, :] = (total - high.astype(f32)).astype(bf16)
+
+
+def small_read(ref):
+    rows = ref.shape[0]
+    return ref[rows - 16 : rows - 8, :].astype(f32) + ref[rows - 8 :, :].astype(f32)
+
+
+def ffn_core_kernel(place, own, got, small, *outs):
+    rows = own.shape[0] // len(outs)
+    total = small[...]
+    for at, out in enumerate(outs):
+        for r in range(0, rows, 256):
+            a = own[at * rows + r : at * rows + r + 256, :].astype(f32)
+            b = got[at * rows + r : at * rows + r + 256, :].astype(f32)
+            out[r : r + 256, :] = (a + b).astype(bf16)
+        small_write(out, total)
+
+
+def ffn_chip_kernel(count, hid, place, *refs):
+    ins, outs = refs[:count], refs[count:]
+    small = small_read(ins[0])
+    for ref in ins[1:]:
+        small = small + small_read(ref)
+    for k, out in enumerate(outs):
+        for which in range(2):
+            at = (which * len(outs) + k) * hid
+            total = ins[0][at : at + hid, :].astype(f32)
+            for ref in ins[1:]:
+                total = total + ref[at : at + hid, :].astype(f32)
+            out[which * hid : (which + 1) * hid, :] = total.astype(bf16)
+        small_write(out, small)
+
+
+def ffn_plane_kernel(place, old, *refs):
+    ins, (out, small_out) = refs[:-2], refs[-2:]
+    rows = out.shape[0]
+    total = old[...].reshape(rows, D)
+    small = small_read(ins[0])
+    for ref in ins:
+        total = total + ref[:rows, :].astype(f32)
+    for ref in ins[1:]:
+        small = small + small_read(ref)
+    out[...] = total.astype(bf16)
+    small_out[...] = small
+
+
+def att_to_owner_kernel(chips, planes, place, *refs):
+    ins, old, outs, scratch = refs[:chips], refs[chips], refs[chips + 1 : -1], refs[-1]
+    span = old.shape[1]
+    for k in range(planes):
+        for which in range(4):
+            at = (k * 4 + which) * span
+            total = ins[0][at : at + span, :].astype(f32)
+            for ref in ins[1:]:
+                total = total + ref[at : at + span, :].astype(f32)
+            if k == 0:
+                total = total + old[which]
+            scratch[which, k * span : (k + 1) * span, :] = total.astype(bf16)
+    for u, out in enumerate(outs):
+        out[...] = scratch[place[0] ^ u]
+
+
+def att_sum_kernel(planes, place, *refs):
+    ins, out = refs[:-1], refs[-1]
+    span = out.shape[0] // planes
+    for k in range(planes):
+        total = jnp.zeros((span, D), f32)
+        for u, ref in enumerate(ins):
+            at = (k ^ u) * span
+            total = total + ref[at : at + span, :].astype(f32)
+        out[k * span : (k + 1) * span, :] = total.astype(bf16)
+
+
+def spread_kernel(spots, place, *refs):
+    halves, outs = refs[:spots], refs[spots:]
+    span = outs[0].shape[0] // spots
+    for at, half in enumerate(halves):
+        to = pl.multiple_of((place[1] ^ at) * span, span)
+        for k, out in enumerate(outs):
+            out[pl.ds(to, span), :] = half[k * span : (k + 1) * span, :]
+
+
+def newton_kernel(planes, spots, first_only, place, *refs):
+    halves, outs, x_ref, low_ref = refs[:spots], refs[spots:-2], refs[-2], refs[-1]
+    dim, cols = x_ref.shape
+    span = cols // (planes * spots)
+    group = spots * span
+    chunk = 512
+    total = jnp.zeros((1, D), f32)
+    for half in halves:
+        part = half[: planes * span, :].astype(f32)
+        total = total + jnp.sum(part * part, axis=0, keepdims=True)
+    inverse = 1.0 / (jnp.sqrt(jnp.sum(total, axis=1, keepdims=True)) + 1e-07)
+    for k in range(planes):
+        rows = [half[k * span : (k + 1) * span, :] for half in halves]
+        part = jnp.concatenate(rows, 0).astype(f32).T * inverse
+        x_ref[:, k * group : (k + 1) * group] = part
+        low_ref[:, k * group : (k + 1) * group] = part.astype(bf16)
+    diagonal = lax.broadcasted_iota(jnp.int32, (dim, dim), 0) == lax.broadcasted_iota(
+        jnp.int32, (dim, dim), 1
+    )
+
+    def step(limit):
+        gram = jnp.zeros((dim, dim), f32)
+        for at in range(0, cols, chunk):
+            part = low_ref[:, at : at + chunk]
+            gram = gram + mm(part, part, nt)
+        trace = jnp.sum(
+            jnp.sum(jnp.where(diagonal, gram, 0.0), axis=0, keepdims=True), axis=1, keepdims=True
+        )
+        shift = trace * (1.0 / dim)
+        rest = jnp.where(diagonal, gram - shift, gram)
+        rest_low = rest.astype(bf16)
+        poly = (newton_two + 2.0 * newton_three * shift) * rest + newton_three * mm(
+            rest_low, rest_low, nn
+        )
+        poly = poly.astype(bf16)
+        scale = newton_one + newton_two * shift + newton_three * shift * shift
+        for at in range(0, limit, chunk):
+            part = scale * x_ref[:, at : at + chunk] + mm(poly, low_ref[:, at : at + chunk], nn)
+            x_ref[:, at : at + chunk] = part
+            low_ref[:, at : at + chunk] = part.astype(bf16)
+
+    @pl.loop(0, 4)
+    def _(_):
+        step(cols)
+
+    step(group if first_only else cols)
+    for k, out in enumerate(outs):
+        part = x_ref[:, k * group : (k + 1) * group].T.astype(bf16)
+        for at in range(spots):
+            to = pl.multiple_of((place[1] ^ at) * span, span)
+            out[pl.ds(to, span), :] = part[at * span : (at + 1) * span, :]
+
+
+def newton(place, halves, planes, first_only, name):
+    spots = len(halves)
+    cols = spots * halves[0].shape[0]
+    count = 1 if first_only else planes
+    return run(
+        functools.partial(newton_kernel, planes, spots, first_only),
+        place,
+        halves,
+        [like((cols // planes, D), bf16)] * count,
+        name,
+        scratch=[pltpu.VMEM((D, cols), f32), pltpu.VMEM((D, cols), bf16)],
+        flops=10 * D * D * (2 * cols + D),
+    )
+
+
+def att_final_kernel(planes, place, *refs):
+    ms, xs = refs[:planes], refs[planes : 2 * planes]
+    old = refs[2 * planes : 2 * planes + 4]
+    outs, scratch = refs[2 * planes + 4 : -1], refs[-1]
+    for u in range(planes):
+        scratch[0, u] = ms[u][...]
+        scratch[1, u] = xs[u][...]
+    for which in range(4):
+        m = scratch[0, place[0] ^ which].astype(f32)
+        x = scratch[1, place[0] ^ which].astype(f32)
+        if which < 3:
+            m, x = m.T, x.T
+        outs[which][...] = m
+        outs[4 + which][...] = old[which][...] - muon_rates[which] * x
+
+
+def ffn_give_kernel(planes, hid, place, *refs):
+    count = len(refs) // 3
+    ins, give, keep = refs[:count], refs[count : 2 * count], refs[2 * count :]
+
+    def fill(given):
+        for m in range(count):
+            for k in range(planes):
+                to = slice(k * hid, (k + 1) * hid)
+                at = (2 * k + given) * hid
+                give[m][to, :] = ins[m][at : at + hid, :]
+                at = (2 * k + 1 - given) * hid
+                keep[m][to, :] = ins[m][at : at + hid, :]
+            give[m][planes * hid :, :] = keep[m][:hid, :]
+
+    @pl.when(place[1] % 2 == 0)
+    def _():
+        fill(0)
+
+    @pl.when(place[1] % 2 == 1)
+    def _():
+        fill(1)
+
+
+def ffn_buffers_kernel(chips, hid, place, *refs):
+    give, keep, got = refs[:chips], refs[chips : 2 * chips], refs[2 * chips : 3 * chips]
+    eo, co = refs[3 * chips :]
+    tail = keep[0].shape[0]
+
+    def fill(kept, given):
+        for m in range(chips):
+            one = pl.multiple_of((place[1] ^ (2 * m)) * hid, hid)
+            two = pl.multiple_of((place[1] ^ (2 * m + 1)) * hid, hid)
+            kept[pl.ds(one, hid), :] = keep[m][:hid, :].astype(f32)
+            kept[pl.ds(two, hid), :] = got[m][:hid, :].astype(f32)
+            given[pl.ds(one, hid), :] = give[m][:hid, :].astype(f32)
+            given[pl.ds(two, hid), :] = got[m][tail:, :].astype(f32)
+
+    @pl.when(place[1] % 2 == 0)
+    def _():
+        fill(eo, co)
+
+    @pl.when(place[1] % 2 == 1)
+    def _():
+        fill(co, eo)
+
+
+def ffn_final_kernel(place, mine, got, we, wc, eo, co):
+    def fill(e, c):
+        eo[...] = we[...] - muon_rates[4] * e[...].astype(f32)
+        co[...] = wc[...] - muon_rates[5] * c[...].astype(f32)
+
+    @pl.when(place[1] % 2 == 0)
+    def _():
+        fill(mine, got)
+
+    @pl.when(place[1] % 2 == 1)
+    def _():
+        fill(got, mine)
+
+
+def shards(
+    layer_in,
+    doc_ids,
+    out_grad,
+    w_query,
+    w_key,
+    w_value,
+    w_output,
+    w_expand,
+    w_contract,
+    small_params,
+    buffer_query,
+    buffer_key,
+    buffer_value,
+    buffer_output,
+    buffer_expand,
+    buffer_contract,
+    small_first,
+    small_second,
+):
+    planes = lax.axis_size("mp")
+    spots = lax.axis_size("dp")
+    chips = spots // 2
+    plane = lax.axis_index("mp")
+    spot = lax.axis_index("dp")
+    place = jnp.stack([plane, spot]).astype(jnp.int32)
+    length = layer_in.shape[1]
+    head_cols = w_query.shape[1]
+    hidden_rows = w_expand.shape[0]
+    span = head_cols // spots
+    hid = hidden_rows // spots
+    to_planes = range(1, planes)
+    to_chips = range(1, chips)
+    weights_old = (w_query, w_key, w_value, w_output, w_expand, w_contract)
+    buffers_old = (
+        buffer_query,
+        buffer_key,
+        buffer_value,
+        buffer_output,
+        buffer_expand,
+        buffer_contract,
+    )
+
+    def around_planes(x):
+        return [x] + [swap(x, "mp", k) for k in to_planes]
+
+    def around_chips(x):
+        return [x] + [swap(x, "dp", 2 * m) for m in to_chips]
+
+    def together(*groups):
+        return lax.optimization_barrier(groups)
+
+    qkv_piece, rest_piece = pieces(
+        weight_pieces_kernel,
+        place,
+        weights_old,
+        [like((3 * span, D), bf16), like((span + 2 * hid, D), bf16)],
+        "weight_pieces",
+    )
+    qkv_own, rest_piece = together(jnp.stack(around_planes(qkv_piece)), rest_piece)
+    qkv_own, rest_own = around_chips(qkv_own), around_planes(rest_piece)
+    up_parts = split_positions(out_grad, place)
+    qkv_own, rest_own, up_parts = together(qkv_own, jnp.stack(rest_own), up_parts)
+    qkv_halves = interleave(qkv_own, [swap(part, "dp", 1) for part in qkv_own])
+    rest_own = around_chips(rest_own)
+    ups = [up_parts[0]] + [swap(up_parts[u], "mp", u) for u in to_planes]
+
+    def to_slots(bias):
+        return reorder(reorder(bias, plane, 0), spot, 1)
+
+    bias = to_slots(small_params[:FF].reshape(planes, spots, hid))
+    bias = bias.reshape(planes, chips, 2, hid).transpose(2, 1, 0, 3)
+    bias = bias.reshape(2, chips, 1, planes * hid)
+    bout = small_params[FF : FF + D].reshape(1, D)
+    alphas = small_params[FF + D :]
+
+    inputs = pick(layer_in, plane)
+    documents = pick(doc_ids, plane)
+    last = (
+        jnp.sum(documents[None, :] <= documents[:, None], axis=1, dtype=jnp.int32)[None, :] - 1
+    )
+    start = jnp.sum(documents[None, :] < documents[:, None], axis=1, dtype=jnp.int32)[None, :]
+
+    qkv, heads = attention(place, last, inputs, qkv_halves)
+    heads, rest_own, ups = together(heads, rest_own, ups)
+    rest_halves = interleave(rest_own, [swap(part, "dp", 1) for part in rest_own])
+    att_old, ffn_old = pieces(
+        buffer_pieces_kernel,
+        place,
+        buffers_old,
+        [like((4, span, D), f32), like((2, hid, D), f32)],
+        "buffer_pieces",
+    )
+    rest_halves, att_old, ffn_old = together(rest_halves, att_old, ffn_old)
+    lays, rest = feed_forward(place, alphas, inputs, heads, ups, rest_halves, bias, bout)
+    ffn_grad, grad_output, heads_grad, middle_grad, gb_in, gb_out, g_alpha = rest
+
+    ffn_grad = ffn_grad.reshape(2, chips * 2 * planes * hid, D)
+    ffn_got = swap(ffn_grad[1], "dp", 1)
+    lay_got = [lays[0]] + [swap(lays[u], "mp", u) for u in to_planes]
+    gb_in = gb_in.reshape(2, chips, planes, hid).transpose(2, 1, 0, 3).reshape(planes, spots, hid)
+    small = jnp.concatenate(
+        [to_slots(gb_in).reshape(-1), gb_out.reshape(-1), jnp.sum(g_alpha, axis=1)]
+    )
+    small = jnp.pad(small, (0, 8 * D - small.size)).reshape(8, D)
+    high = lax.reduce_precision(small, 8, 7)
+    pair = jnp.concatenate([high, lax.reduce_precision(small - high, 8, 7)]).astype(bf16)
+    pair = swap(pair, "dp", 1).astype(f32)
+    small = small + pair[:8] + pair[8:]
+    pairs = planes // 2
+    so_far, keep_one, give_one = attention_back(
+        place, start, inputs, qkv_halves, qkv, heads_grad, grad_output, middle_grad, 0, pairs, False
+    )
+    so_far, ffn_got, small = together(so_far, ffn_got, small)
+    parts = run(
+        ffn_core_kernel,
+        place,
+        [ffn_grad[0], ffn_got, small],
+        [like((2 * planes * hid + 16, D), bf16)] * chips,
+        "ffn_core_sum",
+    )
+    so_far, parts = together(so_far, parts)
+    got = [parts[0]] + [swap(parts[m], "dp", 2 * m) for m in to_chips]
+    ins, keep_two, give_two = attention_back(
+        place,
+        start,
+        inputs,
+        qkv_halves,
+        qkv,
+        heads_grad,
+        grad_output,
+        so_far[0],
+        pairs,
+        planes - pairs,
+        True,
+    )
+    ins, keep_two, give_two, got, lay_got = together(ins, keep_two, give_two, got, lay_got)
+
+    att_keep = jnp.concatenate([keep_one, keep_two], 1)
+    att_give = jnp.concatenate([give_one, give_two], 1)
+    att_rows = chips * planes * 4 * span
+    att_got = swap(att_give.reshape(att_rows, D), "dp", 1)
+    parts = run(
+        functools.partial(ffn_chip_kernel, chips, hid),
+        place,
+        got,
+        [like((2 * hid + 16, D), bf16)] * planes,
+        "ffn_chip_sum",
+    )
+    parts, att_got = together(parts, att_got)
+    got = [parts[0]] + [swap(parts[k], "mp", k) for k in to_planes]
+    att_parts = sum_parts(place, [att_keep.reshape(att_rows, D), att_got], chips, "att_core_sum")
+    got, att_parts = together(got, att_parts)
+    att_got = [att_parts[0]] + [swap(att_parts[m], "dp", 2 * m) for m in to_chips]
+    piece, small_grad = run(
+        ffn_plane_kernel,
+        place,
+        [ffn_old, *got],
+        [like((2 * hid, D), bf16), like((8, D), f32)],
+        "ffn_plane_sum",
+    )
+    small_grad = small_grad.reshape(-1)[: FF + D + 2]
+    piece, att_got = together(piece, att_got)
+    got = around_planes(piece)
+    parts = run(
+        functools.partial(att_to_owner_kernel, chips, planes),
+        place,
+        att_got + [att_old],
+        [like((planes * span, D), bf16)] * planes,
+        "att_chip_sum",
+        scratch=[pltpu.VMEM((4, planes * span, D), bf16)],
+    )
+    got, parts = together(got, parts)
+    att_got = [parts[0]] + [swap(parts[u], "mp", u) for u in to_planes]
+    got = around_chips(jnp.concatenate(got))
+    att_piece = run(
+        functools.partial(att_sum_kernel, planes),
+        place,
+        att_got,
+        [like((planes * span, D), bf16)],
+        "att_plane_sum",
+    )[0]
+    att_piece, ins = together(att_piece, ins)
+    att_own = around_chips(att_piece)
+    in_got = [ins[0]] + [swap(ins[u], "mp", u) for u in to_planes]
+    att_halves = interleave(att_own, [swap(part, "dp", 1) for part in att_own])
+    att_m = run(
+        functools.partial(spread_kernel, spots),
+        place,
+        att_halves,
+        [like((head_cols, D), bf16)] * planes,
+        "att_spread",
+    )
+    att_m, att_halves = together(att_m, att_halves)
+    att_m = [att_m[0]] + [swap(att_m[u], "mp", u) for u in to_planes]
+    att_x = newton(place, att_halves, planes, False, "newton_att")
+    att_x, in_got, att_m = together(att_x, in_got, att_m)
+    att_x = [att_x[0]] + [swap(att_x[u], "mp", u) for u in to_planes]
+    layer_out = join_positions(lay_got, place)
+    in_grad = join_positions(in_got, place)
+
+    outs = run(
+        functools.partial(ffn_give_kernel, planes, hid),
+        place,
+        got,
+        [like(((planes + 1) * hid, D), bf16)] * chips + [like((planes * hid, D), bf16)] * chips,
+        "ffn_give",
+    )
+    give, keep = outs[:chips], outs[chips:]
+    ffn_got = [swap(part, "dp", 1) for part in give]
+    step = newton(place, interleave(keep, ffn_got), planes, True, "newton_ffn")[0]
+    step, give, keep, ffn_got = together(step, give, keep, ffn_got)
+    step_got = swap(step, "dp", 1)
+    new_be, new_bc = run(
+        functools.partial(ffn_buffers_kernel, chips, hid),
+        place,
+        [*give, *keep, *ffn_got],
+        [like((hidden_rows, D), f32)] * 2,
+        "ffn_buffers",
+    )
+    att_out = run(
+        functools.partial(att_final_kernel, planes),
+        place,
+        att_m + att_x + list(weights_old[:4]),
+        [like(w.shape, f32) for w in weights_old[:4]] * 2,
+        "att_final",
+        scratch=[pltpu.VMEM((2, planes, head_cols, D), bf16)],
+    )
+    new_we, new_wc = run(
+        ffn_final_kernel,
+        place,
+        [step, step_got, w_expand, w_contract],
+        [like((hidden_rows, D), f32)] * 2,
+        "ffn_final",
+    )
+
+    first_new = 0.5 * small_first + 0.5 * small_grad
+    second_new = 0.5 * small_second + 0.5 * small_grad * small_grad
+    correction = 1.0 - 0.5**STEP
+    small_new = small_params - adam_rate * (first_new / correction) / (
+        jnp.sqrt(second_new / correction) + 1e-08
+    )
+    return (
+        (layer_out, in_grad)
+        + tuple(att_out[:4])
+        + (new_be, new_bc)
+        + tuple(att_out[4:])
+        + (new_we, new_wc)
+        + (small_new, first_new, second_new)
+    )
+
+
 def solution(mesh):
     in_specs = (
         P("dp", None, None),
@@ -401,4 +1349,5 @@
         P(),
         P(),
     )
-    return jax.shard_map(shards, mesh=mesh, in_specs=in_specs, out_specs=out_specs, check_vma=False)
+    block = mesh.shape["mp"] == 4 and mesh.shape["dp"] == 8
+    return jax.shard_map(shards if block else general_shards, mesh=mesh, in_specs=in_specs, out_specs=out_specs, check_vma=False)

time: 1210 us -> 328 us (0.27)
  waiting for transfers between devices: 719 us -> 49.5 us
  matrix products: 258 us -> 0 us
  Pallas kernels: 0 us -> 173 us
  blocking collectives: 94 us -> 0 us
  starting transfers between devices: 18.9 us -> 75.8 us
  other arithmetic: 43 us -> 7.5 us
  local copies, waits for them, and re-layouts: 46.1 us -> 16.5 us
  between operations: 23.3 us -> 1.96 us
    psum x6 -> x0, waiting for transfers between devices: 612 us -> none  [the longest x5 549 us: shards(): lax.psum(shortened(tuple((gram_part(iterate, column_flag) for iterate, co...]
    dot_general x138 -> x0, matrix products: 258 us -> none  [the longest x15 38.7 us: gram_part(): lax.dot_general(iterate, iterate, (((0,), (0,)), ((), ())), precision=hig...]
    pallas_call x0 -> x22, Pallas kernels: none -> 173 us  [run(): pl.pallas_call(kernel, grid_spec=pltpu.PrefetchScalarGridSpec(num_scalar_...]
    ppermute x0 -> x68, starting transfers between devices: none -> 75.8 us  [swap(): return lax.ppermute(x, axis, [(a, a ^ mask) for a in range(size)])]
    reduce_scatter x5 -> x0, waiting for transfers between devices: 68.2 us -> none  [the longest x2 51.9 us: shards(): lax.psum_scatter(partial_grad.astype(jnp.bfloat16), 'mp', scatter_dimensi...]
    psum x2 -> x0, blocking collectives: 56.6 us -> none  [the longest x1 44.3 us: shards(): small_grad = lax.psum(small_local, ('dp', 'mp'))]
    ppermute x0 -> x68, waiting for transfers between devices: none -> 49.5 us  [swap(): return lax.ppermute(x, axis, [(a, a ^ mask) for a in range(size)])]
    all_to_all x4 -> x0, waiting for transfers between devices: 38.2 us -> none  [the longest x2 24.3 us: shards(): lax.all_to_all(heads_grad_tok, 'mp', split_axis=2, concat_axis=1, tiled=T...]
  transfers between devices with their start and end apart: 17 -> 68, of which waited for: 12 -> 18; matrix products, arithmetic and copies ran while one was open for 15% -> 3% of each run, Pallas kernels for 0% -> 42%
where the time goes in v2:
time: 328 us; the launch traced here: 324 us
  Pallas kernels  173 us (53%)
  starting transfers between devices  75.8 us (23%)
  waiting for transfers between devices  49.5 us (15%)
  local copies, waits for them, and re-layouts  16.5 us (5%)
  other arithmetic  7.5 us (2%)
    pallas_call x22, Pallas kernels, run(): pl.pallas_call(kernel, grid_spec=pltpu.PrefetchScalarGridSpec(num_scalar_...  173 us
    ppermute x68, starting transfers between devices, swap(): return lax.ppermute(x, axis, [(a, a ^ mask) for a in range(size)])  75.8 us
    ppermute x68, waiting for transfers between devices, swap(): return lax.ppermute(x, axis, [(a, a ^ mask) for a in range(size)])  49.5 us
    unnamed x164, local copies, waits for them, and re-layouts  7.32 us
  transfers between devices with their start and end apart: 68, of which 18 were waited for; matrix products, arithmetic and copies ran while one was open for 3% of the time, Pallas kernels for 42%

profile of v2, /device:TPU:0, one launch (start us, length us, event | category | flops | bytes accessed | tf_op | source)
XLA Modules:
  0.0 324.0 jit_solution(8571807095769233539)
XLA Ops:
  4.0 5.0 %collective-permute-start.2 = (bf16[48,512]{1,0:T(8,128)(2,1)}, bf16[48,512]{1,0:T(8,128)(2,1)S(1)}, u32[]{:S(2)}, u32[]{:S(2)}) collective-permute-start(bf16[48,512]{1,0:T(8,128)(2,1)} %get-tuple-element.213), channel_id=1, source_target_pairs={{0,3},{1,2},{2,1},{3,0},{4,7},{5,6},{6,5},{7,4},{8,11},{9,10},{10,... | collective-permute-start | bytes 147464 | tf_op jit(solution)/shard_map/ppermute | solution.py:385
  27.1 3.3 %split_positions.1 = (bf16[256,512]{1,0:T(8,128)(2,1)}, bf16[256,512]{1,0:T(8,128)(2,1)}, bf16[256,512]{1,0:T(8,128)(2,1)}, bf16[256,512]{1,0:T(8,128)(2,1)}) custom-call(s32[2]{0:T(128)} %pad_add_fusion.place, f32[4,256,512]{2,1,0:T(8,128)} %refs_3_.1, f32[4,256,512]{2,1,0:T(8,128)} %refs_3_.1, f32[4,256,512]{2,1,0:T(8,128)} %refs_3_.1, f32[4,256,512]{2,1,0:T(8,128)} %refs_3_.1), custom_call_target="tpu_custom_call" | custom-call | bytes 9437184 | tf_op jit(solution)/shard_map/split_positions/pallas_call | solution.py:409
  31.6 4.8 %collective-permute-start.16 = (bf16[256,512]{1,0:T(8,128)(2,1)}, bf16[256,512]{1,0:T(8,128)(2,1)S(1)}, u32[]{:S(2)}, u32[]{:S(2)}) collective-permute-start(bf16[256,512]{1,0:T(8,128)(2,1)} %get-tuple-element.229), channel_id=1, source_target_pairs={{0,1},{1,0},{2,3},{3,2},{4,5},{5,4},{6,7},{7,6},{8,9},{9,8},{10,11... | collective-permute-start | bytes 786440 | tf_op jit(solution)/shard_map/ppermute | solution.py:385
  45.4 23.0 %attention_forward.1 = (bf16[3,1024,512]{2,1,0:T(8,128)(2,1)}, bf16[1024,512]{1,0:T(8,128)(2,1)}) custom-call(s32[2]{0:T(128)} %pad_add_fusion.place, s32[1,1024]{1,0:T(1,128)} %bitcast.44, bf16[1024,512]{1,0:T(8,128)(2,1)} %dynamic-slice_bitcast_fusion.in_ref.refs_1_, bf16[4,48,512]{2,1,0:T(8,128)(2,1)} %copy-done.30, bf16[4,48,512]{2,1,0:T(8,128)(2,1)} %copy-done.75, ...), custom_call_target="tpu_custom_call" | custom-call | flops 5368709120 | bytes 6819840 | tf_op jit(solution)/shard_map/attention_forward/pallas_call | solution.py:409
  74.5 31.0 %feed_forward.1 = (bf16[256,512]{1,0:T(8,128)(2,1)}, bf16[256,512]{1,0:T(8,128)(2,1)}, bf16[256,512]{1,0:T(8,128)(2,1)}, bf16[256,512]{1,0:T(8,128)(2,1)}, bf16[...) custom-call(s32[2]{0:T(128)} %pad_add_fusion.place, ...), custom_call_target="tpu_custom_call" | custom-call | flops 12884901888 | bytes 16801800 | tf_op jit(solution)/shard_map/feed_forward/pallas_call | solution.py:409
  105.6 4.7 %fusion.4 = (bf16[1,4,2,256,512]{4,3,2,1,0:T(8,128)(2,1)}, bf16[1,4,2,256,512]{4,3,2,1,0:T(8,128)(2,1)}) fusion(bf16[2,4,2,256,512]{4,3,2,1,0:T(8,128)(2,1)} %get-tuple-element.255), kind=kLoop, calls=%fused_computation.54 | loop fusion | bytes 8388608 | tf_op jit(solution)/shard_map/slice | solution.py:1177
  112.5 19.7 %attention_backward.2 = (f32[1024,512]{1,0:T(8,128)}, bf16[4,2,64,512]{3,2,1,0:T(8,128)(2,1)}, bf16[4,2,64,512]{3,2,1,0:T(8,128)(2,1)}) custom-call(s32[2]{0:T(128)} %pad_add_fusion.place, s32[1,1024]{1,0:T(1,128)} %bitcast.48, bf16[1024,512]{1,0:T(8,128)(2,1)} %dynamic-slice_bitcast_fusion.in_ref.refs_1_, bf16[3,1024,512]{2,1,0:T(8,128)(2,1)} %get-tuple-element.225.qkv_ref, ...), custom_call_target="tpu_custom_call" | custom-call | flops 5637144576 | bytes 12587008 | tf_op jit(solution)/shard_map/attention_backward/pallas_call | solution.py:409
  134.1 4.5 %ffn_core_sum.1 = (bf16[528,512]{1,0:T(8,128)(2,1)}, bf16[528,512]{1,0:T(8,128)(2,1)}, bf16[528,512]{1,0:T(8,128)(2,1)}, bf16[528,512]{1,0:T(8,128)(2,1)}) custom-call(s32[2]{0:T(128)} %pad_add_fusion.place, bf16[2048,512]{1,0:T(8,128)(2,1)} %bitcast.29, bf16[2048,512]{1,0:T(8,128)(2,1)} %copy-done.2, f32[8,512]{1,0:T(8,128)} %slice_add_fusion.small), custom_call_target="tpu_custom_call" | custom-call | bytes 6373376 | tf_op jit(solution)/shard_map/ffn_core_sum/pallas_call | solution.py:409
  145.4 19.3 %attention_backward.3 = (bf16[256,512]{1,0:T(8,128)(2,1)}, bf16[256,512]{1,0:T(8,128)(2,1)}, bf16[256,512]{1,0:T(8,128)(2,1)}, bf16[256,512]{1,0:T(8,128)(2,1)},...) custom-call(s32[2]{0:T(128)} %pad_add_fusion.place, s32[1,1024]{1,0:T(1,128)} %bitcast.49, ...), custom_call_target="tpu_custom_call" | custom-call | flops 5637144576 | bytes 11538432 | tf_op jit(solution)/shard_map/attention_backward/pallas_call | solution.py:409
  179.6 7.2 %collective-permute-done.33.refs_2_ = bf16[144,512]{1,0:T(8,128)(2,1)S(1)} collective-permute-done((bf16[144,512]{1,0:T(8,128)(2,1)}, bf16[144,512]{1,0:T(8,128)(2,1)S(1)}, u32[]{:S(2)}, u32[]{:S(2)}) %collective-permute-start.33) | collective-permute-done | bytes 147488 | tf_op jit(solution)/shard_map/ppermute | solution.py:385
  193.0 3.3 %collective-permute-done.35.refs_1_ = bf16[256,512]{1,0:T(8,128)(2,1)S(1)} collective-permute-done((bf16[256,512]{1,0:T(8,128)(2,1)}, bf16[256,512]{1,0:T(8,128)(2,1)S(1)}, u32[]{:S(2)}, u32[]{:S(2)}) %collective-permute-start.35) | collective-permute-done | bytes 262176 | tf_op jit(solution)/shard_map/ppermute | solution.py:385
  201.9 3.7 %collective-permute-start.39 = (bf16[128,512]{1,0:T(8,128)(2,1)}, bf16[128,512]{1,0:T(8,128)(2,1)S(1)}, u32[]{:S(2)}, u32[]{:S(2)}) collective-permute-start(bf16[128,512]{1,0:T(8,128)(2,1)} %get-tuple-element.375), channel_id=1, source_target_pairs={{0,2},{1,3},{2,0},{3,1},{4,6},{5,7},{6,4},{7,5},{8,10},{9,11},{10,... | collective-permute-start | bytes 393224 | tf_op jit(solution)/shard_map/ppermute | solution.py:385
  208.7 5.9 %collective-permute-done.39 = bf16[128,512]{1,0:T(8,128)(2,1)S(1)} collective-permute-done((bf16[128,512]{1,0:T(8,128)(2,1)}, bf16[128,512]{1,0:T(8,128)(2,1)S(1)}, u32[]{:S(2)}, u32[]{:S(2)}) %collective-permute-start.39) | collective-permute-done | bytes 131104 | tf_op jit(solution)/shard_map/ppermute | solution.py:385
  225.4 4.5 %collective-permute-done.43.refs_3_ = bf16[64,512]{1,0:T(8,128)(2,1)S(1)} collective-permute-done((bf16[64,512]{1,0:T(8,128)(2,1)}, bf16[64,512]{1,0:T(8,128)(2,1)S(1)}, u32[]{:S(2)}, u32[]{:S(2)}) %collective-permute-start.43) | collective-permute-done | bytes 65568 | tf_op jit(solution)/shard_map/ppermute | solution.py:385
  236.4 4.6 %collective-permute-done.61.refs_2_ = bf16[512,512]{1,0:T(8,128)(2,1)S(1)} collective-permute-done((bf16[512,512]{1,0:T(8,128)(2,1)S(1)}, bf16[512,512]{1,0:T(8,128)(2,1)S(1)}, u32[]{:S(2)}, u32[]{:S(2)}) %collective-permute-start.61) | collective-permute-done | bytes 524320 | tf_op jit(solution)/shard_map/ppermute | solution.py:385
  242.6 4.0 %ffn_give.1 = (bf16[320,512]{1,0:T(8,128)(2,1)}, bf16[320,512]{1,0:T(8,128)(2,1)}, bf16[320,512]{1,0:T(8,128)(2,1)}, bf16[320,512]{1,0:T(8,128)(2,1)}, bf16[256,...) custom-call(s32[2]{0:T(128)} %pad_add_fusion.place, ...), custom_call_target="tpu_custom_call" | custom-call | bytes 4456448 | tf_op jit(solution)/shard_map/ffn_give/pallas_call | solution.py:409
  252.1 3.3 %join_positions.2 = f32[4,256,512]{2,1,0:T(8,128)} custom-call(s32[2]{0:T(128)} %pad_add_fusion.place, bf16[256,512]{1,0:T(8,128)(2,1)} %get-tuple-element.281.refs_0_, bf16[256,512]{1,0:T(8,128)(2,1)} %copy-done.24, bf16[256,512]{1,0:T(8,128)(2,1)} %copy-done.25, bf16[256,512]{1,0:T(8,128)(2,1)} %copy-done.26), custom_call_target="tpu_custom_call" | custom-call | bytes 3145728 | tf_op jit(solution)/shard_map/join_positions/pallas_call | solution.py:409
  265.3 17.9 %newton_ffn.1.mine = bf16[512,512]{1,0:T(8,128)(2,1)} custom-call(s32[2]{0:T(128)} %pad_add_fusion.place, bf16[256,512]{1,0:T(8,128)(2,1)} %get-tuple-element.391.refs_0_.refs_4_, bf16[320,512]{1,0:T(8,128)(2,1)} %copy-done.16, bf16[256,512]{1,0:T(8,128)(2,1)} %get-tuple-element.392.refs_2_.refs_5_, bf16[320,512]{1,0:T(8,128)(2,1)} %copy-done.17, ...), custom_call_target="tpu_custom_call" | custom-call | flops 12079595520 | bytes 2883584 | tf_op jit(solution)/shard_map/newton_ffn/pallas_call | solution.py:409
  285.1 9.3 %newton_att.1 = (bf16[128,512]{1,0:T(8,128)(2,1)}, bf16[128,512]{1,0:T(8,128)(2,1)}, bf16[128,512]{1,0:T(8,128)(2,1)}, bf16[128,512]{1,0:T(8,128)(2,1)}) custom-call(s32[2]{0:T(128)} %pad_add_fusion.place, bf16[64,512]{1,0:T(8,128)(2,1)} %att_plane_sum.1.refs_0_, bf16[64,512]{1,0:T(8,128)(2,1)} %copy-done.44, bf16[64,512]{1,0:T(8,128)(2,1)} %copy-done.43, ...), custom_call_target="tpu_custom_call" | custom-call | flops 4026531840 | bytes 1048576 | tf_op jit(solution)/shard_map/newton_att/pallas_call | solution.py:409
  299.9 3.3 %join_positions.3 = f32[4,256,512]{2,1,0:T(8,128)} custom-call(s32[2]{0:T(128)} %pad_add_fusion.place, bf16[256,512]{1,0:T(8,128)(2,1)} %get-tuple-element.359.refs_0_, bf16[256,512]{1,0:T(8,128)(2,1)} %copy-done.27, bf16[256,512]{1,0:T(8,128)(2,1)} %copy-done.28, bf16[256,512]{1,0:T(8,128)(2,1)} %copy-done.29), custom_call_target="tpu_custom_call" | custom-call | bytes 3145728 | tf_op jit(solution)/shard_map/join_positions/pallas_call | solution.py:409
  303.2 6.4 %collective-permute-done.58.refs_6_ = bf16[128,512]{1,0:T(8,128)(2,1)S(1)} collective-permute-done((bf16[128,512]{1,0:T(8,128)(2,1)}, bf16[128,512]{1,0:T(8,128)(2,1)S(1)}, u32[]{:S(2)}, u32[]{:S(2)}) %collective-permute-start.58) | collective-permute-done | bytes 131104 | tf_op jit(solution)/shard_map/ppermute | solution.py:385
  310.9 3.8 %att_final.1 = (f32[512,128]{1,0:T(8,128)}, f32[512,128]{1,0:T(8,128)}, f32[512,128]{1,0:T(8,128)}, f32[128,512]{1,0:T(8,128)}, f32[512,128]{1,0:T(8,128)}, /*in...) custom-call(s32[2]{0:T(128)} %pad_add_fusion.place, bf16[128,512]{1,0:T(8,128)(2,1)} %get-tuple-element.363.refs_0_, ...), custom_call_target="tpu_custom_call" | custom-call | bytes 4194304 | tf_op jit(solution)/shard_map/att_final/pallas_call | solution.py:409
  314.6 4.2 %ffn_buffers.1 = (f32[512,512]{1,0:T(8,128)}, f32[512,512]{1,0:T(8,128)}) custom-call(s32[2]{0:T(128)} %pad_add_fusion.place, bf16[320,512]{1,0:T(8,128)(2,1)} %get-tuple-element.387.refs_0_, bf16[320,512]{1,0:T(8,128)(2,1)} %get-tuple-element.388.refs_1_, bf16[320,512]{1,0:T(8,128)(2,1)} %get-tuple-element.389.refs_2_, ...), custom_call_target="tpu_custom_call" | custom-call | bytes 5767168 | tf_op jit(solution)/shard_map/ffn_buffers/pallas_call | solution.py:409
  319.7 4.0 %ffn_final.1 = (f32[512,512]{1,0:T(8,128)}, f32[512,512]{1,0:T(8,128)}) custom-call(s32[2]{0:T(128)} %pad_add_fusion.place, bf16[512,512]{1,0:T(8,128)(2,1)} %newton_ffn.1.mine, bf16[512,512]{1,0:T(8,128)(2,1)} %copy-done.13, f32[512,512]{1,0:T(8,128)} %we.1, f32[512,512]{1,0:T(8,128)} %wc.1), custom_call_target="tpu_custom_call" | custom-call | bytes 5242880 | tf_op jit(solution)/shard_map/ffn_final/pallas_call | solution.py:409
  (336 shorter events, 121.2 us)
Async XLA Ops:
  37.0 31.4 %collective-permute-start.15 = (bf16[4,144,512]{2,1,0:T(8,128)(2,1)S(1)}, bf16[4,144,512]{2,1,0:T(8,128)(2,1)S(1)}, u32[]{:S(2)}, u32[]{:S(2)}) collective-permute-start(bf16[4,144,512]{2,1,0:T(8,128)(2,1)S(1)} %pad_maximum_fusion.2.refs_7_), channel_id=1, source_target_pairs={{0,24},{4,28},{8,16},{12,20},{16,8},{20,12},{24,0},{28,4},{1,25},{... | collective-permute-start | bytes 1769480 | tf_op jit(solution)/shard_map/ppermute | solution.py:385
  38.5 29.9 %collective-permute-start.14 = (bf16[4,144,512]{2,1,0:T(8,128)(2,1)S(1)}, bf16[4,144,512]{2,1,0:T(8,128)(2,1)S(1)}, u32[]{:S(2)}, u32[]{:S(2)}) collective-permute-start(bf16[4,144,512]{2,1,0:T(8,128)(2,1)S(1)} %pad_maximum_fusion.2.refs_7_), channel_id=1, source_target_pairs={{0,16},{4,20},{8,24},{12,28},{16,0},{20,4},{24,8},{28,12},{1,17},{... | collective-permute-start | bytes 1769480 | tf_op jit(solution)/shard_map/ppermute | solution.py:385
  39.0 29.5 %collective-permute-start.13 = (bf16[4,144,512]{2,1,0:T(8,128)(2,1)S(1)}, bf16[4,144,512]{2,1,0:T(8,128)(2,1)S(1)}, u32[]{:S(2)}, u32[]{:S(2)}) collective-permute-start(bf16[4,144,512]{2,1,0:T(8,128)(2,1)S(1)} %pad_maximum_fusion.2.refs_7_), channel_id=1, source_target_pairs={{0,8},{4,12},{8,0},{12,4},{16,24},{20,28},{24,16},{28,20},{1,9},{5... | collective-permute-start | bytes 1769480 | tf_op jit(solution)/shard_map/ppermute | solution.py:385
  42.8 25.6 %collective-permute-start.17 = (bf16[256,512]{1,0:T(8,128)(2,1)S(1)}, bf16[256,512]{1,0:T(8,128)(2,1)S(1)}, u32[]{:S(2)}, u32[]{:S(2)}) collective-permute-start(bf16[256,512]{1,0:T(8,128)(2,1)S(1)} %copy-done.71), channel_id=1, source_target_pairs={{0,2},{1,3},{2,0},{3,1},{4,6},{5,7},{6,4},{7,5},{8,10},{9,11},{10,... | collective-permute-start | bytes 786440 | tf_op jit(solution)/shard_map/ppermute | solution.py:385
  43.2 25.2 %collective-permute-start.18 = (bf16[256,512]{1,0:T(8,128)(2,1)S(1)}, bf16[256,512]{1,0:T(8,128)(2,1)S(1)}, u32[]{:S(2)}, u32[]{:S(2)}) collective-permute-start(bf16[256,512]{1,0:T(8,128)(2,1)S(1)} %copy-done.70), channel_id=1, source_target_pairs={{0,3},{1,2},{2,1},{3,0},{4,7},{5,6},{6,5},{7,4},{8,11},{9,10},{10,... | collective-permute-start | bytes 786440 | tf_op jit(solution)/shard_map/ppermute | solution.py:385
  110.3 22.5 %collective-permute-start.23 = (bf16[2048,512]{1,0:T(8,128)(2,1)}, bf16[2048,512]{1,0:T(8,128)(2,1)S(1)}, u32[]{:S(2)}, u32[]{:S(2)}) collective-permute-start(bf16[2048,512]{1,0:T(8,128)(2,1)} %bitcast.17), channel_id=1, source_target_pairs={{0,4},{4,0},{8,12},{12,8},{16,20},{20,16},{24,28},{28,24},{1,5},{5... | collective-permute-start | bytes 6291464 | tf_op jit(solution)/shard_map/ppermute | solution.py:385
  110.9 21.3 %collective-permute-start.24 = (bf16[16,512]{1,0:T(8,128)(2,1)S(1)}, bf16[16,512]{1,0:T(8,128)(2,1)S(1)}, u32[]{:S(2)}, u32[]{:S(2)}) collective-permute-start(bf16[16,512]{1,0:T(8,128)(2,1)S(1)} %pad_maximum_fusion.6), channel_id=1, source_target_pairs={{0,4},{4,0},{8,12},{12,8},{16,20},{20,16},{24,28},{28,24},{1,5},{5... | collective-permute-start | bytes 49160 | tf_op jit(solution)/shard_map/ppermute | solution.py:385
  111.4 31.9 %collective-permute-start.28 = (bf16[256,512]{1,0:T(8,128)(2,1)S(1)}, bf16[256,512]{1,0:T(8,128)(2,1)S(1)}, u32[]{:S(2)}, u32[]{:S(2)}) collective-permute-start(bf16[256,512]{1,0:T(8,128)(2,1)S(1)} %copy-done.69), channel_id=1, source_target_pairs={{0,1},{1,0},{2,3},{3,2},{4,5},{5,4},{6,7},{7,6},{8,9},{9,8},{10,11... | collective-permute-start | bytes 786440 | tf_op jit(solution)/shard_map/ppermute | solution.py:385
  138.6 26.2 %collective-permute-start.25 = (bf16[528,512]{1,0:T(8,128)(2,1)}, bf16[528,512]{1,0:T(8,128)(2,1)S(1)}, u32[]{:S(2)}, u32[]{:S(2)}) collective-permute-start(bf16[528,512]{1,0:T(8,128)(2,1)} %get-tuple-element.274), channel_id=1, source_target_pairs={{0,8},{4,12},{8,0},{12,4},{16,24},{20,28},{24,16},{28,20},{1,9},{5... | collective-permute-start | bytes 1622024 | tf_op jit(solution)/shard_map/ppermute | solution.py:385
  139.1 25.7 %collective-permute-start.26 = (bf16[528,512]{1,0:T(8,128)(2,1)}, bf16[528,512]{1,0:T(8,128)(2,1)S(1)}, u32[]{:S(2)}, u32[]{:S(2)}) collective-permute-start(bf16[528,512]{1,0:T(8,128)(2,1)} %get-tuple-element.275), channel_id=1, source_target_pairs={{0,16},{4,20},{8,24},{12,28},{16,0},{20,4},{24,8},{28,12},{1,17},{... | collective-permute-start | bytes 1622024 | tf_op jit(solution)/shard_map/ppermute | solution.py:385
  140.7 24.7 %collective-permute-start.27 = (bf16[528,512]{1,0:T(8,128)(2,1)}, bf16[528,512]{1,0:T(8,128)(2,1)S(1)}, u32[]{:S(2)}, u32[]{:S(2)}) collective-permute-start(bf16[528,512]{1,0:T(8,128)(2,1)} %get-tuple-element.276), channel_id=1, source_target_pairs={{0,24},{4,28},{8,16},{12,20},{16,8},{20,12},{24,0},{28,4},{1,25},{... | collective-permute-start | bytes 1622024 | tf_op jit(solution)/shard_map/ppermute | solution.py:385
  142.1 22.7 %collective-permute-start.29 = (bf16[256,512]{1,0:T(8,128)(2,1)S(1)}, bf16[256,512]{1,0:T(8,128)(2,1)S(1)}, u32[]{:S(2)}, u32[]{:S(2)}) collective-permute-start(bf16[256,512]{1,0:T(8,128)(2,1)S(1)} %copy-done.68), channel_id=1, source_target_pairs={{0,2},{1,3},{2,0},{3,1},{4,6},{5,7},{6,4},{7,5},{8,10},{9,11},{10,... | collective-permute-start | bytes 786440 | tf_op jit(solution)/shard_map/ppermute | solution.py:385
  143.3 21.5 %collective-permute-start.30 = (bf16[256,512]{1,0:T(8,128)(2,1)S(1)}, bf16[256,512]{1,0:T(8,128)(2,1)S(1)}, u32[]{:S(2)}, u32[]{:S(2)}) collective-permute-start(bf16[256,512]{1,0:T(8,128)(2,1)S(1)} %copy-done.67), channel_id=1, source_target_pairs={{0,3},{1,2},{2,1},{3,0},{4,7},{5,6},{6,5},{7,4},{8,11},{9,10},{10,... | collective-permute-start | bytes 786440 | tf_op jit(solution)/shard_map/ppermute | solution.py:385
  215.7 19.2 %collective-permute-start.62 = (bf16[512,512]{1,0:T(8,128)(2,1)S(1)}, bf16[512,512]{1,0:T(8,128)(2,1)S(1)}, u32[]{:S(2)}, u32[]{:S(2)}) collective-permute-start(bf16[512,512]{1,0:T(8,128)(2,1)S(1)} %constant_dynamic-update-slice_fusion.refs_0_), channel_id=1, source_target_pairs={{0,24},{4,28},{8,16},{12,20},{16,8},{20,12},{24,0},{28,4},{1,25},{... | collective-permute-start | bytes 1572872 | tf_op jit(solution)/shard_map/ppermute | solution.py:385
  216.2 24.7 %collective-permute-start.61 = (bf16[512,512]{1,0:T(8,128)(2,1)S(1)}, bf16[512,512]{1,0:T(8,128)(2,1)S(1)}, u32[]{:S(2)}, u32[]{:S(2)}) collective-permute-start(bf16[512,512]{1,0:T(8,128)(2,1)S(1)} %constant_dynamic-update-slice_fusion.refs_0_), channel_id=1, source_target_pairs={{0,16},{4,20},{8,24},{12,28},{16,0},{20,4},{24,8},{28,12},{1,17},{... | collective-permute-start | bytes 1572872 | tf_op jit(solution)/shard_map/ppermute | solution.py:385
  217.8 23.2 %collective-permute-start.60 = (bf16[512,512]{1,0:T(8,128)(2,1)S(1)}, bf16[512,512]{1,0:T(8,128)(2,1)S(1)}, u32[]{:S(2)}, u32[]{:S(2)}) collective-permute-start(bf16[512,512]{1,0:T(8,128)(2,1)S(1)} %constant_dynamic-update-slice_fusion.refs_0_), channel_id=1, source_target_pairs={{0,8},{4,12},{8,0},{12,4},{16,24},{20,28},{24,16},{28,20},{1,9},{5... | collective-permute-start | bytes 1572872 | tf_op jit(solution)/shard_map/ppermute | solution.py:385
  247.2 15.5 %collective-permute-start.65 = (bf16[320,512]{1,0:T(8,128)(2,1)}, bf16[320,512]{1,0:T(8,128)(2,1)S(1)}, u32[]{:S(2)}, u32[]{:S(2)}) collective-permute-start(bf16[320,512]{1,0:T(8,128)(2,1)} %get-tuple-element.389.refs_2_), channel_id=1, source_target_pairs={{0,4},{4,0},{8,12},{12,8},{16,20},{20,16},{24,28},{28,24},{1,5},{5... | collective-permute-start | bytes 983048 | tf_op jit(solution)/shard_map/ppermute | solution.py:385
  247.3 15.4 %collective-permute-start.66 = (bf16[320,512]{1,0:T(8,128)(2,1)}, bf16[320,512]{1,0:T(8,128)(2,1)S(1)}, u32[]{:S(2)}, u32[]{:S(2)}) collective-permute-start(bf16[320,512]{1,0:T(8,128)(2,1)} %get-tuple-element.390.refs_3_), channel_id=1, source_target_pairs={{0,4},{4,0},{8,12},{12,8},{16,20},{20,16},{24,28},{28,24},{1,5},{5... | collective-permute-start | bytes 983048 | tf_op jit(solution)/shard_map/ppermute | solution.py:385
  255.5 27.7 %collective-permute-start.51 = (bf16[256,512]{1,0:T(8,128)(2,1)S(1)}, bf16[256,512]{1,0:T(8,128)(2,1)S(1)}, u32[]{:S(2)}, u32[]{:S(2)}) collective-permute-start(bf16[256,512]{1,0:T(8,128)(2,1)S(1)} %copy-done.63), channel_id=1, source_target_pairs={{0,1},{1,0},{2,3},{3,2},{4,5},{5,4},{6,7},{7,6},{8,9},{9,8},{10,11... | collective-permute-start | bytes 786440 | tf_op jit(solution)/shard_map/ppermute | solution.py:385
  258.7 26.4 %collective-permute-start.52 = (bf16[256,512]{1,0:T(8,128)(2,1)S(1)}, bf16[256,512]{1,0:T(8,128)(2,1)S(1)}, u32[]{:S(2)}, u32[]{:S(2)}) collective-permute-start(bf16[256,512]{1,0:T(8,128)(2,1)S(1)} %copy-done.62), channel_id=1, source_target_pairs={{0,2},{1,3},{2,0},{3,1},{4,6},{5,7},{6,4},{7,5},{8,10},{9,11},{10,... | collective-permute-start | bytes 786440 | tf_op jit(solution)/shard_map/ppermute | solution.py:385
  260.8 33.5 %collective-permute-start.53 = (bf16[256,512]{1,0:T(8,128)(2,1)S(1)}, bf16[256,512]{1,0:T(8,128)(2,1)S(1)}, u32[]{:S(2)}, u32[]{:S(2)}) collective-permute-start(bf16[256,512]{1,0:T(8,128)(2,1)S(1)} %copy-done.61), channel_id=1, source_target_pairs={{0,3},{1,2},{2,1},{3,0},{4,7},{5,6},{6,5},{7,4},{8,11},{9,10},{10,... | collective-permute-start | bytes 786440 | tf_op jit(solution)/shard_map/ppermute | solution.py:385
  262.7 31.7 %collective-permute-start.54 = (bf16[128,512]{1,0:T(8,128)(2,1)}, bf16[128,512]{1,0:T(8,128)(2,1)S(1)}, u32[]{:S(2)}, u32[]{:S(2)}) collective-permute-start(bf16[128,512]{1,0:T(8,128)(2,1)} %get-tuple-element.356), channel_id=1, source_target_pairs={{0,1},{1,0},{2,3},{3,2},{4,5},{5,4},{6,7},{7,6},{8,9},{9,8},{10,11... | collective-permute-start | bytes 393224 | tf_op jit(solution)/shard_map/ppermute | solution.py:385
  262.7 31.7 %collective-permute-start.55 = (bf16[128,512]{1,0:T(8,128)(2,1)}, bf16[128,512]{1,0:T(8,128)(2,1)S(1)}, u32[]{:S(2)}, u32[]{:S(2)}) collective-permute-start(bf16[128,512]{1,0:T(8,128)(2,1)} %get-tuple-element.357), channel_id=1, source_target_pairs={{0,2},{1,3},{2,0},{3,1},{4,6},{5,7},{6,4},{7,5},{8,10},{9,11},{10,... | collective-permute-start | bytes 393224 | tf_op jit(solution)/shard_map/ppermute | solution.py:385
  285.1 33.8 %collective-permute-start.67 = (bf16[512,512]{1,0:T(8,128)(2,1)}, bf16[512,512]{1,0:T(8,128)(2,1)S(1)}, u32[]{:S(2)}, u32[]{:S(2)}) collective-permute-start(bf16[512,512]{1,0:T(8,128)(2,1)} %newton_ffn.1.mine), channel_id=1, source_target_pairs={{0,4},{4,0},{8,12},{12,8},{16,20},{20,16},{24,28},{28,24},{1,5},{5... | collective-permute-start | bytes 1572872 | tf_op jit(solution)/shard_map/ppermute | solution.py:385
  (125 other events, 1196.6 us)

commit v3 on v2

--- a/solution.py
+++ b/solution.py
@@ -1,4 +1,5 @@
 import functools
+import math
 
 import jax
 import jax.numpy as jnp
@@ -401,11 +402,15 @@
 
 
 whole = pl.BlockSpec(memory_space=pltpu.VMEM)
-
-
-def run(kernel, place, args, outs, name, grid=(1,), in_specs=None, out_specs=None, scratch=(), flops=0):
+hbm = pl.BlockSpec(memory_space=pl.ANY)
+
+
+def run(kernel, place, args, outs, name, grid=(1,), in_specs=None, out_specs=None, scratch=(), flops=0, spare=4):
     moved = sum(a.size * a.dtype.itemsize for a in args)
     moved += sum(o.size * jnp.dtype(o.dtype).itemsize for o in outs)
+    held = moved + sum(
+        math.prod(b.shape) * b.dtype.itemsize for b in scratch if b.memory_space == pltpu.VMEM
+    )
     return pl.pallas_call(
         kernel,
         grid_spec=pltpu.PrefetchScalarGridSpec(
@@ -416,8 +421,10 @@
             scratch_shapes=list(scratch),
         ),
         out_shape=list(outs),
-        compiler_params=pltpu.CompilerParams(vmem_limit_bytes=56 << 20),
-        cost_estimate=pl.CostEstimate(flops=flops, bytes_accessed=moved, transcendentals=0),
+        compiler_params=pltpu.CompilerParams(vmem_limit_bytes=min(56 << 20, held + (spare << 20))),
+        cost_estimate=pl.CostEstimate(
+            flops=flops, bytes_accessed=moved if flops else 0, transcendentals=0
+        ),
         name=name,
     )(place, *args)
 
@@ -457,6 +464,7 @@
         outs,
         name,
         in_specs=[whole, whole, whole, row(span), row(hid), row(hid)],
+        spare=56,
         scratch=[pltpu.VMEM((q.shape[1], D), f32)],
     )
 
@@ -509,102 +517,162 @@
     return [half for pair in zip(own, other) for half in pair]
 
 
+def in_lanes(low, high, x, rest):
+    lane = lax.broadcasted_iota(jnp.int32, x.shape, 1)
+    return jnp.where((lane >= low) & (lane < high), x, rest)
+
+
+def spare_lanes(half, values, like_x):
+    lane = lax.broadcasted_iota(jnp.int32, like_x.shape, 1)
+    first = HEAD_DIM * (1 - half)
+    out = jnp.zeros_like(like_x)
+    for at, value in enumerate(values):
+        out = jnp.where(lane == first + at, value, out)
+    return out
+
+
+def head_lanes(half, x, values=()):
+    return in_lanes(HEAD_DIM * half, HEAD_DIM * (half + 1), x, spare_lanes(half, values, x))
+
+
+def two_parts(x):
+    high = x.astype(bf16)
+    return high, (x - high.astype(f32)).astype(bf16)
+
+
 def forward_kernel(place, last_ref, in_ref, *refs):
-    halves, (qkv_ref, o_ref) = refs[:-2], refs[-2:]
-    length = in_ref.shape[0]
+    halves, (x_ref, o_ref, bias_ref, q_ref, v_ref) = refs[:-5], refs[-5:]
+    length = in_ref.shape[1]
     span = halves[0].shape[1] // 3
-    for which in range(3):
-        weight = pair_weights(halves, which, span)
-        qkv_ref[which] = mm(in_ref[...], weight, nt).astype(bf16)
-    lane = lax.broadcasted_iota(jnp.int32, (q_rows, 128), 1)
-    for first in range(0, length, q_rows):
-        low, high = window(first), first + q_rows
-        row = first + lax.broadcasted_iota(jnp.int32, (q_rows, high - low), 0)
-        col = low + lax.broadcasted_iota(jnp.int32, (q_rows, high - low), 1)
-        allowed = (col <= row) & (row <= last_ref[:, low:high])
-        query = qkv_ref[0, first:high, :] * jnp.asarray(HEAD_DIM**-0.5, bf16)
-        halves = []
+    blocks = [(first, window(first), first + q_rows) for first in range(0, length, q_rows)]
+
+    @pl.when(pl.program_id(0) == 0)
+    def _():
+        for first, low, high in blocks:
+            row = first + lax.broadcasted_iota(jnp.int32, (q_rows, high - low), 0)
+            col = low + lax.broadcasted_iota(jnp.int32, (q_rows, high - low), 1)
+            allowed = (col <= row) & (row <= last_ref[:, low:high])
+            bias_ref[first:high, : high - low] = jnp.where(allowed, 0.0, mask_fill)
+
+    weight = jnp.concatenate([pair_weights(halves, which, span) for which in range(3)], 0)
+    rows = mm(in_ref[0], weight, nt).astype(bf16)
+    query = rows[:, :128] * jnp.asarray(HEAD_DIM**-0.5, bf16)
+    x_ref[0, 2] = rows[:, 128:256]
+    x_ref[0, 3] = rows[:, 256:]
+    one = jnp.asarray(1, bf16)
+    for half in range(2):
+        q_ref[half] = head_lanes(half, query)
+        v_ref[half] = head_lanes(half, rows[:, 256:], (one,))
+    for first, low, high in blocks:
+        found = []
         for half in range(2):
-            mine = (lane >= HEAD_DIM * half) & (lane < HEAD_DIM * (half + 1))
-            scores = mm(jnp.where(mine, query, jnp.zeros_like(query)), qkv_ref[1, low:high, :], nt)
-            scores = jnp.where(allowed, scores, mask_fill)
-            weight = jnp.exp(scores - jnp.max(scores, axis=1, keepdims=True))
-            total = jnp.sum(weight, axis=1, keepdims=True)
-            halves.append(mm((weight * (1.0 / total)).astype(bf16), qkv_ref[2, low:high, :], nn))
-        o_ref[first:high, :] = jnp.where(lane < HEAD_DIM, halves[0], halves[1]).astype(bf16)
+            spare = HEAD_DIM * (1 - half)
+            scores = mm(q_ref[half, first:high, :], x_ref[0, 2, low:high, :], nt)
+            scores = scores + bias_ref[first:high, : high - low]
+            peak = jnp.max(scores, axis=1, keepdims=True)
+            weight = jnp.exp(scores - peak).astype(bf16)
+            out = mm(weight, v_ref[half, low:high, :], nn)
+            total = out[:, spare : spare + 1]
+            found.append(out * (1.0 / total))
+            parts = two_parts(-(peak + jnp.log(total)))
+            x_ref[0, half, first:high, :] = head_lanes(half, q_ref[half, first:high, :], parts)
+        o_ref[first:high, :] = in_lanes(0, HEAD_DIM, found[0], found[1]).astype(bf16)
 
 
 def attention(place, last, inputs, halves):
-    length = inputs.shape[0]
+    length = inputs.shape[1]
     planes, rows, _ = halves[0].shape
     half = pl.BlockSpec((1, rows, D), lambda h, place: (h, 0, 0))
     return run(
         forward_kernel,
         place,
         [last, inputs, *halves],
-        [like((3, length, D), bf16), like((length, D), bf16)],
+        [like((planes, 4, length, 128), bf16), like((length, D), bf16)],
         "attention_forward",
+        spare=56,
         grid=(planes,),
-        in_specs=[whole, whole] + [half] * len(halves),
+        in_specs=[whole, pl.BlockSpec((1, length, D), lambda h, place: (place[0], 0, 0))]
+        + [half] * len(halves),
         out_specs=[
-            pl.BlockSpec((3, length, 128), lambda h, place: (0, 0, h)),
+            pl.BlockSpec((1, 4, length, 128), lambda h, place: (h, 0, 0, 0)),
             pl.BlockSpec((length, 128), lambda h, place: (0, h)),
         ],
+        scratch=[
+            pltpu.VMEM((length, 768), f32),
+            pltpu.VMEM((2, length, 128), bf16),
+            pltpu.VMEM((2, length, 128), bf16),
+        ],
         flops=8 * length * D * D + 2 * length * 768 * 512 * planes,
     )
 
 
-def backward_kernel(is_last, spots, place, start_ref, in_ref, qkv_ref, g_ref, gout_ref, gmid_ref, *rest):
+def backward_kernel(
+    is_last, spots, place, start_ref, in_hbm, x_ref, g_ref, o_ref, gout_ref, gmid_hbm, *rest
+):
     halves, rest = rest[:spots], rest[spots:]
-    ins, (keep_ref, give_ref, dk_ref, dv_ref, dq_ref, acc_ref) = rest[:-6], rest[-6:]
+    ins, rest = rest[:-12], rest[-12:]
+    keep_ref, give_ref, dk_ref, dv_ref, dq_ref, acc_ref, bias_ref, k_ref, v_ref, gs_ref = rest[:10]
+    in_ref, sems = rest[10:]
     length = in_ref.shape[0]
+    load_acc = pltpu.make_async_copy(gmid_hbm, acc_ref, sems.at[0])
+    load_in = pltpu.make_async_copy(in_hbm.at[place[0]], in_ref, sems.at[1])
     span = halves[0].shape[1] // 3
     chips = spots // 2
     step = pl.program_id(0)
-    lane = lax.broadcasted_iota(jnp.int32, (q_rows, 128), 1)
+    blocks = [(first, window(first), first + q_rows) for first in range(0, length, q_rows)]
+
+    @pl.when(step == 0)
+    def _():
+        load_acc.start()
+        load_in.start()
+        for first, low, high in blocks:
+            col = low + lax.broadcasted_iota(jnp.int32, (high - low, q_rows), 0)
+            row = first + lax.broadcasted_iota(jnp.int32, (high - low, q_rows), 1)
+            allowed = (col <= row) & (col >= start_ref[:, first:high])
+            bias_ref[: high - low, first:high] = jnp.where(allowed, 0.0, mask_fill)
+
     dk_ref[...] = jnp.zeros_like(dk_ref)
     dv_ref[...] = jnp.zeros_like(dv_ref)
-    key_t = qkv_ref[1].astype(f32).T.astype(bf16)
-    for first in range(0, length, q_rows):
-        low, high = window(first), first + q_rows
-        col = low + lax.broadcasted_iota(jnp.int32, (high - low, q_rows), 0)
-        row = first + lax.broadcasted_iota(jnp.int32, (high - low, q_rows), 1)
-        allowed = (col <= row) & (col >= start_ref[:, first:high])
-        query = qkv_ref[0, first:high, :] * jnp.asarray(HEAD_DIM**-0.5, bf16)
-        grad = g_ref[first:high, :]
-        key = qkv_ref[1, low:high, :]
-        value = qkv_ref[2, low:high, :]
-        dk = dk_ref[low:high, :]
-        dv = dv_ref[low:high, :]
-        dq = []
-        for half in range(2):
-            mine = (lane >= HEAD_DIM * half) & (lane < HEAD_DIM * (half + 1))
-            q_half = jnp.where(mine, query, jnp.zeros_like(query))
-            g_half = jnp.where(mine, grad, jnp.zeros_like(grad))
-            scores = jnp.where(allowed, mm(key, q_half, nt), mask_fill)
-            weight = jnp.exp(scores - jnp.max(scores, axis=0, keepdims=True))
-            probs = weight * (1.0 / jnp.sum(weight, axis=0, keepdims=True))
-            g_probs = mm(value, g_half, nt)
-            delta = jnp.sum(probs * g_probs, axis=0, keepdims=True)
-            g_scores = (probs * (g_probs - delta)).astype(bf16)
-            dv = dv + mm(probs.astype(bf16), g_half, nn)
-            dk = dk + mm(g_scores, q_half, nn)
-            dq.append(mm(key_t[HEAD_DIM * half : HEAD_DIM * (half + 1), low:high], g_scores, nn))
-        dk_ref[low:high, :] = dk
-        dv_ref[low:high, :] = dv
-        dq = jnp.concatenate(dq, 0) * HEAD_DIM**-0.5
-        dq_ref[first:high, :] = dq.T.astype(bf16)
+    one = jnp.asarray(1, bf16)
+    product = g_ref[...].astype(f32) * o_ref[...].astype(f32)
+    for half in range(2):
+        k_ref[half] = head_lanes(half, x_ref[0, 2], (one, one))
+        v_ref[half] = head_lanes(half, x_ref[0, 3], (one, one))
+        delta = jnp.sum(head_lanes(half, product), axis=1, keepdims=True)
+        gs_ref[half] = head_lanes(half, g_ref[...], two_parts(-delta))
+    for first, low, high in blocks:
+        q_both = jnp.concatenate([head_lanes(half, x_ref[0, half, first:high, :]) for half in range(2)], 0)
+        g_both = jnp.concatenate([head_lanes(half, g_ref[first:high, :]) for half in range(2)], 0)
+        dq = jnp.zeros((q_rows, 128), f32)
+        for at in range(low, high, q_rows):
+            keys = slice(at, at + q_rows)
+            bias = bias_ref[at - low : at - low + q_rows, first:high]
+            probs, g_scores = [], []
+            for half in range(2):
+                scores = mm(k_ref[half, keys, :], x_ref[0, half, first:high, :], nt) + bias
+                weight = jnp.exp(scores)
+                g_probs = mm(v_ref[half, keys, :], gs_ref[half, first:high, :], nt)
+                probs.append(weight.astype(bf16))
+                g_scores.append((weight * g_probs).astype(bf16))
+            k_both = jnp.concatenate([head_lanes(half, x_ref[0, 2, keys, :]) for half in range(2)], 0)
+            dq = dq + mm(jnp.concatenate(g_scores, 0), k_both, tn)
+            dv_ref[keys, :] += mm(jnp.concatenate(probs, 1), g_both, nn)
+            dk_ref[keys, :] += mm(jnp.concatenate(g_scores, 1), q_both, nn)
+        dq_ref[first:high, :] = (dq * HEAD_DIM**-0.5).astype(bf16)
     grads = (dq_ref[...], dk_ref[...].astype(bf16), dv_ref[...].astype(bf16))
+    grads = jnp.concatenate(grads, 1)
+    weight = jnp.concatenate([pair_weights(halves, which, span) for which in range(3)], 0)
 
     @pl.when(step == 0)
     def _():
-        acc_ref[...] = gmid_ref[...]
-
-    for which, grad in enumerate(grads):
-        acc_ref[...] += mm(grad, pair_weights(halves, which, span), nn)
+        load_acc.wait()
+        load_in.wait()
+
+    acc_ref[...] += mm(grads, weight, nn)
+    all_rows = mm(grads, in_ref[...], tn).astype(bf16)
     for which in range(4):
         if which < 3:
-            rows = mm(grads[which], in_ref[...], tn).astype(bf16)
+            rows = all_rows[which * 128 : (which + 1) * 128, :]
         else:
             rows = gout_ref[...]
         for m in range(chips):
@@ -615,7 +683,9 @@
     @pl.when(step == pl.num_programs(0) - 1)
     def _():
         if not is_last:
-            ins[0][...] = acc_ref[...]
+            save = pltpu.make_async_copy(acc_ref, ins[0], sems.at[0])
+            save.start()
+            save.wait()
             return
         rows = ins[0].shape[0]
         for u, ref in enumerate(ins):
@@ -624,9 +694,9 @@
 
 
 def attention_back(
-    place, start, inputs, halves, qkv, heads_grad, grad_output, so_far, first, count, is_last
+    place, start, inputs, halves, qkv, heads_grad, heads, grad_output, so_far, first, count, is_last
 ):
-    length = inputs.shape[0]
+    length = inputs.shape[1]
     planes, rows, _ = halves[0].shape
     spots = len(halves)
     chips = spots // 2
@@ -637,65 +707,95 @@
     out = run(
         functools.partial(backward_kernel, is_last, spots),
         place,
-        [start, inputs, qkv, heads_grad, grad_output, so_far, *halves],
+        [start, inputs, qkv, heads_grad, heads, grad_output, so_far, *halves],
         outs + [like((chips, count, 4 * span, D), bf16)] * 2,
         "attention_backward",
+        spare=56,
         grid=(count,),
         in_specs=[
             whole,
-            whole,
-            pl.BlockSpec((3, length, 128), lambda h, place: (0, 0, first + h)),
+            hbm,
+            pl.BlockSpec((1, 4, length, 128), lambda h, place: (first + h, 0, 0, 0)),
+            pl.BlockSpec((length, 128), lambda h, place: (0, first + h)),
             pl.BlockSpec((length, 128), lambda h, place: (0, first + h)),
             pl.BlockSpec((128, D), lambda h, place: (first + h, 0)),
-            whole,
+            hbm,
         ]
         + [half] * spots,
-        out_specs=[whole] * len(outs) + [out_half] * 2,
+        out_specs=([whole] * planes if is_last else [hbm]) + [out_half] * 2,
         scratch=[
             pltpu.VMEM((length, 128), f32),
             pltpu.VMEM((length, 128), f32),
             pltpu.VMEM((length, 128), bf16),
             pltpu.VMEM((length, D), f32),
+            pltpu.VMEM((768, length), f32),
+            pltpu.VMEM((2, length, 128), bf16),
+            pltpu.VMEM((2, length, 128), bf16),
+            pltpu.VMEM((2, length, 128), bf16),
+            pltpu.VMEM((length, D), bf16),
+            pltpu.SemaphoreType.DMA((2,)),
         ],
         flops=(12 * length * D * D + 5 * length * 768 * 512 * planes) * count // planes,
     )
     return out[:-2], out[-2], out[-1]
 
 
-def ffn_kernel(planes, spots, place, *refs):
-    alphas, in_ref, heads_ref = refs[:3]
+def ffn_kernel(planes, spots, per, place, *refs):
+    alphas, in_hbm, heads_hbm = refs[:3]
     ups = refs[3 : 3 + planes]
     halves = refs[3 + planes : 3 + planes + spots]
     bias_ref, bout_ref = refs[3 + planes + spots : 5 + planes + spots]
     outs = refs[5 + planes + spots :]
     lays = outs[:planes]
-    g_ref, gout_ref, gheads_ref, gmid_ref, gbin_ref, gbout_ref, galpha_ref = outs[
-        planes : planes + 7
+    keep_ref, give_ref, gout_ref, gheads_hbm, gmid_hbm, gbin_ref, gbout_ref, galpha_ref = outs[
+        planes : planes + 8
     ]
-    attended, middle, mid_low, g_low, up, branch, o_low, lay, weights = outs[planes + 7 :]
+    (
+        attended, middle, mid_low, g_low, up, branch, o_low, lay, weights, in_ref, heads_ref,
+        o_parts, gmid_ref, gheads_ref, sems, w_sems, out_sems,
+    ) = outs[planes + 8 :]
     chips = spots // 2
     length = in_ref.shape[0]
     block = length // planes
-    hid = g_ref.shape[3] // planes
+    hid = keep_ref.shape[2] // planes
     span = halves[0].shape[1] - 2 * hid
-    core, chip = pl.program_id(0), pl.program_id(1)
+    step = pl.program_id(0)
+    steps = pl.num_programs(0)
     alpha_att, alpha_ffn = alphas[0], alphas[1]
-    tiles = [slice(at, at + 256) for at in range(0, length, 256)]
-
-    @pl.when((core == 0) & (chip == 0))
+    size = 512
+    tiles = [slice(at, at + size) for at in range(0, length, size)]
+
+    def order(at):
+        return 2 * (at % chips) + at // chips
+
+    def weight_copy(at):
+        return pltpu.make_async_copy(
+            halves[order(at)].at[:, span:, :], weights.at[at], w_sems.at[at]
+        )
+
+    @pl.when(step == 0)
     def _():
-        for k in range(planes):
-            for at, half in enumerate(halves):
-                m, c = at // 2, at % 2
-                row = (k * spots + at) * span
-                o_low[row : row + span, :] = half[k, :span, :]
-                row = span
-                for which in range(2):
-                    weights[c, m, which, k * hid : (k + 1) * hid, :] = half[k, row : row + hid, :]
-                    row += hid
+        first = [
+            pltpu.make_async_copy(half.at[:, :span, :], o_parts.at[at], sems.at[at])
+            for at, half in enumerate(halves)
+        ]
+        first.append(pltpu.make_async_copy(heads_hbm, heads_ref, sems.at[spots]))
+        first.append(pltpu.make_async_copy(in_hbm.at[place[0]], in_ref, sems.at[spots + 1]))
         for u in range(planes):
             at = pl.multiple_of((place[0] ^ u) * block, block)
-            up[pl.ds(at, block), :] = ups[u][...]
+            first.append(
+                pltpu.make_async_copy(ups[u], up.at[pl.ds(at, block), :], sems.at[spots + 2 + u])
+            )
+        for copy in first:
+            copy.start()
+        for at in range(spots):
+            weight_copy(at).start()
+        for copy in first:
+            copy.wait()
+        for k in range(planes):
+            for at in range(spots):
+                row = (k * spots + at) * span
+                o_low[row : row + span, :] = o_parts[at, k]
         total = jnp.zeros((1, D), f32)
         for t in tiles:
             found = mm(heads_ref[t, :], o_low[...], nn)
@@ -707,16 +807,23 @@
             grad = (alpha_ffn * upstream).astype(bf16)
             g_low[t, :] = grad
             total = total + jnp.sum(grad.astype(f32), axis=0, keepdims=True)
-            branch[t, :] = jnp.zeros((256, D), f32)
+            branch[t, :] = jnp.zeros((size, D), f32)
             gmid_ref[t, :] = upstream
         gbout_ref[...] = total
 
-    expand = weights[core, chip, 0]
-    contract = weights[core, chip, 1]
-    bias = bias_ref[0, 0]
-    gc = jnp.zeros((planes * hid, D), f32)
-    ge = jnp.zeros((planes * hid, D), f32)
-    gb = jnp.zeros((1, planes * hid), f32)
+    for at in range(spots):
+
+        @pl.when(step == at // per)
+        def _():
+            weight_copy(at).wait()
+
+    rows = [weights[step * per + g] for g in range(per)]
+    expand = jnp.concatenate([row[:, :hid, :].reshape(planes * hid, D) for row in rows], 0)
+    contract = jnp.concatenate([row[:, hid:, :].reshape(planes * hid, D) for row in rows], 0)
+    bias = bias_ref[0]
+    gc = jnp.zeros((per * planes * hid, D), f32)
+    ge = jnp.zeros((per * planes * hid, D), f32)
+    gb = jnp.zeros((1, per * planes * hid), f32)
     for t in tiles:
         mid = mid_low[t, :]
         grad = g_low[t, :]
@@ -734,60 +841,99 @@
         gc = gc + mm(hidden, grad, tn)
         ge = ge + mm(g_pre, mid, tn)
         gb = gb + jnp.sum(g_pre.astype(f32), axis=0, keepdims=True)
-    g_ref[0, 0, 0] = gc.astype(bf16)
-    g_ref[0, 0, 1] = ge.astype(bf16)
-    gbin_ref[0, 0] = gb
-
-    @pl.when((core == 1) & (chip == chips - 1))
+    gc = gc.astype(bf16)
+    ge = ge.astype(bf16)
+    group = planes * hid
+
+    def store(ref):
+        for g in range(per):
+            ref[g, 0] = gc[g * group : (g + 1) * group, :]
+            ref[g, 1] = ge[g * group : (g + 1) * group, :]
+
+    pl.when(step < steps // 2)(lambda: store(keep_ref))
+    pl.when(step >= steps // 2)(lambda: store(give_ref))
+    gbin_ref[0] = gb
+
+    @pl.when(step == steps - 1)
     def _():
         sum_ffn = jnp.zeros((1, D), f32)
         sum_att = jnp.zeros((1, D), f32)
         gout = jnp.zeros((D, D), f32)
-        for t in tiles:
+        copies = []
+        for at, t in enumerate(tiles):
+            gm = gmid_ref[t, :]
+            copies.append(
+                pltpu.make_async_copy(gmid_ref.at[t, :], gmid_hbm.at[t, :], out_sems.at[0, at])
+            )
+            copies[-1].start()
+            g_att = (alpha_att * gm).astype(bf16)
+            gheads_ref[t, :] = mm(g_att, o_low[...], nt).astype(bf16)
+            copies.append(
+                pltpu.make_async_copy(gheads_ref.at[t, :], gheads_hbm.at[t, :], out_sems.at[1, at])
+            )
+            copies[-1].start()
+            gout = gout + mm(heads_ref[t, :], g_att, tn)
+            sum_att = sum_att + jnp.sum(gm * attended[t, :], axis=0, keepdims=True)
             final = branch[t, :] + bout_ref[...]
             lay[t, :] = middle[t, :] + alpha_ffn * final
             sum_ffn = sum_ffn + jnp.sum(up[t, :].astype(f32) * final, axis=0, keepdims=True)
-            gm = gmid_ref[t, :]
-            sum_att = sum_att + jnp.sum(gm * attended[t, :], axis=0, keepdims=True)
-            g_att = (alpha_att * gm).astype(bf16)
-            gout = gout + mm(heads_ref[t, :], g_att, tn)
-            gheads_ref[t, :] = mm(g_att, o_low[...], nt).astype(bf16)
         gout_ref[...] = gout.astype(bf16)
         galpha_ref[0:1, :] = sum_att
         galpha_ref[1:2, :] = sum_ffn
         for u, ref in enumerate(lays):
             at = pl.multiple_of((place[0] ^ u) * block, block)
             ref[...] = lay[pl.ds(at, block), :].astype(bf16)
+        for copy in copies:
+            copy.wait()
 
 
 def feed_forward(place, alphas, inputs, heads, ups, halves, bias, bout):
-    length = inputs.shape[0]
+    length = inputs.shape[1]
     planes = len(ups)
     spots = len(halves)
     chips = spots // 2
-    hid = bias.shape[-1]
-    step = lambda *tail: pl.BlockSpec((1, 1) + tail, lambda c, m, place: (c, m) + (0,) * len(tail))
+    span, hid = heads.shape[1] // (planes * spots), bias.shape[-1] // planes
+    per = 2 if chips % 2 == 0 else 1
+    steps = spots // per
+    bias = bias.reshape(steps, 1, per * planes * hid)
+    tiles = length // 512
+    group = planes * hid
     out = run(
-        functools.partial(ffn_kernel, planes, spots),
+        functools.partial(ffn_kernel, planes, spots, per),
         place,
         [alphas, inputs, heads, *ups, *halves, bias, bout],
         [like((length // planes, D), bf16)] * planes
         + [
-            like((2, chips, 2, hid, D), bf16),
+            like((chips, 2, group, D), bf16),
+            like((chips, 2, group, D), bf16),
             like((D, D), bf16),
             like((length, D), bf16),
             like((length, D), f32),
-            like((2, chips, 1, hid), f32),
+            like((steps, 1, per * group), f32),
             like((1, D), f32),
             like((2, D), f32),
         ],
         "feed_forward",
-        grid=(2, chips),
+        spare=56,
+        grid=(steps,),
         in_specs=[pl.BlockSpec(memory_space=pltpu.SMEM)]
-        + [whole] * (2 + planes + spots)
-        + [step(1, hid), whole],
+        + [hbm] * (2 + planes + spots)
+        + [pl.BlockSpec((1, 1, per * group), lambda t, place: (t, 0, 0)), whole],
         out_specs=[whole] * planes
-        + [step(2, hid, D), whole, whole, whole, step(1, hid), whole, whole],
+        + [
+            pl.BlockSpec(
+                (per, 2, group, D), lambda t, place: (jnp.minimum(t, steps // 2 - 1), 0, 0, 0)
+            ),
+            pl.BlockSpec(
+                (per, 2, group, D), lambda t, place: (jnp.maximum(t - steps // 2, 0), 0, 0, 0)
+            ),
+            whole,
+            hbm,
+            hbm,
+            pl.BlockSpec((1, 1, per * group), lambda t, place: (t, 0, 0)),
+            whole,
+            whole,
+        ],
         scratch=[
             pltpu.VMEM((length, D), f32),
             pltpu.VMEM((length, D), f32),
@@ -797,33 +943,27 @@
             pltpu.VMEM((length, D), f32),
             pltpu.VMEM((D, D), bf16),
             pltpu.VMEM((length, D), f32),
-            pltpu.VMEM((2, chips, 2, hid, D), bf16),
+            pltpu.VMEM((spots, planes, 2 * hid, D), bf16),
+            pltpu.VMEM((length, D), bf16),
+            pltpu.VMEM((length, D), bf16),
+            pltpu.VMEM((spots, planes, span, D), bf16),
+            pltpu.VMEM((length, D), f32),
+            pltpu.VMEM((length, D), bf16),
+            pltpu.SemaphoreType.DMA((spots + 2 + planes,)),
+            pltpu.SemaphoreType.DMA((spots,)),
+            pltpu.SemaphoreType.DMA((2, tiles)),
         ],
-        flops=12 * length * D * 2 * chips * hid,
+        flops=12 * length * D * 2 * chips * group,
     )
     return out[:planes], out[planes:]
 
 
-def sum_kernel(count, place, *refs):
-    ins, outs = refs[:count], refs[count:]
-    rows = outs[0].shape[0]
-    for at, out in enumerate(outs):
-        span = slice(at * rows, (at + 1) * rows)
-        total = ins[0][span, :].astype(f32)
-        for ref in ins[1:]:
-            total = total + ref[span, :].astype(f32)
-        out[...] = total.astype(out.dtype)
-
-
-def sum_parts(place, ins, parts, name):
-    rows = ins[0].shape[0] // parts
-    return run(
-        functools.partial(sum_kernel, len(ins)),
-        place,
-        ins,
-        [like((rows, ins[0].shape[1]), bf16)] * parts,
-        name,
-    )
+def att_core_kernel(place, keep, got, *outs):
+    rows = keep.shape[2]
+    for m, out in enumerate(outs):
+        for k in range(keep.shape[1]):
+            total = keep[m, k].astype(f32) + got[m, k].astype(f32)
+            out[k * rows : (k + 1) * rows, :] = total.astype(bf16)
 
 
 def small_write(out, total):
@@ -864,64 +1004,70 @@
         small_write(out, small)
 
 
-def ffn_plane_kernel(place, old, *refs):
-    ins, (out, small_out) = refs[:-2], refs[-2:]
-    rows = out.shape[0]
-    total = old[...].reshape(rows, D)
-    small = small_read(ins[0])
-    for ref in ins:
+def plane_messages_kernel(chips, planes, place, *refs):
+    ffn, refs = refs[:planes], refs[planes:]
+    att, (ffn_old, att_old), refs = refs[:chips], refs[chips : chips + 2], refs[chips + 2 :]
+    outs, small_out, scratch = refs[:planes], refs[planes], refs[planes + 1]
+    rows = 2 * ffn_old.shape[1]
+    span = att_old.shape[1]
+    small = small_read(ffn[0])
+    total = ffn_old[...].reshape(rows, D) + ffn[0][:rows, :].astype(f32)
+    for ref in ffn[1:]:
+        small = small + small_read(ref)
         total = total + ref[:rows, :].astype(f32)
-    for ref in ins[1:]:
-        small = small + small_read(ref)
-    out[...] = total.astype(bf16)
     small_out[...] = small
-
-
-def att_to_owner_kernel(chips, planes, place, *refs):
-    ins, old, outs, scratch = refs[:chips], refs[chips], refs[chips + 1 : -1], refs[-1]
-    span = old.shape[1]
+    total = total.astype(bf16)
     for k in range(planes):
         for which in range(4):
             at = (k * 4 + which) * span
-            total = ins[0][at : at + span, :].astype(f32)
-            for ref in ins[1:]:
-                total = total + ref[at : at + span, :].astype(f32)
+            one = att[0][at : at + span, :].astype(f32)
+            for ref in att[1:]:
+                one = one + ref[at : at + span, :].astype(f32)
             if k == 0:
-                total = total + old[which]
-            scratch[which, k * span : (k + 1) * span, :] = total.astype(bf16)
+                one = one + att_old[which]
+            scratch[which, k * span : (k + 1) * span, :] = one.astype(bf16)
     for u, out in enumerate(outs):
-        out[...] = scratch[place[0] ^ u]
-
-
-def att_sum_kernel(planes, place, *refs):
+        out[:rows, :] = total
+        out[rows:, :] = scratch[place[0] ^ u]
+
+
+def plane_split_kernel(rows, place, *refs):
     ins, out = refs[:-1], refs[-1]
-    span = out.shape[0] // planes
+    planes = len(ins)
+    span = (ins[0].shape[0] - rows) // planes
+    for u, ref in enumerate(ins):
+        out[u * rows : (u + 1) * rows, :] = ref[:rows, :]
     for k in range(planes):
         total = jnp.zeros((span, D), f32)
         for u, ref in enumerate(ins):
-            at = (k ^ u) * span
+            at = rows + (k ^ u) * span
             total = total + ref[at : at + span, :].astype(f32)
-        out[k * span : (k + 1) * span, :] = total.astype(bf16)
-
-
-def spread_kernel(spots, place, *refs):
-    halves, outs = refs[:spots], refs[spots:]
-    span = outs[0].shape[0] // spots
-    for at, half in enumerate(halves):
-        to = pl.multiple_of((place[1] ^ at) * span, span)
-        for k, out in enumerate(outs):
-            out[pl.ds(to, span), :] = half[k * span : (k + 1) * span, :]
+        at = planes * rows + k * span
+        out[at : at + span, :] = total.astype(bf16)
 
 
 def newton_kernel(planes, spots, first_only, place, *refs):
-    halves, outs, x_ref, low_ref = refs[:spots], refs[spots:-2], refs[-2], refs[-1]
+    x_ref, low_ref = refs[-2:]
     dim, cols = x_ref.shape
     span = cols // (planes * spots)
     group = spots * span
+    if first_only:
+        chips = spots // 2
+        got, outs = refs[chips], refs[chips + 1 : -2]
+        tall = (planes + 1) * span
+        halves = []
+        for m in range(chips):
+            halves += [refs[m], got.at[m * tall : m * tall + planes * span, :]]
+    else:
+        outs = refs[2:-2]
+        halves = []
+        for at in range(spots):
+            from_at = refs[0].shape[0] - (spots // 2 - at // 2) * planes * span
+            halves.append(refs[at % 2].at[from_at : from_at + planes * span, :])
     chunk = 512
     total = jnp.zeros((1, D), f32)
     for half in halves:
-        part = half[: planes * span, :].astype(f32)
+        part = half[...].astype(f32)
         total = total + jnp.sum(part * part, axis=0, keepdims=True)
     inverse = 1.0 / (jnp.sqrt(jnp.sum(total, axis=1, keepdims=True)) + 1e-07)
     for k in range(planes):
@@ -961,55 +1107,73 @@
     step(group if first_only else cols)
     for k, out in enumerate(outs):
         part = x_ref[:, k * group : (k + 1) * group].T.astype(bf16)
-        for at in range(spots):
-            to = pl.multiple_of((place[1] ^ at) * span, span)
+        if first_only:
+            for at in range(spots):
+                to = pl.multiple_of((place[1] ^ at) * span, span)
+                out[pl.ds(to, span), :] = part[at * span : (at + 1) * span, :]
+            continue
+        for at in range(0, spots, 2):
+            to = pl.multiple_of((place[1] // 2 ^ at // 2) * span, span)
+            out[pl.ds(to, span), :] = halves[at][k * span : (k + 1) * span, :]
+            to = pl.multiple_of((place[1] // 2 ^ at // 2) * span + group // 2, span)
             out[pl.ds(to, span), :] = part[at * span : (at + 1) * span, :]
 
 
-def newton(place, halves, planes, first_only, name):
-    spots = len(halves)
-    cols = spots * halves[0].shape[0]
-    count = 1 if first_only else planes
+def newton(place, halves, planes, spots, cols, first_only, name):
     return run(
         functools.partial(newton_kernel, planes, spots, first_only),
         place,
         halves,
-        [like((cols // planes, D), bf16)] * count,
+        [like((cols // planes, D), bf16)] * (1 if first_only else planes),
         name,
         scratch=[pltpu.VMEM((D, cols), f32), pltpu.VMEM((D, cols), bf16)],
         flops=10 * D * D * (2 * cols + D),
     )
 
 
-def att_final_kernel(planes, place, *refs):
-    ms, xs = refs[:planes], refs[planes : 2 * planes]
-    old = refs[2 * planes : 2 * planes + 4]
-    outs, scratch = refs[2 * planes + 4 : -1], refs[-1]
-    for u in range(planes):
-        scratch[0, u] = ms[u][...]
-        scratch[1, u] = xs[u][...]
+def att_final_kernel(planes, span, place, mine, got, *refs):
+    old, outs, rows = refs[:4], refs[4:-1], refs[-1]
+    half = mine.shape[1] // 2
+    core = place[1] % 2
     for which in range(4):
-        m = scratch[0, place[0] ^ which].astype(f32)
-        x = scratch[1, place[0] ^ which].astype(f32)
-        if which < 3:
-            m, x = m.T, x.T
-        outs[which][...] = m
-        outs[4 + which][...] = old[which][...] - muon_rates[which] * x
-
-
-def ffn_give_kernel(planes, hid, place, *refs):
-    count = len(refs) // 3
-    ins, give, keep = refs[:count], refs[count : 2 * count], refs[2 * count :]
+        slot = place[0] ^ which
+        for kind in range(2):
+            for at in range(0, half, span):
+                from_at = kind * half + at
+                rows[pl.ds(pl.multiple_of(2 * at + core * span, span), span), :] = mine[
+                    slot, from_at : from_at + span, :
+                ]
+                rows[pl.ds(pl.multiple_of(2 * at + (1 - core) * span, span), span), :] = got[
+                    slot, from_at : from_at + span, :
+                ]
+            part = rows[...].astype(f32)
+            part = part.T if which < 3 else part
+            if kind == 0:
+                outs[which][...] = part
+            else:
+                outs[4 + which][...] = old[which][...] - muon_rates[which] * part
+
+
+def ffn_give_kernel(planes, hid, span, place, *refs):
+    count = len(refs) // 2
+    ins, give, keep = refs[:count], refs[count], refs[count + 1 :]
+    tall = (planes + 1) * hid
+    wide = planes * span
+
+    for m in range(count):
+        at, to = 2 * planes * hid, count * tall + m * wide
+        give[to : to + wide, :] = ins[m][at : at + wide, :]
 
     def fill(given):
         for m in range(count):
             for k in range(planes):
+                to = slice(m * tall + k * hid, m * tall + (k + 1) * hid)
+                at = (2 * k + given) * hid
+                give[to, :] = ins[m][at : at + hid, :]
                 to = slice(k * hid, (k + 1) * hid)
-                at = (2 * k + given) * hid
-                give[m][to, :] = ins[m][at : at + hid, :]
                 at = (2 * k + 1 - given) * hid
                 keep[m][to, :] = ins[m][at : at + hid, :]
-            give[m][planes * hid :, :] = keep[m][:hid, :]
+            give[m * tall + planes * hid : (m + 1) * tall, :] = keep[m][:hid, :]
 
     @pl.when(place[1] % 2 == 0)
     def _():
@@ -1020,19 +1184,20 @@
         fill(1)
 
 
-def ffn_buffers_kernel(chips, hid, place, *refs):
-    give, keep, got = refs[:chips], refs[chips : 2 * chips], refs[2 * chips : 3 * chips]
-    eo, co = refs[3 * chips :]
-    tail = keep[0].shape[0]
+def ffn_buffers_kernel(chips, hid, place, give, got, *refs):
+    keep, (eo, co) = refs[:chips], refs[chips:]
+    tall = keep[0].shape[0] + hid
+    tail = tall - hid
 
     def fill(kept, given):
         for m in range(chips):
             one = pl.multiple_of((place[1] ^ (2 * m)) * hid, hid)
             two = pl.multiple_of((place[1] ^ (2 * m + 1)) * hid, hid)
+            at = m * tall
             kept[pl.ds(one, hid), :] = keep[m][:hid, :].astype(f32)
-            kept[pl.ds(two, hid), :] = got[m][:hid, :].astype(f32)
-            given[pl.ds(one, hid), :] = give[m][:hid, :].astype(f32)
-            given[pl.ds(two, hid), :] = got[m][tail:, :].astype(f32)
+            kept[pl.ds(two, hid), :] = got[at : at + hid, :].astype(f32)
+            given[pl.ds(one, hid), :] = give[at : at + hid, :].astype(f32)
+            given[pl.ds(two, hid), :] = got[at + tail : at + tall, :].astype(f32)
 
     @pl.when(place[1] % 2 == 0)
     def _():
@@ -1109,6 +1274,9 @@
     def together(*groups):
         return lax.optimization_barrier(groups)
 
+    def together(*groups):
+        return lax.optimization_barrier(groups)
+
     qkv_piece, rest_piece = pieces(
         weight_pieces_kernel,
         place,
@@ -1116,13 +1284,12 @@
         [like((3 * span, D), bf16), like((span + 2 * hid, D), bf16)],
         "weight_pieces",
     )
-    qkv_own, rest_piece = together(jnp.stack(around_planes(qkv_piece)), rest_piece)
-    qkv_own, rest_own = around_chips(qkv_own), around_planes(rest_piece)
-    up_parts = split_positions(out_grad, place)
-    qkv_own, rest_own, up_parts = together(qkv_own, jnp.stack(rest_own), up_parts)
-    qkv_halves = interleave(qkv_own, [swap(part, "dp", 1) for part in qkv_own])
-    rest_own = around_chips(rest_own)
-    ups = [up_parts[0]] + [swap(up_parts[u], "mp", u) for u in to_planes]
+    inputs = layer_in
+    documents = pick(doc_ids, plane)
+    last = (
+        jnp.sum(documents[None, :] <= documents[:, None], axis=1, dtype=jnp.int32)[None, :] - 1
+    )
+    start = jnp.sum(documents[None, :] < documents[:, None], axis=1, dtype=jnp.int32)[None, :]
 
     def to_slots(bias):
         return reorder(reorder(bias, plane, 0), spot, 1)
@@ -1132,31 +1299,26 @@
     bias = bias.reshape(2, chips, 1, planes * hid)
     bout = small_params[FF : FF + D].reshape(1, D)
     alphas = small_params[FF + D :]
-
-    inputs = pick(layer_in, plane)
-    documents = pick(doc_ids, plane)
-    last = (
-        jnp.sum(documents[None, :] <= documents[:, None], axis=1, dtype=jnp.int32)[None, :] - 1
-    )
-    start = jnp.sum(documents[None, :] < documents[:, None], axis=1, dtype=jnp.int32)[None, :]
-
+    token_span = length // planes
+    ups = split_positions(out_grad, place)
+
+    qkv_own, ups = together(around_planes(qkv_piece), ups)
+    qkv_own = around_chips(jnp.stack(qkv_own))
+    rest_own = around_planes(rest_piece)
+    qkv_own, rest_own, last, start, bias = together(
+        qkv_own, rest_own, last, start, bias
+    )
+    qkv_halves = interleave(qkv_own, [swap(part, "dp", 1) for part in qkv_own])
+    rest_own = around_chips(jnp.stack(rest_own))
+    ups = [ups[0]] + [swap(ups[u], "mp", u) for u in to_planes]
     qkv, heads = attention(place, last, inputs, qkv_halves)
     heads, rest_own, ups = together(heads, rest_own, ups)
     rest_halves = interleave(rest_own, [swap(part, "dp", 1) for part in rest_own])
-    att_old, ffn_old = pieces(
-        buffer_pieces_kernel,
-        place,
-        buffers_old,
-        [like((4, span, D), f32), like((2, hid, D), f32)],
-        "buffer_pieces",
-    )
-    rest_halves, att_old, ffn_old = together(rest_halves, att_old, ffn_old)
     lays, rest = feed_forward(place, alphas, inputs, heads, ups, rest_halves, bias, bout)
-    ffn_grad, grad_output, heads_grad, middle_grad, gb_in, gb_out, g_alpha = rest
-
-    ffn_grad = ffn_grad.reshape(2, chips * 2 * planes * hid, D)
-    ffn_got = swap(ffn_grad[1], "dp", 1)
-    lay_got = [lays[0]] + [swap(lays[u], "mp", u) for u in to_planes]
+    ffn_keep, ffn_give, grad_output, heads_grad, middle_grad, gb_in, gb_out, g_alpha = rest
+
+    ffn_rows = (chips * 2 * planes * hid, D)
+    ffn_got = swap(ffn_give.reshape(ffn_rows), "dp", 1)
     gb_in = gb_in.reshape(2, chips, planes, hid).transpose(2, 1, 0, 3).reshape(planes, spots, hid)
     small = jnp.concatenate(
         [to_slots(gb_in).reshape(-1), gb_out.reshape(-1), jnp.sum(g_alpha, axis=1)]
@@ -1166,39 +1328,22 @@
     pair = jnp.concatenate([high, lax.reduce_precision(small - high, 8, 7)]).astype(bf16)
     pair = swap(pair, "dp", 1).astype(f32)
     small = small + pair[:8] + pair[8:]
-    pairs = planes // 2
-    so_far, keep_one, give_one = attention_back(
-        place, start, inputs, qkv_halves, qkv, heads_grad, grad_output, middle_grad, 0, pairs, False
-    )
-    so_far, ffn_got, small = together(so_far, ffn_got, small)
     parts = run(
         ffn_core_kernel,
         place,
-        [ffn_grad[0], ffn_got, small],
+        [ffn_keep.reshape(ffn_rows), ffn_got, small],
         [like((2 * planes * hid + 16, D), bf16)] * chips,
         "ffn_core_sum",
     )
-    so_far, parts = together(so_far, parts)
+    middle_grad, parts, lays = together(middle_grad, parts, lays)
     got = [parts[0]] + [swap(parts[m], "dp", 2 * m) for m in to_chips]
-    ins, keep_two, give_two = attention_back(
-        place,
-        start,
-        inputs,
-        qkv_halves,
-        qkv,
-        heads_grad,
-        grad_output,
-        so_far[0],
-        pairs,
-        planes - pairs,
-        True,
-    )
-    ins, keep_two, give_two, got, lay_got = together(ins, keep_two, give_two, got, lay_got)
-
-    att_keep = jnp.concatenate([keep_one, keep_two], 1)
-    att_give = jnp.concatenate([give_one, give_two], 1)
-    att_rows = chips * planes * 4 * span
-    att_got = swap(att_give.reshape(att_rows, D), "dp", 1)
+    lay_far = [swap(lays[u], "mp", u) for u in to_planes[1:]]
+    ins, att_keep, att_give = attention_back(
+        place, start, inputs, qkv_halves, qkv, heads_grad, heads, grad_output, middle_grad,
+        0, planes, True,
+    )
+    ins, att_keep, att_give, got, lay_far = together(ins, att_keep, att_give, got, lay_far)
+
     parts = run(
         functools.partial(ffn_chip_kernel, chips, hid),
         place,
@@ -1206,84 +1351,81 @@
         [like((2 * hid + 16, D), bf16)] * planes,
         "ffn_chip_sum",
     )
-    parts, att_got = together(parts, att_got)
+    parts, att_give, buffers_old = together(parts, att_give, buffers_old)
     got = [parts[0]] + [swap(parts[k], "mp", k) for k in to_planes]
-    att_parts = sum_parts(place, [att_keep.reshape(att_rows, D), att_got], chips, "att_core_sum")
-    got, att_parts = together(got, att_parts)
+    att_got = swap(att_give, "dp", 1)
+    att_old, ffn_old = pieces(
+        buffer_pieces_kernel,
+        place,
+        buffers_old,
+        [like((4, span, D), f32), like((2, hid, D), f32)],
+        "buffer_pieces",
+    )
+
+    att_parts = run(
+        att_core_kernel,
+        place,
+        [att_keep, att_got],
+        [like((planes * 4 * span, D), bf16)] * chips,
+        "att_core_sum",
+    )
     att_got = [att_parts[0]] + [swap(att_parts[m], "dp", 2 * m) for m in to_chips]
-    piece, small_grad = run(
-        ffn_plane_kernel,
-        place,
-        [ffn_old, *got],
-        [like((2 * hid, D), bf16), like((8, D), f32)],
-        "ffn_plane_sum",
-    )
-    small_grad = small_grad.reshape(-1)[: FF + D + 2]
-    piece, att_got = together(piece, att_got)
-    got = around_planes(piece)
-    parts = run(
-        functools.partial(att_to_owner_kernel, chips, planes),
-        place,
-        att_got + [att_old],
-        [like((planes * span, D), bf16)] * planes,
-        "att_chip_sum",
+    outs = run(
+        functools.partial(plane_messages_kernel, chips, planes),
+        place,
+        [*got, *att_got, ffn_old, att_old],
+        [like((2 * hid + planes * span, D), bf16)] * planes + [like((8, D), f32)],
+        "plane_messages",
         scratch=[pltpu.VMEM((4, planes * span, D), bf16)],
     )
-    got, parts = together(got, parts)
-    att_got = [parts[0]] + [swap(parts[u], "mp", u) for u in to_planes]
-    got = around_chips(jnp.concatenate(got))
-    att_piece = run(
-        functools.partial(att_sum_kernel, planes),
-        place,
-        att_got,
-        [like((planes * span, D), bf16)],
-        "att_plane_sum",
+    small_grad = outs[-1].reshape(-1)[: FF + D + 2]
+    got = [outs[0]] + [swap(outs[k], "mp", k) for k in to_planes]
+    message = run(
+        functools.partial(plane_split_kernel, 2 * hid),
+        place,
+        got,
+        [like((planes * (2 * hid + span), D), bf16)],
+        "plane_split",
     )[0]
-    att_piece, ins = together(att_piece, ins)
-    att_own = around_chips(att_piece)
-    in_got = [ins[0]] + [swap(ins[u], "mp", u) for u in to_planes]
-    att_halves = interleave(att_own, [swap(part, "dp", 1) for part in att_own])
-    att_m = run(
-        functools.partial(spread_kernel, spots),
-        place,
-        att_halves,
-        [like((head_cols, D), bf16)] * planes,
-        "att_spread",
-    )
-    att_m, att_halves = together(att_m, att_halves)
-    att_m = [att_m[0]] + [swap(att_m[u], "mp", u) for u in to_planes]
-    att_x = newton(place, att_halves, planes, False, "newton_att")
-    att_x, in_got, att_m = together(att_x, in_got, att_m)
-    att_x = [att_x[0]] + [swap(att_x[u], "mp", u) for u in to_planes]
-    layer_out = join_positions(lay_got, place)
-    in_grad = join_positions(in_got, place)
-
+    message, ins = together(message, ins)
+    got = around_chips(message)
+    near = swap(jnp.concatenate([ins[1], lays[1]]), "mp", 1)
+    in_far = [swap(ins[u], "mp", u) for u in to_planes[1:]]
+    in_grad = join_positions([ins[0], near[:token_span], *in_far], place)
+    layer_out = join_positions([lays[0], near[token_span:], *lay_far], place)
+    got, in_grad, layer_out = together(got, in_grad, layer_out)
     outs = run(
-        functools.partial(ffn_give_kernel, planes, hid),
+        functools.partial(ffn_give_kernel, planes, hid, span),
         place,
         got,
-        [like(((planes + 1) * hid, D), bf16)] * chips + [like((planes * hid, D), bf16)] * chips,
+        [like((chips * ((planes + 1) * hid + planes * span), D), bf16)]
+        + [like((planes * hid, D), bf16)] * chips,
         "ffn_give",
     )
-    give, keep = outs[:chips], outs[chips:]
-    ffn_got = [swap(part, "dp", 1) for part in give]
-    step = newton(place, interleave(keep, ffn_got), planes, True, "newton_ffn")[0]
-    step, give, keep, ffn_got = together(step, give, keep, ffn_got)
+    give, keep = outs[0], outs[1:]
+    ffn_got = swap(give, "dp", 1)
+    att_x = newton(place, [give, ffn_got], planes, spots, D, False, "newton_att")
+    att_x = jnp.stack([att_x[0]] + [swap(att_x[u], "mp", u) for u in to_planes])
+    step = newton(
+        place, [*keep, ffn_got], planes, spots, planes * hidden_rows, True, "newton_ffn"
+    )[0]
+    step, give, keep, ffn_got, att_x = together(step, give, keep, ffn_got, att_x)
     step_got = swap(step, "dp", 1)
+    att_other = swap(att_x, "dp", 1)
     new_be, new_bc = run(
         functools.partial(ffn_buffers_kernel, chips, hid),
         place,
-        [*give, *keep, *ffn_got],
+        [give, ffn_got, *keep],
         [like((hidden_rows, D), f32)] * 2,
         "ffn_buffers",
     )
     att_out = run(
-        functools.partial(att_final_kernel, planes),
-        place,
-        att_m + att_x + list(weights_old[:4]),
+        functools.partial(att_final_kernel, planes, span),
+        place,
+        [att_x, att_other, *weights_old[:4]],
         [like(w.shape, f32) for w in weights_old[:4]] * 2,
         "att_final",
-        scratch=[pltpu.VMEM((2, planes, head_cols, D), bf16)],
+        scratch=[pltpu.VMEM((head_cols, D), bf16)],
     )
     new_we, new_wc = run(
         ffn_final_kernel,

time: 328 us -> 254 us (0.77); the launches traced: 324 us -> 254 us
  Pallas kernels: 173 us -> 116 us
  starting transfers between devices: 75.8 us -> 64.1 us
  waiting for transfers between devices: 49.5 us -> 59.1 us
  local copies, waits for them, and re-layouts: 16.5 us -> 6.9 us
    pallas_call x22 -> x19, Pallas kernels: 173 us -> 116 us  [run(): pl.pallas_call(kernel, grid_spec=pltpu.PrefetchScalarGridSpec(num_scalar_...]
    ppermute x68 -> x52, starting transfers between devices: 75.8 us -> 64.1 us  [swap(): return lax.ppermute(x, axis, [(a, a ^ mask) for a in range(size)])]
    ppermute x68 -> x52, waiting for transfers between devices: 49.5 us -> 59.1 us  [swap(): return lax.ppermute(x, axis, [(a, a ^ mask) for a in range(size)])]
    slice x1, local copies, waits for them, and re-layouts: 4.72 us -> 0.03 us  [shards(): layer_out = join_positions([lays[0], near[token_span:], *lay_far], place)]
    unnamed x164 -> x89, local copies, waits for them, and re-layouts: 7.32 us -> 4.65 us
  transfers between devices with their start and end apart: 68 -> 52, of which waited for: 18 -> 20; matrix products, arithmetic and copies ran while one was open for 3% -> 3% of each run, Pallas kernels for 42% -> 28%
where the time goes in v3:
time: 254 us
  Pallas kernels  116 us (46%)
  starting transfers between devices  64.1 us (25%)
  waiting for transfers between devices  59.1 us (23%)
  local copies, waits for them, and re-layouts  6.9 us (3%)
  other arithmetic  5.66 us (2%)
    pallas_call x19, Pallas kernels, run(): pl.pallas_call(kernel, grid_spec=pltpu.PrefetchScalarGridSpec(num_scalar_...  116 us
    ppermute x52, starting transfers between devices, swap(): return lax.ppermute(x, axis, [(a, a ^ mask) for a in range(size)])  64.1 us
    ppermute x52, waiting for transfers between devices, swap(): return lax.ppermute(x, axis, [(a, a ^ mask) for a in range(size)])  59.1 us
  transfers between devices with their start and end apart: 52, of which 20 were waited for; matrix products, arithmetic and copies ran while one was open for 3% of the time, Pallas kernels for 28%

profile of v3, /device:TPU:0, one launch (start us, length us, event | category | flops | bytes accessed | tf_op | source)
XLA Modules:
  0.0 253.6 jit_solution(2197498388818773806)
XLA Ops:
  1.4 2.9 %weight_pieces.1 = (bf16[48,512]{1,0:T(8,128)(2,1)}, bf16[144,512]{1,0:T(8,128)(2,1)}) custom-call(s32[2]{0:T(128)} %pad_add_fusion.place, f32[512,128]{1,0:T(8,128)} %refs_0_.3, f32[512,128]{1,0:T(8,128)} %refs_1_.5, f32[512,128]{1,0:T(8,128)} %refs_2_.3, f32[128,512]{1,0:T(8,128)} %refs_3_.3, f32[512,512]{1,0:T(8,128)} %we.1, f32[512,512]{1,0:T(8,128)} %wc.1), custom_call_target="tpu_custom_call" | custom-call | tf_op jit(solution)/shard_map/weight_pieces/pallas_call | solution.py:414
  4.3 5.0 %collective-permute-start.2 = (bf16[48,512]{1,0:T(8,128)(2,1)}, bf16[48,512]{1,0:T(8,128)(2,1)S(1)}, u32[]{:S(2)}, u32[]{:S(2)}) collective-permute-start(bf16[48,512]{1,0:T(8,128)(2,1)} %get-tuple-element.167), channel_id=1, source_target_pairs={{0,3},{1,2},{2,1},{3,0},{4,7},{5,6},{6,5},{7,4},{8,11},{9,10},{10,... | collective-permute-start | bytes 147464 | tf_op jit(solution)/shard_map/ppermute | solution.py:386
  9.9 3.8 %collective-permute-start.8 = (bf16[144,512]{1,0:T(8,128)(2,1)}, bf16[144,512]{1,0:T(8,128)(2,1)S(1)}, u32[]{:S(2)}, u32[]{:S(2)}) collective-permute-start(bf16[144,512]{1,0:T(8,128)(2,1)} %get-tuple-element.180), channel_id=1, source_target_pairs={{0,3},{1,2},{2,1},{3,0},{4,7},{5,6},{6,5},{7,4},{8,11},{9,10},{10,... | collective-permute-start | bytes 442376 | tf_op jit(solution)/shard_map/ppermute | solution.py:386
  17.7 3.4 %collective-permute-done.1 = bf16[48,512]{1,0:T(8,128)(2,1)S(1)} collective-permute-done((bf16[48,512]{1,0:T(8,128)(2,1)}, bf16[48,512]{1,0:T(8,128)(2,1)S(1)}, u32[]{:S(2)}, u32[]{:S(2)}) %collective-permute-start.1) | collective-permute-done | bytes 49184 | tf_op jit(solution)/shard_map/ppermute | solution.py:386
  21.1 2.5 collective-permute-start.5
  31.1 3.2 %collective-permute-done.16.refs_4_ = bf16[256,512]{1,0:T(8,128)(2,1)} collective-permute-done((bf16[256,512]{1,0:T(8,128)(2,1)S(1)}, bf16[256,512]{1,0:T(8,128)(2,1)}, u32[]{:S(2)}, u32[]{:S(2)}) %collective-permute-start.16) | collective-permute-done | bytes 262176 | tf_op jit(solution)/shard_map/ppermute | solution.py:386
  40.9 17.9 %attention_forward.1 = (bf16[4,4,1024,128]{3,2,1,0:T(8,128)(2,1)}, bf16[1024,512]{1,0:T(8,128)(2,1)}) custom-call(s32[2]{0:T(128)} %pad_add_fusion.place, s32[1,1024]{1,0:T(1,128)} %bitcast.48, bf16[4,1024,512]{2,1,0:T(8,128)(2,1)} %in_hbm.1, bf16[4,48,512]{2,1,0:T(8,128)(2,1)} %copy-done.23, bf16[4,48,512]{2,1,0:T(8,128)(2,1)} %copy-done.40, ...), custom_call_target="tpu_custom_call" | custom-call | flops 5368709120 | bytes 11014144 | tf_op jit(solution)/shard_map/attention_forward/pallas_call | solution.py:414
  58.9 2.6 %collective-permute-done.14.refs_11_ = bf16[4,144,512]{2,1,0:T(8,128)(2,1)S(1)} collective-permute-done((bf16[4,144,512]{2,1,0:T(8,128)(2,1)S(1)}, bf16[4,144,512]{2,1,0:T(8,128)(2,1)S(1)}, u32[]{:S(2)}, u32[]{:S(2)}) %collective-permute-start.14) | collective-permute-done | bytes 589856 | tf_op jit(solution)/shard_map/ppermute | solution.py:386
  66.4 27.7 %feed_forward.1 = (bf16[256,512]{1,0:T(8,128)(2,1)}, bf16[256,512]{1,0:T(8,128)(2,1)}, bf16[256,512]{1,0:T(8,128)(2,1)}, bf16[256,512]{1,0:T(8,128)(2,1)}, bf16[...) custom-call(s32[2]{0:T(128)} %pad_add_fusion.place, ...), custom_call_target="tpu_custom_call" | custom-call | flops 12884901888 | bytes 19947528 | tf_op jit(solution)/shard_map/feed_forward/pallas_call | solution.py:414
  101.2 2.6 %collective-permute-start.28 = (bf16[256,512]{1,0:T(8,128)(2,1)S(1)}, bf16[256,512]{1,0:T(8,128)(2,1)S(1)}, u32[]{:S(2)}, u32[]{:S(2)}) collective-permute-start(bf16[256,512]{1,0:T(8,128)(2,1)S(1)} %copy-done.37), channel_id=1, source_target_pairs={{0,2},{1,3},{2,0},{3,1},{4,6},{5,7},{6,4},{7,5},{8,10},{9,11},{10,... | collective-permute-start | bytes 786440 | tf_op jit(solution)/shard_map/ppermute | solution.py:386
  108.3 26.5 %attention_backward.1 = (bf16[256,512]{1,0:T(8,128)(2,1)}, bf16[256,512]{1,0:T(8,128)(2,1)}, bf16[256,512]{1,0:T(8,128)(2,1)}, bf16[256,512]{1,0:T(8,128)(2,1)},...) custom-call(s32[2]{0:T(128)} %pad_add_fusion.place, s32[1,1024]{1,0:T(1,128)} %bitcast.53, ...), custom_call_target="tpu_custom_call" | custom-call | flops 11274289152 | bytes 17829888 | tf_op jit(solution)/shard_map/attention_backward/pallas_call | solution.py:414
  145.9 3.0 %buffer_pieces.1 = (f32[4,16,512]{2,1,0:T(8,128)}, f32[2,64,512]{2,1,0:T(8,128)}) custom-call(s32[2]{0:T(128)} %pad_add_fusion.place, f32[512,128]{1,0:T(8,128)} %q.2, f32[512,128]{1,0:T(8,128)} %k.2, f32[512,128]{1,0:T(8,128)} %v.2, f32[128,512]{1,0:T(8,128)} %o.2, f32[512,512]{1,0:T(8,128)} %e.2, f32[512,512]{1,0:T(8,128)} %c.2), custom_call_target="tpu_custom_call" | custom-call | tf_op jit(solution)/shard_map/buffer_pieces/pallas_call | solution.py:414
  148.9 6.7 %collective-permute-done.31.refs_2_ = bf16[144,512]{1,0:T(8,128)(2,1)S(1)} collective-permute-done((bf16[144,512]{1,0:T(8,128)(2,1)S(1)}, bf16[144,512]{1,0:T(8,128)(2,1)S(1)}, u32[]{:S(2)}, u32[]{:S(2)}) %collective-permute-start.31) | collective-permute-done | bytes 147488 | tf_op jit(solution)/shard_map/ppermute | solution.py:386
  158.4 3.4 %collective-permute-start.37 = (bf16[192,512]{1,0:T(8,128)(2,1)S(1)}, bf16[192,512]{1,0:T(8,128)(2,1)S(1)}, u32[]{:S(2)}, u32[]{:S(2)}) collective-permute-start(bf16[192,512]{1,0:T(8,128)(2,1)S(1)} %get-tuple-element.255), channel_id=1, source_target_pairs={{0,1},{1,0},{2,3},{3,2},{4,5},{5,4},{6,7},{7,6},{8,9},{9,8},{10,11... | collective-permute-start | bytes 589832 | tf_op jit(solution)/shard_map/ppermute | solution.py:386
  164.7 5.6 %collective-permute-done.37.refs_1_ = bf16[192,512]{1,0:T(8,128)(2,1)S(1)} collective-permute-done((bf16[192,512]{1,0:T(8,128)(2,1)S(1)}, bf16[192,512]{1,0:T(8,128)(2,1)S(1)}, u32[]{:S(2)}, u32[]{:S(2)}) %collective-permute-start.37) | collective-permute-done | bytes 196640 | tf_op jit(solution)/shard_map/ppermute | solution.py:386
  170.3 8.7 %collective-permute-done.38.refs_2_ = bf16[192,512]{1,0:T(8,128)(2,1)S(1)} collective-permute-done((bf16[192,512]{1,0:T(8,128)(2,1)S(1)}, bf16[192,512]{1,0:T(8,128)(2,1)S(1)}, u32[]{:S(2)}, u32[]{:S(2)}) %collective-permute-start.38) | collective-permute-done | bytes 196640 | tf_op jit(solution)/shard_map/ppermute | solution.py:386
  179.7 3.3 %collective-permute-start.43 = (bf16[512,512]{1,0:T(8,128)(2,1)S(1)}, bf16[512,512]{1,0:T(8,128)(2,1)S(1)}, u32[]{:S(2)}, u32[]{:S(2)}) collective-permute-start(bf16[512,512]{1,0:T(8,128)(2,1)S(1)} %pad_maximum_fusion.1), channel_id=1, source_target_pairs={{0,1},{1,0},{2,3},{3,2},{4,5},{5,4},{6,7},{7,6},{8,9},{9,8},{10,11... | collective-permute-start | bytes 1572872 | tf_op jit(solution)/shard_map/ppermute | solution.py:386
  188.2 11.2 %collective-permute-done.43 = bf16[512,512]{1,0:T(8,128)(2,1)S(1)} collective-permute-done((bf16[512,512]{1,0:T(8,128)(2,1)S(1)}, bf16[512,512]{1,0:T(8,128)(2,1)S(1)}, u32[]{:S(2)}, u32[]{:S(2)}) %collective-permute-start.43) | collective-permute-done | bytes 524320 | tf_op jit(solution)/shard_map/ppermute | solution.py:386
  199.4 3.4 %collective-permute-start.45 = (bf16[256,512]{1,0:T(8,128)(2,1)S(1)}, bf16[256,512]{1,0:T(8,128)(2,1)S(1)}, u32[]{:S(2)}, u32[]{:S(2)}) collective-permute-start(bf16[256,512]{1,0:T(8,128)(2,1)S(1)} %copy-done.34), channel_id=1, source_target_pairs={{0,3},{1,2},{2,1},{3,0},{4,7},{5,6},{6,5},{7,4},{8,11},{9,10},{10,... | collective-permute-start | bytes 786440 | tf_op jit(solution)/shard_map/ppermute | solution.py:386
  204.8 3.4 %collective-permute-done.45.refs_3_ = bf16[256,512]{1,0:T(8,128)(2,1)S(1)} collective-permute-done((bf16[256,512]{1,0:T(8,128)(2,1)S(1)}, bf16[256,512]{1,0:T(8,128)(2,1)S(1)}, u32[]{:S(2)}, u32[]{:S(2)}) %collective-permute-start.45) | collective-permute-done | bytes 262176 | tf_op jit(solution)/shard_map/ppermute | solution.py:386
  211.0 3.4 %collective-permute-done.46.refs_4_.refs_1_.got = bf16[1536,512]{1,0:T(8,128)(2,1)S(1)} collective-permute-done((bf16[1536,512]{1,0:T(8,128)(2,1)S(1)}, bf16[1536,512]{1,0:T(8,128)(2,1)S(1)}, u32[]{:S(2)}, u32[]{:S(2)}) %collective-permute-start.46) | collective-permute-done | bytes 1572896 | tf_op jit(solution)/shard_map/ppermute | solution.py:386
  214.4 7.6 %newton_att.1 = (bf16[128,512]{1,0:T(8,128)(2,1)S(1)}, bf16[128,512]{1,0:T(8,128)(2,1)S(1)}, bf16[128,512]{1,0:T(8,128)(2,1)S(1)}, bf16[128,512]{1,0:T(8,128)(2,1)S(1)}) custom-call(s32[2]{0:T(128)S(1)} %copy-done.18, bf16[1536,512]{1,0:T(8,128)(2,1)S(1)} %get-tuple-element.291.refs_0_.give, bf16[1536,512]{1,0:T(8,128)(2,1)S(1)} %collective-permute-done.46.refs_4_.refs_1_.got), custom_call_target="tpu_custom_call" | custom-call | flops 4026531840 | bytes 3670016 | tf_op jit(solution)/shard_map/newton_att/pallas_call | solution.py:414
  222.0 6.2 %collective-permute-start.47 = (bf16[128,512]{1,0:T(8,128)(2,1)S(1)}, bf16[128,512]{1,0:T(8,128)(2,1)S(1)}, u32[]{:S(2)}, u32[]{:S(2)}) collective-permute-start(bf16[128,512]{1,0:T(8,128)(2,1)S(1)} %get-tuple-element.283), channel_id=1, source_target_pairs={{0,1},{1,0},{2,3},{3,2},{4,5},{5,4},{6,7},{7,6},{8,9},{9,8},{10,11... | collective-permute-start | bytes 393224 | tf_op jit(solution)/shard_map/ppermute | solution.py:386
  230.6 15.2 %newton_ffn.1.mine = bf16[512,512]{1,0:T(8,128)(2,1)S(1)} custom-call(s32[2]{0:T(128)S(1)} %copy-done.18, bf16[256,512]{1,0:T(8,128)(2,1)S(1)} %get-tuple-element.293.refs_0_, bf16[256,512]{1,0:T(8,128)(2,1)S(1)} %get-tuple-element.294.refs_1_, bf16[256,512]{1,0:T(8,128)(2,1)S(1)} %get-tuple-element.295.refs_2_, ...), custom_call_target="tpu_custom_call" | custom-call | flops 12079595520 | bytes 3145728 | tf_op jit(solution)/shard_map/newton_ffn/pallas_call | solution.py:414
  (225 shorter events, 72.9 us)
Async XLA Ops:
  9.9 14.2 %collective-permute-start.8 = (bf16[144,512]{1,0:T(8,128)(2,1)}, bf16[144,512]{1,0:T(8,128)(2,1)S(1)}, u32[]{:S(2)}, u32[]{:S(2)}) collective-permute-start(bf16[144,512]{1,0:T(8,128)(2,1)} %get-tuple-element.180), channel_id=1, source_target_pairs={{0,3},{1,2},{2,1},{3,0},{4,7},{5,6},{6,5},{7,4},{8,11},{9,10},{10,... | collective-permute-start | bytes 442376 | tf_op jit(solution)/shard_map/ppermute | solution.py:386
  34.4 24.5 %collective-permute-start.15 = (bf16[4,144,512]{2,1,0:T(8,128)(2,1)S(1)}, bf16[4,144,512]{2,1,0:T(8,128)(2,1)S(1)}, u32[]{:S(2)}, u32[]{:S(2)}) collective-permute-start(bf16[4,144,512]{2,1,0:T(8,128)(2,1)S(1)} %pad_maximum_fusion.refs_7_), channel_id=1, source_target_pairs={{0,24},{4,28},{8,16},{12,20},{16,8},{20,12},{24,0},{28,4},{1,25},{... | collective-permute-start | bytes 1769480 | tf_op jit(solution)/shard_map/ppermute | solution.py:386
  36.8 24.7 %collective-permute-start.14 = (bf16[4,144,512]{2,1,0:T(8,128)(2,1)S(1)}, bf16[4,144,512]{2,1,0:T(8,128)(2,1)S(1)}, u32[]{:S(2)}, u32[]{:S(2)}) collective-permute-start(bf16[4,144,512]{2,1,0:T(8,128)(2,1)S(1)} %pad_maximum_fusion.refs_7_), channel_id=1, source_target_pairs={{0,16},{4,20},{8,24},{12,28},{16,0},{20,4},{24,8},{28,12},{1,17},{... | collective-permute-start | bytes 1769480 | tf_op jit(solution)/shard_map/ppermute | solution.py:386
  37.3 24.4 %collective-permute-start.13 = (bf16[4,144,512]{2,1,0:T(8,128)(2,1)S(1)}, bf16[4,144,512]{2,1,0:T(8,128)(2,1)}, u32[]{:S(2)}, u32[]{:S(2)}) collective-permute-start(bf16[4,144,512]{2,1,0:T(8,128)(2,1)S(1)} %pad_maximum_fusion.refs_7_), channel_id=1, source_target_pairs={{0,8},{4,12},{8,0},{12,4},{16,24},{20,28},{24,16},{28,20},{1,9},{5... | collective-permute-start | bytes 1769480 | tf_op jit(solution)/shard_map/ppermute | solution.py:386
  37.9 20.9 %collective-permute-start.17 = (bf16[256,512]{1,0:T(8,128)(2,1)S(1)}, bf16[256,512]{1,0:T(8,128)(2,1)S(1)}, u32[]{:S(2)}, u32[]{:S(2)}) collective-permute-start(bf16[256,512]{1,0:T(8,128)(2,1)S(1)} %get-tuple-element.186), channel_id=1, source_target_pairs={{0,2},{1,3},{2,0},{3,1},{4,6},{5,7},{6,4},{7,5},{8,10},{9,11},{10,... | collective-permute-start | bytes 786440 | tf_op jit(solution)/shard_map/ppermute | solution.py:386
  39.6 19.2 %collective-permute-start.18 = (bf16[256,512]{1,0:T(8,128)(2,1)S(1)}, bf16[256,512]{1,0:T(8,128)(2,1)S(1)}, u32[]{:S(2)}, u32[]{:S(2)}) collective-permute-start(bf16[256,512]{1,0:T(8,128)(2,1)S(1)} %get-tuple-element.187), channel_id=1, source_target_pairs={{0,3},{1,2},{2,1},{3,0},{4,7},{5,6},{6,5},{7,4},{8,11},{9,10},{10,... | collective-permute-start | bytes 786440 | tf_op jit(solution)/shard_map/ppermute | solution.py:386
  101.2 33.6 %collective-permute-start.28 = (bf16[256,512]{1,0:T(8,128)(2,1)S(1)}, bf16[256,512]{1,0:T(8,128)(2,1)S(1)}, u32[]{:S(2)}, u32[]{:S(2)}) collective-permute-start(bf16[256,512]{1,0:T(8,128)(2,1)S(1)} %copy-done.37), channel_id=1, source_target_pairs={{0,2},{1,3},{2,0},{3,1},{4,6},{5,7},{6,4},{7,5},{8,10},{9,11},{10,... | collective-permute-start | bytes 786440 | tf_op jit(solution)/shard_map/ppermute | solution.py:386
  103.9 31.0 %collective-permute-start.29 = (bf16[256,512]{1,0:T(8,128)(2,1)S(1)}, bf16[256,512]{1,0:T(8,128)(2,1)S(1)}, u32[]{:S(2)}, u32[]{:S(2)}) collective-permute-start(bf16[256,512]{1,0:T(8,128)(2,1)S(1)} %copy-done.36), channel_id=1, source_target_pairs={{0,3},{1,2},{2,1},{3,0},{4,7},{5,6},{6,5},{7,4},{8,11},{9,10},{10,... | collective-permute-start | bytes 786440 | tf_op jit(solution)/shard_map/ppermute | solution.py:386
  104.8 30.0 %collective-permute-start.25 = (bf16[528,512]{1,0:T(8,128)(2,1)S(1)}, bf16[528,512]{1,0:T(8,128)(2,1)S(1)}, u32[]{:S(2)}, u32[]{:S(2)}) collective-permute-start(bf16[528,512]{1,0:T(8,128)(2,1)S(1)} %get-tuple-element.222), channel_id=1, source_target_pairs={{0,8},{4,12},{8,0},{12,4},{16,24},{20,28},{24,16},{28,20},{1,9},{5... | collective-permute-start | bytes 1622024 | tf_op jit(solution)/shard_map/ppermute | solution.py:386
  106.3 28.5 %collective-permute-start.26 = (bf16[528,512]{1,0:T(8,128)(2,1)S(1)}, bf16[528,512]{1,0:T(8,128)(2,1)S(1)}, u32[]{:S(2)}, u32[]{:S(2)}) collective-permute-start(bf16[528,512]{1,0:T(8,128)(2,1)S(1)} %get-tuple-element.223), channel_id=1, source_target_pairs={{0,16},{4,20},{8,24},{12,28},{16,0},{20,4},{24,8},{28,12},{1,17},{... | collective-permute-start | bytes 1622024 | tf_op jit(solution)/shard_map/ppermute | solution.py:386
  107.1 27.8 %collective-permute-start.27 = (bf16[528,512]{1,0:T(8,128)(2,1)S(1)}, bf16[528,512]{1,0:T(8,128)(2,1)S(1)}, u32[]{:S(2)}, u32[]{:S(2)}) collective-permute-start(bf16[528,512]{1,0:T(8,128)(2,1)S(1)} %get-tuple-element.224), channel_id=1, source_target_pairs={{0,24},{4,28},{8,16},{12,20},{16,8},{20,12},{24,0},{28,4},{1,25},{... | collective-permute-start | bytes 1622024 | tf_op jit(solution)/shard_map/ppermute | solution.py:386
  139.5 16.2 %collective-permute-start.34 = (bf16[256,512]{1,0:T(8,128)(2,1)S(1)}, bf16[256,512]{1,0:T(8,128)(2,1)S(1)}, u32[]{:S(2)}, u32[]{:S(2)}) collective-permute-start(bf16[256,512]{1,0:T(8,128)(2,1)S(1)} %get-tuple-element.243), channel_id=1, source_target_pairs={{0,8},{4,12},{8,0},{12,4},{16,24},{20,28},{24,16},{28,20},{1,9},{5... | collective-permute-start | bytes 786440 | tf_op jit(solution)/shard_map/ppermute | solution.py:386
  141.1 14.6 %collective-permute-start.35 = (bf16[256,512]{1,0:T(8,128)(2,1)S(1)}, bf16[256,512]{1,0:T(8,128)(2,1)S(1)}, u32[]{:S(2)}, u32[]{:S(2)}) collective-permute-start(bf16[256,512]{1,0:T(8,128)(2,1)S(1)} %get-tuple-element.244), channel_id=1, source_target_pairs={{0,16},{4,20},{8,24},{12,28},{16,0},{20,4},{24,8},{28,12},{1,17},{... | collective-permute-start | bytes 786440 | tf_op jit(solution)/shard_map/ppermute | solution.py:386
  141.8 13.8 %collective-permute-start.36 = (bf16[256,512]{1,0:T(8,128)(2,1)S(1)}, bf16[256,512]{1,0:T(8,128)(2,1)S(1)}, u32[]{:S(2)}, u32[]{:S(2)}) collective-permute-start(bf16[256,512]{1,0:T(8,128)(2,1)S(1)} %get-tuple-element.245), channel_id=1, source_target_pairs={{0,24},{4,28},{8,16},{12,20},{16,8},{20,12},{24,0},{28,4},{1,25},{... | collective-permute-start | bytes 786440 | tf_op jit(solution)/shard_map/ppermute | solution.py:386
  161.8 17.2 %collective-permute-start.38 = (bf16[192,512]{1,0:T(8,128)(2,1)S(1)}, bf16[192,512]{1,0:T(8,128)(2,1)S(1)}, u32[]{:S(2)}, u32[]{:S(2)}) collective-permute-start(bf16[192,512]{1,0:T(8,128)(2,1)S(1)} %get-tuple-element.256), channel_id=1, source_target_pairs={{0,2},{1,3},{2,0},{3,1},{4,6},{5,7},{6,4},{7,5},{8,10},{9,11},{10,... | collective-permute-start | bytes 589832 | tf_op jit(solution)/shard_map/ppermute | solution.py:386
  163.3 15.7 %collective-permute-start.39 = (bf16[192,512]{1,0:T(8,128)(2,1)S(1)}, bf16[192,512]{1,0:T(8,128)(2,1)S(1)}, u32[]{:S(2)}, u32[]{:S(2)}) collective-permute-start(bf16[192,512]{1,0:T(8,128)(2,1)S(1)} %get-tuple-element.257), channel_id=1, source_target_pairs={{0,3},{1,2},{2,1},{3,0},{4,7},{5,6},{6,5},{7,4},{8,11},{9,10},{10,... | collective-permute-start | bytes 589832 | tf_op jit(solution)/shard_map/ppermute | solution.py:386
  179.7 19.7 %collective-permute-start.43 = (bf16[512,512]{1,0:T(8,128)(2,1)S(1)}, bf16[512,512]{1,0:T(8,128)(2,1)S(1)}, u32[]{:S(2)}, u32[]{:S(2)}) collective-permute-start(bf16[512,512]{1,0:T(8,128)(2,1)S(1)} %pad_maximum_fusion.1), channel_id=1, source_target_pairs={{0,1},{1,0},{2,3},{3,2},{4,5},{5,4},{6,7},{7,6},{8,9},{9,8},{10,11... | collective-permute-start | bytes 1572872 | tf_op jit(solution)/shard_map/ppermute | solution.py:386
  183.0 27.2 %collective-permute-start.42 = (bf16[576,512]{1,0:T(8,128)(2,1)S(1)}, bf16[576,512]{1,0:T(8,128)(2,1)S(1)}, u32[]{:S(2)}, u32[]{:S(2)}) collective-permute-start(bf16[576,512]{1,0:T(8,128)(2,1)S(1)} %plane_split.1.refs_0_), channel_id=1, source_target_pairs={{0,24},{4,28},{8,16},{12,20},{16,8},{20,12},{24,0},{28,4},{1,25},{... | collective-permute-start | bytes 1769480 | tf_op jit(solution)/shard_map/ppermute | solution.py:386
  184.4 25.8 %collective-permute-start.41 = (bf16[576,512]{1,0:T(8,128)(2,1)S(1)}, bf16[576,512]{1,0:T(8,128)(2,1)S(1)}, u32[]{:S(2)}, u32[]{:S(2)}) collective-permute-start(bf16[576,512]{1,0:T(8,128)(2,1)S(1)} %plane_split.1.refs_0_), channel_id=1, source_target_pairs={{0,16},{4,20},{8,24},{12,28},{16,0},{20,4},{24,8},{28,12},{1,17},{... | collective-permute-start | bytes 1769480 | tf_op jit(solution)/shard_map/ppermute | solution.py:386
  186.0 24.2 %collective-permute-start.40 = (bf16[576,512]{1,0:T(8,128)(2,1)S(1)}, bf16[576,512]{1,0:T(8,128)(2,1)S(1)}, u32[]{:S(2)}, u32[]{:S(2)}) collective-permute-start(bf16[576,512]{1,0:T(8,128)(2,1)S(1)} %plane_split.1.refs_0_), channel_id=1, source_target_pairs={{0,8},{4,12},{8,0},{12,4},{16,24},{20,28},{24,16},{28,20},{1,9},{5... | collective-permute-start | bytes 1769480 | tf_op jit(solution)/shard_map/ppermute | solution.py:386
  186.5 18.3 %collective-permute-start.44 = (bf16[256,512]{1,0:T(8,128)(2,1)S(1)}, bf16[256,512]{1,0:T(8,128)(2,1)S(1)}, u32[]{:S(2)}, u32[]{:S(2)}) collective-permute-start(bf16[256,512]{1,0:T(8,128)(2,1)S(1)} %copy-done.35), channel_id=1, source_target_pairs={{0,2},{1,3},{2,0},{3,1},{4,6},{5,7},{6,4},{7,5},{8,10},{9,11},{10,... | collective-permute-start | bytes 786440 | tf_op jit(solution)/shard_map/ppermute | solution.py:386
  222.0 23.8 %collective-permute-start.47 = (bf16[128,512]{1,0:T(8,128)(2,1)S(1)}, bf16[128,512]{1,0:T(8,128)(2,1)S(1)}, u32[]{:S(2)}, u32[]{:S(2)}) collective-permute-start(bf16[128,512]{1,0:T(8,128)(2,1)S(1)} %get-tuple-element.283), channel_id=1, source_target_pairs={{0,1},{1,0},{2,3},{3,2},{4,5},{5,4},{6,7},{7,6},{8,9},{9,8},{10,11... | collective-permute-start | bytes 393224 | tf_op jit(solution)/shard_map/ppermute | solution.py:386
  228.2 17.7 %collective-permute-start.48 = (bf16[128,512]{1,0:T(8,128)(2,1)S(1)}, bf16[128,512]{1,0:T(8,128)(2,1)S(1)}, u32[]{:S(2)}, u32[]{:S(2)}) collective-permute-start(bf16[128,512]{1,0:T(8,128)(2,1)S(1)} %get-tuple-element.284), channel_id=1, source_target_pairs={{0,2},{1,3},{2,0},{3,1},{4,6},{5,7},{6,4},{7,5},{8,10},{9,11},{10,... | collective-permute-start | bytes 393224 | tf_op jit(solution)/shard_map/ppermute | solution.py:386
  228.2 17.7 %collective-permute-start.49 = (bf16[128,512]{1,0:T(8,128)(2,1)S(1)}, bf16[128,512]{1,0:T(8,128)(2,1)S(1)}, u32[]{:S(2)}, u32[]{:S(2)}) collective-permute-start(bf16[128,512]{1,0:T(8,128)(2,1)S(1)} %get-tuple-element.285), channel_id=1, source_target_pairs={{0,3},{1,2},{2,1},{3,0},{4,7},{5,6},{6,5},{7,4},{8,11},{9,10},{10,... | collective-permute-start | bytes 393224 | tf_op jit(solution)/shard_map/ppermute | solution.py:386
  (73 other events, 732.8 us)

commit v4 on v3

--- a/solution.py
+++ b/solution.py
@@ -509,8 +509,13 @@
     return max(0, first_row + 1 - max_doc) // 128 * 128
 
 
-def pair_weights(halves, which, span):
-    return jnp.concatenate([half[0, which * span : (which + 1) * span, :] for half in halves], 0)
+def pair_weights(own, other, span):
+    parts = []
+    for which in range(3):
+        for m in range(own.shape[0]):
+            for half in (own, other):
+                parts.append(half[m, 0, which * span : (which + 1) * span, :])
+    return jnp.concatenate(parts, 0)
 
 
 def interleave(own, other):
@@ -541,9 +546,9 @@
 
 
 def forward_kernel(place, last_ref, in_ref, *refs):
-    halves, (x_ref, o_ref, bias_ref, q_ref, v_ref) = refs[:-5], refs[-5:]
+    own, other, x_ref, o_ref, bias_ref, q_ref, v_ref = refs
     length = in_ref.shape[1]
-    span = halves[0].shape[1] // 3
+    span = own.shape[2] // 3
     blocks = [(first, window(first), first + q_rows) for first in range(0, length, q_rows)]
 
     @pl.when(pl.program_id(0) == 0)
@@ -554,7 +559,7 @@
             allowed = (col <= row) & (row <= last_ref[:, low:high])
             bias_ref[first:high, : high - low] = jnp.where(allowed, 0.0, mask_fill)
 
-    weight = jnp.concatenate([pair_weights(halves, which, span) for which in range(3)], 0)
+    weight = pair_weights(own, other, span)
     rows = mm(in_ref[0], weight, nt).astype(bf16)
     query = rows[:, :128] * jnp.asarray(HEAD_DIM**-0.5, bf16)
     x_ref[0, 2] = rows[:, 128:256]
@@ -581,8 +586,8 @@
 
 def attention(place, last, inputs, halves):
     length = inputs.shape[1]
-    planes, rows, _ = halves[0].shape
-    half = pl.BlockSpec((1, rows, D), lambda h, place: (h, 0, 0))
+    chips, planes, rows, _ = halves[0].shape
+    half = pl.BlockSpec((chips, 1, rows, D), lambda h, place: (0, h, 0, 0))
     return run(
         forward_kernel,
         place,
@@ -609,14 +614,14 @@
 def backward_kernel(
     is_last, spots, place, start_ref, in_hbm, x_ref, g_ref, o_ref, gout_ref, gmid_hbm, *rest
 ):
-    halves, rest = rest[:spots], rest[spots:]
+    own, other, rest = rest[0], rest[1], rest[2:]
     ins, rest = rest[:-12], rest[-12:]
     keep_ref, give_ref, dk_ref, dv_ref, dq_ref, acc_ref, bias_ref, k_ref, v_ref, gs_ref = rest[:10]
     in_ref, sems = rest[10:]
     length = in_ref.shape[0]
     load_acc = pltpu.make_async_copy(gmid_hbm, acc_ref, sems.at[0])
     load_in = pltpu.make_async_copy(in_hbm.at[place[0]], in_ref, sems.at[1])
-    span = halves[0].shape[1] // 3
+    span = own.shape[2] // 3
     chips = spots // 2
     step = pl.program_id(0)
     blocks = [(first, window(first), first + q_rows) for first in range(0, length, q_rows)]
@@ -661,7 +666,7 @@
         dq_ref[first:high, :] = (dq * HEAD_DIM**-0.5).astype(bf16)
     grads = (dq_ref[...], dk_ref[...].astype(bf16), dv_ref[...].astype(bf16))
     grads = jnp.concatenate(grads, 1)
-    weight = jnp.concatenate([pair_weights(halves, which, span) for which in range(3)], 0)
+    weight = pair_weights(own, other, span)
 
     @pl.when(step == 0)
     def _():
@@ -697,11 +702,10 @@
     place, start, inputs, halves, qkv, heads_grad, heads, grad_output, so_far, first, count, is_last
 ):
     length = inputs.shape[1]
-    planes, rows, _ = halves[0].shape
-    spots = len(halves)
-    chips = spots // 2
+    chips, planes, rows, _ = halves[0].shape
+    spots = 2 * chips
     span = rows // 3
-    half = pl.BlockSpec((1, rows, D), lambda h, place: (first + h, 0, 0))
+    half = pl.BlockSpec((chips, 1, rows, D), lambda h, place: (0, first + h, 0, 0))
     out_half = pl.BlockSpec((chips, 1, 4 * span, D), lambda h, place: (0, h, 0, 0))
     outs = [like((length // planes, D), bf16)] * planes if is_last else [like((length, D), f32)]
     out = run(
@@ -721,7 +725,7 @@
             pl.BlockSpec((128, D), lambda h, place: (first + h, 0)),
             hbm,
         ]
-        + [half] * spots,
+        + [half] * 2,
         out_specs=([whole] * planes if is_last else [hbm]) + [out_half] * 2,
         scratch=[
             pltpu.VMEM((length, 128), f32),
@@ -989,89 +993,93 @@
         small_write(out, total)
 
 
-def ffn_chip_kernel(count, hid, place, *refs):
-    ins, outs = refs[:count], refs[count:]
+def ffn_chip_kernel(chips, planes, place, old, *refs):
+    ins, give, keep, both = refs[:chips], refs[-3], refs[-2], refs[-1]
+    hid = old.shape[1]
+    rows = planes * hid
     small = small_read(ins[0])
     for ref in ins[1:]:
         small = small + small_read(ref)
-    for k, out in enumerate(outs):
-        for which in range(2):
-            at = (which * len(outs) + k) * hid
+    for which in range(2):
+        for k in range(planes):
+            at = which * rows + k * hid
             total = ins[0][at : at + hid, :].astype(f32)
             for ref in ins[1:]:
                 total = total + ref[at : at + hid, :].astype(f32)
-            out[which * hid : (which + 1) * hid, :] = total.astype(bf16)
-        small_write(out, small)
-
-
-def plane_messages_kernel(chips, planes, place, *refs):
-    ffn, refs = refs[:planes], refs[planes:]
-    att, (ffn_old, att_old), refs = refs[:chips], refs[chips : chips + 2], refs[chips + 2 :]
-    outs, small_out, scratch = refs[:planes], refs[planes], refs[planes + 1]
-    rows = 2 * ffn_old.shape[1]
-    span = att_old.shape[1]
-    small = small_read(ffn[0])
-    total = ffn_old[...].reshape(rows, D) + ffn[0][:rows, :].astype(f32)
-    for ref in ffn[1:]:
-        small = small + small_read(ref)
-        total = total + ref[:rows, :].astype(f32)
-    small_out[...] = small
-    total = total.astype(bf16)
+            if k == 0:
+                total = total + old[which]
+            both[which, k * hid : (k + 1) * hid, :] = total.astype(bf16)
+    mine = place[0] // (planes // 2)
+    keep[:rows, :] = both[mine]
+    give[:rows, :] = both[1 - mine]
+    small_write(keep, small)
+    small_write(give, small)
+
+
+def plane_sum_kernel(mask, planes, place, keep, got, out):
+    rows = keep.shape[0] - 16
+    hid = rows // planes
+    for k in range(planes):
+        at, by = k * hid, (k ^ mask) * hid
+        total = keep[at : at + hid, :].astype(f32) + got[by : by + hid, :].astype(f32)
+        out[at : at + hid, :] = total.astype(bf16)
+    small_write(out, small_read(keep) + small_read(got))
+
+
+def att_to_owner_kernel(chips, planes, place, *refs):
+    ins, old, outs, scratch = refs[:chips], refs[chips], refs[chips + 1 : -1], refs[-1]
+    span = old.shape[1]
     for k in range(planes):
         for which in range(4):
             at = (k * 4 + which) * span
-            one = att[0][at : at + span, :].astype(f32)
-            for ref in att[1:]:
-                one = one + ref[at : at + span, :].astype(f32)
+            total = ins[0][at : at + span, :].astype(f32)
+            for ref in ins[1:]:
+                total = total + ref[at : at + span, :].astype(f32)
             if k == 0:
-                one = one + att_old[which]
-            scratch[which, k * span : (k + 1) * span, :] = one.astype(bf16)
+                total = total + old[which]
+            scratch[which, k * span : (k + 1) * span, :] = total.astype(bf16)
     for u, out in enumerate(outs):
-        out[:rows, :] = total
-        out[rows:, :] = scratch[place[0] ^ u]
-
-
-def plane_split_kernel(rows, place, *refs):
-    ins, out = refs[:-1], refs[-1]
-    planes = len(ins)
-    span = (ins[0].shape[0] - rows) // planes
-    for u, ref in enumerate(ins):
-        out[u * rows : (u + 1) * rows, :] = ref[:rows, :]
+        out[...] = scratch[place[0] ^ u]
+
+
+def near_sum_kernel(planes, place, keep, got, *refs):
+    ins, (out, small_out) = refs[:planes], refs[planes:]
+    rows = keep.shape[0] - 16
+    hid = rows // planes
+    span = ins[0].shape[0] // planes
     for k in range(planes):
+        at, by = k * hid, (k ^ 1) * hid
+        total = keep[at : at + hid, :].astype(f32) + got[by : by + hid, :].astype(f32)
+        out[at : at + hid, :] = total.astype(bf16)
         total = jnp.zeros((span, D), f32)
         for u, ref in enumerate(ins):
-            at = rows + (k ^ u) * span
+            at = (k ^ u) * span
             total = total + ref[at : at + span, :].astype(f32)
-        at = planes * rows + k * span
-        out[at : at + span, :] = total.astype(bf16)
-
-
-def newton_kernel(planes, spots, first_only, place, *refs):
-    x_ref, low_ref = refs[-2:]
+        out[rows + k * span : rows + (k + 1) * span, :] = total.astype(bf16)
+    small_out[...] = small_read(keep) + small_read(got)
+
+
+def newton_kernel(planes, chips, base_row, groups, with_rows, place, own, other, *refs):
+    outs, x_ref, low_ref = refs[:-2], refs[-2], refs[-1]
     dim, cols = x_ref.shape
-    span = cols // (planes * spots)
-    group = spots * span
-    if first_only:
-        chips = spots // 2
-        got, outs = refs[chips], refs[chips + 1 : -2]
-        tall = (planes + 1) * span
-        halves = []
-        for m in range(chips):
-            halves += [refs[m], got.at[m * tall : m * tall + planes * span, :]]
-    else:
-        outs = refs[2:-2]
-        halves = []
-        for at in range(spots):
-            from_at = refs[0].shape[0] - (spots // 2 - at // 2) * planes * span
-            halves.append(refs[at % 2].at[from_at : from_at + planes * span, :])
+    group = cols // planes
+    half_group = group // 2
+    span = half_group // chips
+    tall = own.shape[0] // chips
     chunk = 512
     total = jnp.zeros((1, D), f32)
-    for half in halves:
-        part = half[...].astype(f32)
-        total = total + jnp.sum(part * part, axis=0, keepdims=True)
+    for half in (own, other):
+        for m in range(chips):
+            at = m * tall + base_row
+            part = half[at : at + planes * span, :].astype(f32)
+            total = total + jnp.sum(part * part, axis=0, keepdims=True)
     inverse = 1.0 / (jnp.sqrt(jnp.sum(total, axis=1, keepdims=True)) + 1e-07)
     for k in range(planes):
-        rows = [half[k * span : (k + 1) * span, :] for half in halves]
+        rows = []
+        for half in (own, other):
+            for m in range(chips):
+                at = m * tall + base_row + k * span
+                rows.append(half[at : at + span, :])
         part = jnp.concatenate(rows, 0).astype(f32).T * inverse
         x_ref[:, k * group : (k + 1) * group] = part
         low_ref[:, k * group : (k + 1) * group] = part.astype(bf16)
@@ -1079,7 +1087,7 @@
         jnp.int32, (dim, dim), 1
     )
 
-    def step(limit):
+    def step(spans):
         gram = jnp.zeros((dim, dim), f32)
         for at in range(0, cols, chunk):
             part = low_ref[:, at : at + chunk]
@@ -1095,40 +1103,51 @@
         )
         poly = poly.astype(bf16)
         scale = newton_one + newton_two * shift + newton_three * shift * shift
-        for at in range(0, limit, chunk):
-            part = scale * x_ref[:, at : at + chunk] + mm(poly, low_ref[:, at : at + chunk], nn)
-            x_ref[:, at : at + chunk] = part
-            low_ref[:, at : at + chunk] = part.astype(bf16)
-
-    @pl.loop(0, 4)
-    def _(_):
-        step(cols)
-
-    step(group if first_only else cols)
-    for k, out in enumerate(outs):
+        for part in spans:
+            new = scale * x_ref[:, part] + mm(poly, low_ref[:, part], nn)
+            x_ref[:, part] = new
+            low_ref[:, part] = new.astype(bf16)
+
+    everything = [slice(at, at + chunk) for at in range(0, cols, chunk)]
+    for _ in range(4):
+        step(everything)
+    if with_rows:
+        step(everything)
+    else:
+        step([slice(k * group, k * group + half_group) for k in groups])
+    for k, out in zip(groups, outs):
         part = x_ref[:, k * group : (k + 1) * group].T.astype(bf16)
-        if first_only:
-            for at in range(spots):
-                to = pl.multiple_of((place[1] ^ at) * span, span)
-                out[pl.ds(to, span), :] = part[at * span : (at + 1) * span, :]
-            continue
-        for at in range(0, spots, 2):
-            to = pl.multiple_of((place[1] // 2 ^ at // 2) * span, span)
-            out[pl.ds(to, span), :] = halves[at][k * span : (k + 1) * span, :]
-            to = pl.multiple_of((place[1] // 2 ^ at // 2) * span + group // 2, span)
-            out[pl.ds(to, span), :] = part[at * span : (at + 1) * span, :]
-
-
-def newton(place, halves, planes, spots, cols, first_only, name):
+        base = half_group if with_rows else 0
+        for m in range(chips):
+            chip = place[1] // 2 ^ m
+            if with_rows:
+                at = m * tall + base_row + k * span
+                out[pl.ds(pl.multiple_of(chip * span, span), span), :] = own[at : at + span, :]
+            to = pl.multiple_of(base + chip * span, span)
+            out[pl.ds(to, span), :] = part[m * span : (m + 1) * span, :]
+
+
+def newton(place, own, other, planes, base_row, cols, groups, with_rows, name):
+    rows = cols // planes // 2 * (2 if with_rows else 1)
     return run(
-        functools.partial(newton_kernel, planes, spots, first_only),
-        place,
-        halves,
-        [like((cols // planes, D), bf16)] * (1 if first_only else planes),
+        functools.partial(
+            newton_kernel, planes, lax.axis_size("dp") // 2, base_row, groups, with_rows
+        ),
+        place,
+        [own, other],
+        [like((rows, D), bf16)] * len(groups),
         name,
         scratch=[pltpu.VMEM((D, cols), f32), pltpu.VMEM((D, cols), bf16)],
         flops=10 * D * D * (2 * cols + D),
     )
+
+
+def momentum_rows_kernel(planes, chips, group, place, own, out):
+    span = out.shape[0] // chips
+    for m in range(chips):
+        to = pl.multiple_of((place[1] // 2 ^ m) * span, span)
+        at = m * (own.shape[0] // chips) + group * span
+        out[pl.ds(to, span), :] = own[at : at + span, :]
 
 
 def att_final_kernel(planes, span, place, mine, got, *refs):
@@ -1154,72 +1173,48 @@
                 outs[4 + which][...] = old[which][...] - muon_rates[which] * part
 
 
-def ffn_give_kernel(planes, hid, span, place, *refs):
-    count = len(refs) // 2
-    ins, give, keep = refs[:count], refs[count], refs[count + 1 :]
-    tall = (planes + 1) * hid
-    wide = planes * span
-
-    for m in range(count):
-        at, to = 2 * planes * hid, count * tall + m * wide
-        give[to : to + wide, :] = ins[m][at : at + wide, :]
-
-    def fill(given):
-        for m in range(count):
-            for k in range(planes):
-                to = slice(m * tall + k * hid, m * tall + (k + 1) * hid)
-                at = (2 * k + given) * hid
-                give[to, :] = ins[m][at : at + hid, :]
-                to = slice(k * hid, (k + 1) * hid)
-                at = (2 * k + 1 - given) * hid
-                keep[m][to, :] = ins[m][at : at + hid, :]
-            give[m * tall + planes * hid : (m + 1) * tall, :] = keep[m][:hid, :]
-
-    @pl.when(place[1] % 2 == 0)
-    def _():
-        fill(0)
-
-    @pl.when(place[1] % 2 == 1)
-    def _():
-        fill(1)
-
-
-def ffn_buffers_kernel(chips, hid, place, give, got, *refs):
-    keep, (eo, co) = refs[:chips], refs[chips:]
-    tall = keep[0].shape[0] + hid
-    tail = tall - hid
-
-    def fill(kept, given):
+def ffn_buffers_kernel(planes, chips, place, own, other, far, far_got, eo, co):
+    span = far.shape[0] // chips
+    core = place[1] % 2
+
+    def fill(mine_out, far_out):
         for m in range(chips):
-            one = pl.multiple_of((place[1] ^ (2 * m)) * hid, hid)
-            two = pl.multiple_of((place[1] ^ (2 * m + 1)) * hid, hid)
-            at = m * tall
-            kept[pl.ds(one, hid), :] = keep[m][:hid, :].astype(f32)
-            kept[pl.ds(two, hid), :] = got[at : at + hid, :].astype(f32)
-            given[pl.ds(one, hid), :] = give[at : at + hid, :].astype(f32)
-            given[pl.ds(two, hid), :] = got[at + tail : at + tall, :].astype(f32)
-
-    @pl.when(place[1] % 2 == 0)
-    def _():
-        fill(eo, co)
-
-    @pl.when(place[1] % 2 == 1)
-    def _():
-        fill(co, eo)
-
-
-def ffn_final_kernel(place, mine, got, we, wc, eo, co):
-    def fill(e, c):
-        eo[...] = we[...] - muon_rates[4] * e[...].astype(f32)
-        co[...] = wc[...] - muon_rates[5] * c[...].astype(f32)
-
-    @pl.when(place[1] % 2 == 0)
-    def _():
-        fill(mine, got)
-
-    @pl.when(place[1] % 2 == 1)
-    def _():
-        fill(got, mine)
+            chip = place[1] // 2 ^ m
+            here = pl.multiple_of((2 * chip + core) * span, span)
+            there = pl.multiple_of((2 * chip + 1 - core) * span, span)
+            at = m * (own.shape[0] // chips)
+            mine_out[pl.ds(here, span), :] = own[at : at + span, :].astype(f32)
+            mine_out[pl.ds(there, span), :] = other[at : at + span, :].astype(f32)
+            at = m * span
+            here = pl.multiple_of((2 * m + core) * span, span)
+            there = pl.multiple_of((2 * m + 1 - core) * span, span)
+            far_out[pl.ds(here, span), :] = far[at : at + span, :].astype(f32)
+            far_out[pl.ds(there, span), :] = got[at : at + span, :].astype(f32)
+
+    got = far_got
+    pl.when(place[0] < planes // 2)(lambda: fill(co, eo))
+    pl.when(place[0] >= planes // 2)(lambda: fill(eo, co))
+
+
+def ffn_final_kernel(planes, chips, place, mine, far, got, we, wc, eo, co):
+    rows = mine.shape[0]
+    span = rows // chips
+    core = place[1] % 2
+
+    def fill(mine_out, mine_w, mine_rate, far_out, far_w, far_rate):
+        for m in range(chips):
+            at = slice(m * span, (m + 1) * span)
+            far_at = slice(rows + m * span, rows + (m + 1) * span)
+            here = pl.ds(pl.multiple_of((2 * m + core) * span, span), span)
+            there = pl.ds(pl.multiple_of((2 * m + 1 - core) * span, span), span)
+            mine_out[here, :] = mine_w[here, :] - mine_rate * mine[at, :].astype(f32)
+            mine_out[there, :] = mine_w[there, :] - mine_rate * got[at, :].astype(f32)
+            far_out[here, :] = far_w[here, :] - far_rate * far[at, :].astype(f32)
+            far_out[there, :] = far_w[there, :] - far_rate * got[far_at, :].astype(f32)
+
+    expand, contract = (eo, we, muon_rates[4]), (co, wc, muon_rates[5])
+    pl.when(place[0] < planes // 2)(lambda: fill(*contract, *expand))
+    pl.when(place[0] >= planes // 2)(lambda: fill(*expand, *contract))
 
 
 def shards(
@@ -1308,12 +1303,22 @@
     qkv_own, rest_own, last, start, bias = together(
         qkv_own, rest_own, last, start, bias
     )
-    qkv_halves = interleave(qkv_own, [swap(part, "dp", 1) for part in qkv_own])
-    rest_own = around_chips(jnp.stack(rest_own))
+    qkv_own = jnp.stack(qkv_own)
+    qkv_halves = [qkv_own, swap(qkv_own, "dp", 1)]
+    rest_own, ups = together(jnp.stack(rest_own), ups)
+    rest_own = around_chips(rest_own)
     ups = [ups[0]] + [swap(ups[u], "mp", u) for u in to_planes]
     qkv, heads = attention(place, last, inputs, qkv_halves)
-    heads, rest_own, ups = together(heads, rest_own, ups)
+    heads, rest_own, ups, buffers_old = together(heads, rest_own, ups, buffers_old)
     rest_halves = interleave(rest_own, [swap(part, "dp", 1) for part in rest_own])
+    att_old, ffn_old = pieces(
+        buffer_pieces_kernel,
+        place,
+        buffers_old,
+        [like((4, span, D), f32), like((2, hid, D), f32)],
+        "buffer_pieces",
+    )
+    rest_halves, att_old, ffn_old = together(rest_halves, att_old, ffn_old)
     lays, rest = feed_forward(place, alphas, inputs, heads, ups, rest_halves, bias, bout)
     ffn_keep, ffn_give, grad_output, heads_grad, middle_grad, gb_in, gb_out, g_alpha = rest
 
@@ -1335,7 +1340,7 @@
         [like((2 * planes * hid + 16, D), bf16)] * chips,
         "ffn_core_sum",
     )
-    middle_grad, parts, lays = together(middle_grad, parts, lays)
+    middle_grad, parts = together(middle_grad, parts)
     got = [parts[0]] + [swap(parts[m], "dp", 2 * m) for m in to_chips]
     lay_far = [swap(lays[u], "mp", u) for u in to_planes[1:]]
     ins, att_keep, att_give = attention_back(
@@ -1344,24 +1349,21 @@
     )
     ins, att_keep, att_give, got, lay_far = together(ins, att_keep, att_give, got, lay_far)
 
-    parts = run(
-        functools.partial(ffn_chip_kernel, chips, hid),
-        place,
-        got,
-        [like((2 * hid + 16, D), bf16)] * planes,
+    far = planes // 2
+    parts = got
+    rows = planes * hid
+    give, keep = run(
+        functools.partial(ffn_chip_kernel, chips, planes),
+        place,
+        [ffn_old, *parts],
+        [like((rows + 16, D), bf16)] * 2,
         "ffn_chip_sum",
-    )
-    parts, att_give, buffers_old = together(parts, att_give, buffers_old)
-    got = [parts[0]] + [swap(parts[k], "mp", k) for k in to_planes]
+        scratch=[pltpu.VMEM((2, rows, D), bf16)],
+    )
+    give, att_give, lays = together(give, att_give, lays)
+    got = swap(give, "mp", far)
+    lay_near = swap(lays[1], "mp", 1)
     att_got = swap(att_give, "dp", 1)
-    att_old, ffn_old = pieces(
-        buffer_pieces_kernel,
-        place,
-        buffers_old,
-        [like((4, span, D), f32), like((2, hid, D), f32)],
-        "buffer_pieces",
-    )
-
     att_parts = run(
         att_core_kernel,
         place,
@@ -1370,76 +1372,94 @@
         "att_core_sum",
     )
     att_got = [att_parts[0]] + [swap(att_parts[m], "dp", 2 * m) for m in to_chips]
-    outs = run(
-        functools.partial(plane_messages_kernel, chips, planes),
-        place,
-        [*got, *att_got, ffn_old, att_old],
-        [like((2 * hid + planes * span, D), bf16)] * planes + [like((8, D), f32)],
-        "plane_messages",
+    got, att_got, lay_near = together(got, att_got, lay_near)
+    half_sum = run(
+        functools.partial(plane_sum_kernel, far, planes),
+        place,
+        [keep, got],
+        [like((rows + 16, D), bf16)],
+        "ffn_far_sum",
+    )[0]
+    got = swap(half_sum, "mp", 1)
+    att_parts = run(
+        functools.partial(att_to_owner_kernel, chips, planes),
+        place,
+        att_got + [att_old],
+        [like((planes * span, D), bf16)] * planes,
+        "att_chip_sum",
         scratch=[pltpu.VMEM((4, planes * span, D), bf16)],
     )
-    small_grad = outs[-1].reshape(-1)[: FF + D + 2]
-    got = [outs[0]] + [swap(outs[k], "mp", k) for k in to_planes]
-    message = run(
-        functools.partial(plane_split_kernel, 2 * hid),
-        place,
-        got,
-        [like((planes * (2 * hid + span), D), bf16)],
-        "plane_split",
-    )[0]
+    att_got = [att_parts[0]] + [swap(att_parts[u], "mp", u) for u in to_planes]
+    message, small_grad = run(
+        functools.partial(near_sum_kernel, planes),
+        place,
+        [half_sum, got, *att_got],
+        [like((rows + planes * span, D), bf16), like((8, D), f32)],
+        "near_sum",
+    )
+    small_grad = small_grad.reshape(-1)[: FF + D + 2]
     message, ins = together(message, ins)
     got = around_chips(message)
-    near = swap(jnp.concatenate([ins[1], lays[1]]), "mp", 1)
-    in_far = [swap(ins[u], "mp", u) for u in to_planes[1:]]
-    in_grad = join_positions([ins[0], near[:token_span], *in_far], place)
-    layer_out = join_positions([lays[0], near[token_span:], *lay_far], place)
-    got, in_grad, layer_out = together(got, in_grad, layer_out)
-    outs = run(
-        functools.partial(ffn_give_kernel, planes, hid, span),
-        place,
-        got,
-        [like((chips * ((planes + 1) * hid + planes * span), D), bf16)]
-        + [like((planes * hid, D), bf16)] * chips,
-        "ffn_give",
-    )
-    give, keep = outs[0], outs[1:]
-    ffn_got = swap(give, "dp", 1)
-    att_x = newton(place, [give, ffn_got], planes, spots, D, False, "newton_att")
-    att_x = jnp.stack([att_x[0]] + [swap(att_x[u], "mp", u) for u in to_planes])
-    step = newton(
-        place, [*keep, ffn_got], planes, spots, planes * hidden_rows, True, "newton_ffn"
-    )[0]
-    step, give, keep, ffn_got, att_x = together(step, give, keep, ffn_got, att_x)
-    step_got = swap(step, "dp", 1)
-    att_other = swap(att_x, "dp", 1)
-    new_be, new_bc = run(
-        functools.partial(ffn_buffers_kernel, chips, hid),
-        place,
-        [give, ffn_got, *keep],
-        [like((hidden_rows, D), f32)] * 2,
-        "ffn_buffers",
-    )
-    att_out = run(
-        functools.partial(att_final_kernel, planes, span),
-        place,
-        [att_x, att_other, *weights_old[:4]],
-        [like(w.shape, f32) for w in weights_old[:4]] * 2,
-        "att_final",
-        scratch=[pltpu.VMEM((head_cols, D), bf16)],
-    )
-    new_we, new_wc = run(
-        ffn_final_kernel,
-        place,
-        [step, step_got, w_expand, w_contract],
-        [like((hidden_rows, D), f32)] * 2,
-        "ffn_final",
-    )
-
+    in_got = [ins[0], None, swap(ins[2], "mp", 2), None]
     first_new = 0.5 * small_first + 0.5 * small_grad
     second_new = 0.5 * small_second + 0.5 * small_grad * small_grad
     correction = 1.0 - 0.5**STEP
     small_new = small_params - adam_rate * (first_new / correction) / (
         jnp.sqrt(second_new / correction) + 1e-08
+    )
+    smalls = (small_new, first_new, second_new)
+    got, smalls, in_got, ins = together(got, smalls, in_got, ins)
+    in_got[3] = swap(ins[3], "mp", 3)
+    in_got[1] = swap(ins[1], "mp", 1)
+    own = jnp.concatenate(got)
+    other = swap(own, "dp", 1)
+    far_m = run(
+        functools.partial(momentum_rows_kernel, planes, chips, far),
+        place,
+        [own],
+        [like((hidden_rows // 2, D), bf16)],
+        "momentum_rows",
+    )[0]
+    far_m = swap(far_m, "mp", far)
+    att_x = newton(
+        place, own, other, planes, rows, D, tuple(range(planes)), True, "newton_att"
+    )
+    att_x, in_got, other = together(att_x, in_got, other)
+    att_x = jnp.stack([att_x[0]] + [swap(att_x[u], "mp", u) for u in to_planes])
+    step, far_step = newton(
+        place, own, other, planes, 0, planes * hidden_rows, (0, far), False, "newton_ffn"
+    )
+    step, att_x = together(step, att_x)
+    far_step = swap(far_step, "mp", far)
+    far_m_got = swap(far_m, "dp", 1)
+    att_other = swap(att_x, "dp", 1)
+    new_be, new_bc = run(
+        functools.partial(ffn_buffers_kernel, planes, chips),
+        place,
+        [own, other, far_m, far_m_got],
+        [like((hidden_rows, D), f32)] * 2,
+        "ffn_buffers",
+    )
+    layer_out = join_positions([lays[0], lay_near, *lay_far], place)
+    in_grad = join_positions(in_got, place)
+    att_out = run(
+        functools.partial(att_final_kernel, planes, span),
+        place,
+        [att_x, att_other, *weights_old[:4]],
+        [like(w.shape, f32) for w in weights_old[:4]] * 2,
+        "att_final",
+        scratch=[pltpu.VMEM((head_cols, D), bf16)],
+    )
+    far_step, new_be, layer_out, in_grad, att_out = together(
+        far_step, new_be, layer_out, in_grad, att_out
+    )
+    got = swap(jnp.concatenate([step, far_step]), "dp", 1)
+    new_we, new_wc = run(
+        functools.partial(ffn_final_kernel, planes, chips),
+        place,
+        [step, far_step, got, w_expand, w_contract],
+        [like((hidden_rows, D), f32)] * 2,
+        "ffn_final",
     )
     return (
         (layer_out, in_grad)
@@ -1447,7 +1467,7 @@
         + (new_be, new_bc)
         + tuple(att_out[4:])
         + (new_we, new_wc)
-        + (small_new, first_new, second_new)
+        + smalls
     )
 
 

time: 254 us -> 250 us (0.984); the launches traced: 254 us -> 247 us
  waiting for transfers between devices: 59.1 us -> 53.1 us
    ppermute x52, waiting for transfers between devices: 59.1 us -> 53.1 us  [swap(): return lax.ppermute(x, axis, [(a, a ^ mask) for a in range(size)])]
    pallas_call x19 -> x20, Pallas kernels: 116 us -> 116 us  [run(): pl.pallas_call(kernel, grid_spec=pltpu.PrefetchScalarGridSpec(num_scalar_...]
  transfers between devices with their start and end apart: 52 -> 52, of which waited for: 20 -> 17; matrix products, arithmetic and copies ran while one was open for 3% -> 3% of each run, Pallas kernels for 28% -> 33%
where the time goes in v4:
time: 250 us; the launch traced here: 247 us
  Pallas kernels  116 us (46%)
  starting transfers between devices  64.4 us (26%)
  waiting for transfers between devices  53.1 us (21%)
  local copies, waits for them, and re-layouts  6.45 us (3%)
  other arithmetic  5.67 us (2%)
    pallas_call x20, Pallas kernels, run(): pl.pallas_call(kernel, grid_spec=pltpu.PrefetchScalarGridSpec(num_scalar_...  116 us
    ppermute x52, starting transfers between devices, swap(): return lax.ppermute(x, axis, [(a, a ^ mask) for a in range(size)])  64.4 us
    ppermute x52, waiting for transfers between devices, swap(): return lax.ppermute(x, axis, [(a, a ^ mask) for a in range(size)])  53.1 us
  transfers between devices with their start and end apart: 52, of which 17 were waited for; matrix products, arithmetic and copies ran while one was open for 3% of the time, Pallas kernels for 33%

profile of v4, /device:TPU:0, one launch (start us, length us, event | category | flops | bytes accessed | tf_op | source)
XLA Modules:
  0.0 246.9 jit_solution(902475915736392222)
XLA Ops:
  1.3 2.9 %weight_pieces.1 = (bf16[48,512]{1,0:T(8,128)(2,1)}, bf16[144,512]{1,0:T(8,128)(2,1)}) custom-call(s32[2]{0:T(128)} %pad_add_fusion.place, f32[512,128]{1,0:T(8,128)} %refs_0_.3, f32[512,128]{1,0:T(8,128)} %refs_1_.5, f32[512,128]{1,0:T(8,128)} %refs_2_.3, f32[128,512]{1,0:T(8,128)} %refs_3_.3, f32[512,512]{1,0:T(8,128)} %we.1, f32[512,512]{1,0:T(8,128)} %wc.1), custom_call_target="tpu_custom_call" | custom-call | tf_op jit(solution)/shard_map/weight_pieces/pallas_call | solution.py:414
  4.2 5.0 %collective-permute-start.2 = (bf16[48,512]{1,0:T(8,128)(2,1)}, bf16[48,512]{1,0:T(8,128)(2,1)S(1)}, u32[]{:S(2)}, u32[]{:S(2)}) collective-permute-start(bf16[48,512]{1,0:T(8,128)(2,1)} %get-tuple-element.199), channel_id=1, source_target_pairs={{0,3},{1,2},{2,1},{3,0},{4,7},{5,6},{6,5},{7,4},{8,11},{9,10},{10,... | collective-permute-start | bytes 147464 | tf_op jit(solution)/shard_map/ppermute | solution.py:386
  9.8 3.8 %collective-permute-start.8 = (bf16[144,512]{1,0:T(8,128)(2,1)}, bf16[144,512]{1,0:T(8,128)(2,1)S(1)}, u32[]{:S(2)}, u32[]{:S(2)}) collective-permute-start(bf16[144,512]{1,0:T(8,128)(2,1)} %get-tuple-element.210), channel_id=1, source_target_pairs={{0,3},{1,2},{2,1},{3,0},{4,7},{5,6},{6,5},{7,4},{8,11},{9,10},{10,... | collective-permute-start | bytes 442376 | tf_op jit(solution)/shard_map/ppermute | solution.py:386
  17.2 3.4 %collective-permute-done.1 = bf16[48,512]{1,0:T(8,128)(2,1)S(1)} collective-permute-done((bf16[48,512]{1,0:T(8,128)(2,1)}, bf16[48,512]{1,0:T(8,128)(2,1)S(1)}, u32[]{:S(2)}, u32[]{:S(2)}) %collective-permute-start.1) | collective-permute-done | bytes 49184 | tf_op jit(solution)/shard_map/ppermute | solution.py:386
  20.6 2.5 %collective-permute-start.5 = (bf16[4,48,512]{2,1,0:T(8,128)(2,1)S(1)}, bf16[4,48,512]{2,1,0:T(8,128)(2,1)S(1)}, u32[]{:S(2)}, u32[]{:S(2)}) collective-permute-start(bf16[4,48,512]{2,1,0:T(8,128)(2,1)S(1)} %pad_maximum_fusion.4), channel_id=1, source_target_pairs={{0,24},{4,28},{8,16},{12,20},{16,8},{20,12},{24,0},{28,4},{1,25},{... | collective-permute-start | bytes 589832 | tf_op jit(solution)/shard_map/ppermute | solution.py:386
  31.1 2.5 collective-permute-start.12
  34.6 3.9 %collective-permute-done.13.refs_4_ = bf16[256,512]{1,0:T(8,128)(2,1)S(1)} collective-permute-done((bf16[256,512]{1,0:T(8,128)(2,1)S(1)}, bf16[256,512]{1,0:T(8,128)(2,1)S(1)}, u32[]{:S(2)}, u32[]{:S(2)}) %collective-permute-start.13) | collective-permute-done | bytes 262176 | tf_op jit(solution)/shard_map/ppermute | solution.py:386
  42.2 18.1 %attention_forward.1 = (bf16[4,4,1024,128]{3,2,1,0:T(8,128)(2,1)}, bf16[1024,512]{1,0:T(8,128)(2,1)}) custom-call(s32[2]{0:T(128)} %pad_add_fusion.place, s32[1,1024]{1,0:T(1,128)} %bitcast.56, bf16[4,1024,512]{2,1,0:T(8,128)(2,1)} %in_hbm.1, bf16[4,4,48,512]{3,2,1,0:T(8,128)(2,1)} %copy-done.19, bf16[4,4,48,512]{3,2,1,0:T(8,128)(2,1)} %copy-done.27), custom_call_target="tpu_custom_call" | custom-call | flops 5368709120 | bytes 11014144 | tf_op jit(solution)/shard_map/attention_forward/pallas_call | solution.py:414
  63.3 2.8 %buffer_pieces.1 = (f32[4,16,512]{2,1,0:T(8,128)}, f32[2,64,512]{2,1,0:T(8,128)}) custom-call(s32[2]{0:T(128)} %pad_add_fusion.place, f32[512,128]{1,0:T(8,128)} %q.2, f32[512,128]{1,0:T(8,128)} %k.2, f32[512,128]{1,0:T(8,128)} %v.2, f32[128,512]{1,0:T(8,128)} %o.2, f32[512,512]{1,0:T(8,128)} %e.2, f32[512,512]{1,0:T(8,128)} %c.2), custom_call_target="tpu_custom_call" | custom-call | tf_op jit(solution)/shard_map/buffer_pieces/pallas_call | solution.py:414
  67.4 28.0 %feed_forward.1 = (bf16[256,512]{1,0:T(8,128)(2,1)}, bf16[256,512]{1,0:T(8,128)(2,1)}, bf16[256,512]{1,0:T(8,128)(2,1)}, bf16[256,512]{1,0:T(8,128)(2,1)}, bf16[...) custom-call(s32[2]{0:T(128)} %pad_add_fusion.place, ...), custom_call_target="tpu_custom_call" | custom-call | flops 12884901888 | bytes 19947528 | tf_op jit(solution)/shard_map/feed_forward/pallas_call | solution.py:414
  98.5 4.9 %collective-permute-start.25 = (bf16[256,512]{1,0:T(8,128)(2,1)}, bf16[256,512]{1,0:T(8,128)(2,1)S(1)}, u32[]{:S(2)}, u32[]{:S(2)}) collective-permute-start(bf16[256,512]{1,0:T(8,128)(2,1)} %get-tuple-element.275), channel_id=1, source_target_pairs={{0,2},{1,3},{2,0},{3,1},{4,6},{5,7},{6,4},{7,5},{8,10},{9,11},{10,... | collective-permute-start | bytes 786440 | tf_op jit(solution)/shard_map/ppermute | solution.py:386
  111.5 26.5 %attention_backward.1 = (bf16[256,512]{1,0:T(8,128)(2,1)}, bf16[256,512]{1,0:T(8,128)(2,1)}, bf16[256,512]{1,0:T(8,128)(2,1)}, bf16[256,512]{1,0:T(8,128)(2,1)},...) custom-call(s32[2]{0:T(128)} %pad_add_fusion.place, s32[1,1024]{1,0:T(1,128)} %bitcast.61, ...), custom_call_target="tpu_custom_call" | custom-call | flops 11274289152 | bytes 17829888 | tf_op jit(solution)/shard_map/attention_backward/pallas_call | solution.py:414
  139.4 2.4 collective-permute-start.32
  146.3 5.5 %collective-permute-done.32.refs_1_ = bf16[256,512]{1,0:T(8,128)(2,1)S(1)} collective-permute-done((bf16[256,512]{1,0:T(8,128)(2,1)S(1)}, bf16[256,512]{1,0:T(8,128)(2,1)S(1)}, u32[]{:S(2)}, u32[]{:S(2)}) %collective-permute-start.32) | collective-permute-done | bytes 262176 | tf_op jit(solution)/shard_map/ppermute | solution.py:386
  151.8 2.7 %collective-permute-done.27.got = bf16[272,512]{1,0:T(8,128)(2,1)S(1)} collective-permute-done((bf16[272,512]{1,0:T(8,128)(2,1)S(1)}, bf16[272,512]{1,0:T(8,128)(2,1)S(1)}, u32[]{:S(2)}, u32[]{:S(2)}) %collective-permute-start.27) | collective-permute-done | bytes 278560 | tf_op jit(solution)/shard_map/ppermute | solution.py:386
  154.5 3.5 %collective-permute-done.30.refs_2_ = bf16[256,512]{1,0:T(8,128)(2,1)S(1)} collective-permute-done((bf16[256,512]{1,0:T(8,128)(2,1)S(1)}, bf16[256,512]{1,0:T(8,128)(2,1)S(1)}, u32[]{:S(2)}, u32[]{:S(2)}) %collective-permute-start.30) | collective-permute-done | bytes 262176 | tf_op jit(solution)/shard_map/ppermute | solution.py:386
  164.0 5.8 %collective-permute-done.34.refs_1_ = bf16[64,512]{1,0:T(8,128)(2,1)S(1)} collective-permute-done((bf16[64,512]{1,0:T(8,128)(2,1)S(1)}, bf16[64,512]{1,0:T(8,128)(2,1)S(1)}, u32[]{:S(2)}, u32[]{:S(2)}) %collective-permute-start.34) | collective-permute-done | bytes 65568 | tf_op jit(solution)/shard_map/ppermute | solution.py:386
  175.8 10.3 %collective-permute-done.40.refs_2_ = bf16[256,512]{1,0:T(8,128)(2,1)S(1)} collective-permute-done((bf16[256,512]{1,0:T(8,128)(2,1)S(1)}, bf16[256,512]{1,0:T(8,128)(2,1)S(1)}, u32[]{:S(2)}, u32[]{:S(2)}) %collective-permute-start.40) | collective-permute-done | bytes 262176 | tf_op jit(solution)/shard_map/ppermute | solution.py:386
  191.6 6.9 %newton_att.1 = (bf16[128,512]{1,0:T(8,128)(2,1)S(1)}, bf16[128,512]{1,0:T(8,128)(2,1)S(1)}, bf16[128,512]{1,0:T(8,128)(2,1)S(1)}, bf16[128,512]{1,0:T(8,128)(2,1)S(1)}) custom-call(s32[2]{0:T(128)S(1)} %copy-done.17, bf16[1280,512]{1,0:T(8,128)(2,1)S(1)} %constant_dynamic-update-slice_fusion.own, bf16[1280,512]{1,0:T(8,128)(2,1)S(1)} %collective-permute-done.41.other), custom_call_target="tpu_custom_call" | custom-call | flops 4026531840 | bytes 3145728 | tf_op jit(solution)/shard_map/newton_att/pallas_call | solution.py:414
  198.6 4.2 %collective-permute-done.43.refs_3_ = bf16[256,512]{1,0:T(8,128)(2,1)S(1)} collective-permute-done((bf16[256,512]{1,0:T(8,128)(2,1)S(1)}, bf16[256,512]{1,0:T(8,128)(2,1)S(1)}, u32[]{:S(2)}, u32[]{:S(2)}) %collective-permute-start.43) | collective-permute-done | bytes 262176 | tf_op jit(solution)/shard_map/ppermute | solution.py:386
  202.7 7.8 %collective-permute-start.47 = (bf16[128,512]{1,0:T(8,128)(2,1)S(1)}, bf16[128,512]{1,0:T(8,128)(2,1)S(1)}, u32[]{:S(2)}, u32[]{:S(2)}) collective-permute-start(bf16[128,512]{1,0:T(8,128)(2,1)S(1)} %get-tuple-element.340), channel_id=1, source_target_pairs={{0,1},{1,0},{2,3},{3,2},{4,5},{5,4},{6,7},{7,6},{8,9},{9,8},{10,11... | collective-permute-start | bytes 393224 | tf_op jit(solution)/shard_map/ppermute | solution.py:386
  212.9 14.0 %newton_ffn.1 = (bf16[256,512]{1,0:T(8,128)(2,1)S(1)}, bf16[256,512]{1,0:T(8,128)(2,1)S(1)}) custom-call(s32[2]{0:T(128)S(1)} %copy-done.17, bf16[1280,512]{1,0:T(8,128)(2,1)S(1)} %constant_dynamic-update-slice_fusion.own, bf16[1280,512]{1,0:T(8,128)(2,1)S(1)} %collective-permute-done.41.other), custom_call_target="tpu_custom_call" | custom-call | flops 12079595520 | bytes 3145728 | tf_op jit(solution)/shard_map/newton_ffn/pallas_call | solution.py:414
  235.1 2.2 att_final.1
  237.4 5.1 %collective-permute-done.44.far = bf16[256,512]{1,0:T(8,128)(2,1)S(1)} collective-permute-done((bf16[256,512]{1,0:T(8,128)(2,1)S(1)}, bf16[256,512]{1,0:T(8,128)(2,1)S(1)}, u32[]{:S(2)}, u32[]{:S(2)}) %collective-permute-start.44) | collective-permute-done | bytes 262176 | tf_op jit(solution)/shard_map/ppermute | solution.py:386
  (218 shorter events, 70.3 us)
Async XLA Ops:
  9.8 13.8 %collective-permute-start.8 = (bf16[144,512]{1,0:T(8,128)(2,1)}, bf16[144,512]{1,0:T(8,128)(2,1)S(1)}, u32[]{:S(2)}, u32[]{:S(2)}) collective-permute-start(bf16[144,512]{1,0:T(8,128)(2,1)} %get-tuple-element.210), channel_id=1, source_target_pairs={{0,3},{1,2},{2,1},{3,0},{4,7},{5,6},{6,5},{7,4},{8,11},{9,10},{10,... | collective-permute-start | bytes 442376 | tf_op jit(solution)/shard_map/ppermute | solution.py:386
  13.6 13.1 %collective-permute-start.7 = (bf16[144,512]{1,0:T(8,128)(2,1)}, bf16[144,512]{1,0:T(8,128)(2,1)S(1)}, u32[]{:S(2)}, u32[]{:S(2)}) collective-permute-start(bf16[144,512]{1,0:T(8,128)(2,1)} %get-tuple-element.210), channel_id=1, source_target_pairs={{0,2},{1,3},{2,0},{3,1},{4,6},{5,7},{6,4},{7,5},{8,10},{9,11},{10,... | collective-permute-start | bytes 442376 | tf_op jit(solution)/shard_map/ppermute | solution.py:386
  31.1 29.3 %collective-permute-start.12 = (bf16[4,144,512]{2,1,0:T(8,128)(2,1)S(1)}, bf16[4,144,512]{2,1,0:T(8,128)(2,1)}, u32[]{:S(2)}, u32[]{:S(2)}) collective-permute-start(bf16[4,144,512]{2,1,0:T(8,128)(2,1)S(1)} %pad_maximum_fusion.1.refs_7_), channel_id=1, source_target_pairs={{0,24},{4,28},{8,16},{12,20},{16,8},{20,12},{24,0},{28,4},{1,25},{... | collective-permute-start | bytes 1769480 | tf_op jit(solution)/shard_map/ppermute | solution.py:386
  33.6 26.8 %collective-permute-start.11 = (bf16[4,144,512]{2,1,0:T(8,128)(2,1)S(1)}, bf16[4,144,512]{2,1,0:T(8,128)(2,1)}, u32[]{:S(2)}, u32[]{:S(2)}) collective-permute-start(bf16[4,144,512]{2,1,0:T(8,128)(2,1)S(1)} %pad_maximum_fusion.1.refs_7_), channel_id=1, source_target_pairs={{0,16},{4,20},{8,24},{12,28},{16,0},{20,4},{24,8},{28,12},{1,17},{... | collective-permute-start | bytes 1769480 | tf_op jit(solution)/shard_map/ppermute | solution.py:386
  34.1 26.3 %collective-permute-start.10 = (bf16[4,144,512]{2,1,0:T(8,128)(2,1)S(1)}, bf16[4,144,512]{2,1,0:T(8,128)(2,1)}, u32[]{:S(2)}, u32[]{:S(2)}) collective-permute-start(bf16[4,144,512]{2,1,0:T(8,128)(2,1)S(1)} %pad_maximum_fusion.1.refs_7_), channel_id=1, source_target_pairs={{0,8},{4,12},{8,0},{12,4},{16,24},{20,28},{24,16},{28,20},{1,9},{5... | collective-permute-start | bytes 1769480 | tf_op jit(solution)/shard_map/ppermute | solution.py:386
  38.5 21.8 %collective-permute-start.14 = (bf16[256,512]{1,0:T(8,128)(2,1)S(1)}, bf16[256,512]{1,0:T(8,128)(2,1)S(1)}, u32[]{:S(2)}, u32[]{:S(2)}) collective-permute-start(bf16[256,512]{1,0:T(8,128)(2,1)S(1)} %get-tuple-element.221), channel_id=1, source_target_pairs={{0,2},{1,3},{2,0},{3,1},{4,6},{5,7},{6,4},{7,5},{8,10},{9,11},{10,... | collective-permute-start | bytes 786440 | tf_op jit(solution)/shard_map/ppermute | solution.py:386
  40.6 19.7 %collective-permute-start.15 = (bf16[256,512]{1,0:T(8,128)(2,1)S(1)}, bf16[256,512]{1,0:T(8,128)(2,1)S(1)}, u32[]{:S(2)}, u32[]{:S(2)}) collective-permute-start(bf16[256,512]{1,0:T(8,128)(2,1)S(1)} %get-tuple-element.222), channel_id=1, source_target_pairs={{0,3},{1,2},{2,1},{3,0},{4,7},{5,6},{6,5},{7,4},{8,11},{9,10},{10,... | collective-permute-start | bytes 786440 | tf_op jit(solution)/shard_map/ppermute | solution.py:386
  98.5 39.6 %collective-permute-start.25 = (bf16[256,512]{1,0:T(8,128)(2,1)}, bf16[256,512]{1,0:T(8,128)(2,1)S(1)}, u32[]{:S(2)}, u32[]{:S(2)}) collective-permute-start(bf16[256,512]{1,0:T(8,128)(2,1)} %get-tuple-element.275), channel_id=1, source_target_pairs={{0,2},{1,3},{2,0},{3,1},{4,6},{5,7},{6,4},{7,5},{8,10},{9,11},{10,... | collective-permute-start | bytes 786440 | tf_op jit(solution)/shard_map/ppermute | solution.py:386
  103.4 34.7 %collective-permute-start.26 = (bf16[256,512]{1,0:T(8,128)(2,1)}, bf16[256,512]{1,0:T(8,128)(2,1)S(1)}, u32[]{:S(2)}, u32[]{:S(2)}) collective-permute-start(bf16[256,512]{1,0:T(8,128)(2,1)} %get-tuple-element.276), channel_id=1, source_target_pairs={{0,3},{1,2},{2,1},{3,0},{4,7},{5,6},{6,5},{7,4},{8,11},{9,10},{10,... | collective-permute-start | bytes 786440 | tf_op jit(solution)/shard_map/ppermute | solution.py:386
  108.0 30.1 %collective-permute-start.22 = (bf16[528,512]{1,0:T(8,128)(2,1)S(1)}, bf16[528,512]{1,0:T(8,128)(2,1)S(1)}, u32[]{:S(2)}, u32[]{:S(2)}) collective-permute-start(bf16[528,512]{1,0:T(8,128)(2,1)S(1)} %get-tuple-element.272), channel_id=1, source_target_pairs={{0,8},{4,12},{8,0},{12,4},{16,24},{20,28},{24,16},{28,20},{1,9},{5... | collective-permute-start | bytes 1622024 | tf_op jit(solution)/shard_map/ppermute | solution.py:386
  109.6 28.5 %collective-permute-start.23 = (bf16[528,512]{1,0:T(8,128)(2,1)S(1)}, bf16[528,512]{1,0:T(8,128)(2,1)S(1)}, u32[]{:S(2)}, u32[]{:S(2)}) collective-permute-start(bf16[528,512]{1,0:T(8,128)(2,1)S(1)} %get-tuple-element.273), channel_id=1, source_target_pairs={{0,16},{4,20},{8,24},{12,28},{16,0},{20,4},{24,8},{28,12},{1,17},{... | collective-permute-start | bytes 1622024 | tf_op jit(solution)/shard_map/ppermute | solution.py:386
  110.7 27.4 %collective-permute-start.24 = (bf16[528,512]{1,0:T(8,128)(2,1)S(1)}, bf16[528,512]{1,0:T(8,128)(2,1)S(1)}, u32[]{:S(2)}, u32[]{:S(2)}) collective-permute-start(bf16[528,512]{1,0:T(8,128)(2,1)S(1)} %get-tuple-element.274), channel_id=1, source_target_pairs={{0,24},{4,28},{8,16},{12,20},{16,8},{20,12},{24,0},{28,4},{1,25},{... | collective-permute-start | bytes 1622024 | tf_op jit(solution)/shard_map/ppermute | solution.py:386
  139.3 15.2 %collective-permute-start.27 = (bf16[272,512]{1,0:T(8,128)(2,1)S(1)}, bf16[272,512]{1,0:T(8,128)(2,1)S(1)}, u32[]{:S(2)}, u32[]{:S(2)}) collective-permute-start(bf16[272,512]{1,0:T(8,128)(2,1)S(1)} %get-tuple-element.286), channel_id=1, source_target_pairs={{0,2},{1,3},{2,0},{3,1},{4,6},{5,7},{6,4},{7,5},{8,10},{9,11},{10,... | collective-permute-start | bytes 835592 | tf_op jit(solution)/shard_map/ppermute | solution.py:386
  139.4 12.4 %collective-permute-start.32 = (bf16[256,512]{1,0:T(8,128)(2,1)S(1)}, bf16[256,512]{1,0:T(8,128)(2,1)S(1)}, u32[]{:S(2)}, u32[]{:S(2)}) collective-permute-start(bf16[256,512]{1,0:T(8,128)(2,1)S(1)} %copy-done.33), channel_id=1, source_target_pairs={{0,1},{1,0},{2,3},{3,2},{4,5},{5,4},{6,7},{7,6},{8,9},{9,8},{10,11... | collective-permute-start | bytes 786440 | tf_op jit(solution)/shard_map/ppermute | solution.py:386
  144.3 13.7 %collective-permute-start.30 = (bf16[256,512]{1,0:T(8,128)(2,1)S(1)}, bf16[256,512]{1,0:T(8,128)(2,1)S(1)}, u32[]{:S(2)}, u32[]{:S(2)}) collective-permute-start(bf16[256,512]{1,0:T(8,128)(2,1)S(1)} %get-tuple-element.291), channel_id=1, source_target_pairs={{0,16},{4,20},{8,24},{12,28},{16,0},{20,4},{24,8},{28,12},{1,17},{... | collective-permute-start | bytes 786440 | tf_op jit(solution)/shard_map/ppermute | solution.py:386
  171.4 14.7 %collective-permute-start.39 = (bf16[320,512]{1,0:T(8,128)(2,1)S(1)}, bf16[320,512]{1,0:T(8,128)(2,1)S(1)}, u32[]{:S(2)}, u32[]{:S(2)}) collective-permute-start(bf16[320,512]{1,0:T(8,128)(2,1)S(1)} %get-tuple-element.315), channel_id=1, source_target_pairs={{0,24},{4,28},{8,16},{12,20},{16,8},{20,12},{24,0},{28,4},{1,25},{... | collective-permute-start | bytes 983048 | tf_op jit(solution)/shard_map/ppermute | solution.py:386
  172.9 14.3 %collective-permute-start.38 = (bf16[320,512]{1,0:T(8,128)(2,1)S(1)}, bf16[320,512]{1,0:T(8,128)(2,1)S(1)}, u32[]{:S(2)}, u32[]{:S(2)}) collective-permute-start(bf16[320,512]{1,0:T(8,128)(2,1)S(1)} %get-tuple-element.315), channel_id=1, source_target_pairs={{0,16},{4,20},{8,24},{12,28},{16,0},{20,4},{24,8},{28,12},{1,17},{... | collective-permute-start | bytes 983048 | tf_op jit(solution)/shard_map/ppermute | solution.py:386
  174.5 12.7 %collective-permute-start.37 = (bf16[320,512]{1,0:T(8,128)(2,1)S(1)}, bf16[320,512]{1,0:T(8,128)(2,1)S(1)}, u32[]{:S(2)}, u32[]{:S(2)}) collective-permute-start(bf16[320,512]{1,0:T(8,128)(2,1)S(1)} %get-tuple-element.315), channel_id=1, source_target_pairs={{0,8},{4,12},{8,0},{12,4},{16,24},{20,28},{24,16},{28,20},{1,9},{5... | collective-permute-start | bytes 983048 | tf_op jit(solution)/shard_map/ppermute | solution.py:386
  188.2 14.5 %collective-permute-start.43 = (bf16[256,512]{1,0:T(8,128)(2,1)S(1)}, bf16[256,512]{1,0:T(8,128)(2,1)S(1)}, u32[]{:S(2)}, u32[]{:S(2)}) collective-permute-start(bf16[256,512]{1,0:T(8,128)(2,1)S(1)} %copy-done.31), channel_id=1, source_target_pairs={{0,3},{1,2},{2,1},{3,0},{4,7},{5,6},{6,5},{7,4},{8,11},{9,10},{10,... | collective-permute-start | bytes 786440 | tf_op jit(solution)/shard_map/ppermute | solution.py:386
  189.9 37.2 %collective-permute-start.45 = (bf16[256,512]{1,0:T(8,128)(2,1)S(1)}, bf16[256,512]{1,0:T(8,128)(2,1)S(1)}, u32[]{:S(2)}, u32[]{:S(2)}) collective-permute-start(bf16[256,512]{1,0:T(8,128)(2,1)S(1)} %momentum_rows.1), channel_id=1, source_target_pairs={{0,2},{1,3},{2,0},{3,1},{4,6},{5,7},{6,4},{7,5},{8,10},{9,11},{10,... | collective-permute-start | bytes 786440 | tf_op jit(solution)/shard_map/ppermute | solution.py:386
  202.7 24.2 %collective-permute-start.47 = (bf16[128,512]{1,0:T(8,128)(2,1)S(1)}, bf16[128,512]{1,0:T(8,128)(2,1)S(1)}, u32[]{:S(2)}, u32[]{:S(2)}) collective-permute-start(bf16[128,512]{1,0:T(8,128)(2,1)S(1)} %get-tuple-element.340), channel_id=1, source_target_pairs={{0,1},{1,0},{2,3},{3,2},{4,5},{5,4},{6,7},{7,6},{8,9},{9,8},{10,11... | collective-permute-start | bytes 393224 | tf_op jit(solution)/shard_map/ppermute | solution.py:386
  210.5 16.4 %collective-permute-start.48 = (bf16[128,512]{1,0:T(8,128)(2,1)S(1)}, bf16[128,512]{1,0:T(8,128)(2,1)S(1)}, u32[]{:S(2)}, u32[]{:S(2)}) collective-permute-start(bf16[128,512]{1,0:T(8,128)(2,1)S(1)} %get-tuple-element.341), channel_id=1, source_target_pairs={{0,2},{1,3},{2,0},{3,1},{4,6},{5,7},{6,4},{7,5},{8,10},{9,11},{10,... | collective-permute-start | bytes 393224 | tf_op jit(solution)/shard_map/ppermute | solution.py:386
  210.8 16.2 %collective-permute-start.49 = (bf16[128,512]{1,0:T(8,128)(2,1)S(1)}, bf16[128,512]{1,0:T(8,128)(2,1)S(1)}, u32[]{:S(2)}, u32[]{:S(2)}) collective-permute-start(bf16[128,512]{1,0:T(8,128)(2,1)S(1)} %get-tuple-element.342), channel_id=1, source_target_pairs={{0,3},{1,2},{2,1},{3,0},{4,7},{5,6},{6,5},{7,4},{8,11},{9,10},{10,... | collective-permute-start | bytes 393224 | tf_op jit(solution)/shard_map/ppermute | solution.py:386
  227.6 14.8 %collective-permute-start.44 = (bf16[256,512]{1,0:T(8,128)(2,1)S(1)}, bf16[256,512]{1,0:T(8,128)(2,1)S(1)}, u32[]{:S(2)}, u32[]{:S(2)}) collective-permute-start(bf16[256,512]{1,0:T(8,128)(2,1)S(1)} %get-tuple-element.328), channel_id=1, source_target_pairs={{0,2},{1,3},{2,0},{3,1},{4,6},{5,7},{6,4},{7,5},{8,10},{9,11},{10,... | collective-permute-start | bytes 786440 | tf_op jit(solution)/shard_map/ppermute | solution.py:386
  (67 other events, 697.6 us)

commit v5 on v4

--- a/solution.py
+++ b/solution.py
@@ -1307,10 +1307,11 @@
     qkv_halves = [qkv_own, swap(qkv_own, "dp", 1)]
     rest_own, ups = together(jnp.stack(rest_own), ups)
     rest_own = around_chips(rest_own)
-    ups = [ups[0]] + [swap(ups[u], "mp", u) for u in to_planes]
+    up_near = ups[1]
+    ups = [ups[0], None] + [swap(ups[u], "mp", u) for u in to_planes[1:]]
     qkv, heads = attention(place, last, inputs, qkv_halves)
-    heads, rest_own, ups, buffers_old = together(heads, rest_own, ups, buffers_old)
-    rest_halves = interleave(rest_own, [swap(part, "dp", 1) for part in rest_own])
+    heads, up_near, buffers_old = together(heads, up_near, buffers_old)
+    ups[1] = swap(up_near, "mp", 1)
     att_old, ffn_old = pieces(
         buffer_pieces_kernel,
         place,
@@ -1318,7 +1319,8 @@
         [like((4, span, D), f32), like((2, hid, D), f32)],
         "buffer_pieces",
     )
-    rest_halves, att_old, ffn_old = together(rest_halves, att_old, ffn_old)
+    heads, rest_own, ups, att_old, ffn_old = together(heads, rest_own, ups, att_old, ffn_old)
+    rest_halves = interleave(rest_own, [swap(part, "dp", 1) for part in rest_own])
     lays, rest = feed_forward(place, alphas, inputs, heads, ups, rest_halves, bias, bout)
     ffn_keep, ffn_give, grad_output, heads_grad, middle_grad, gb_in, gb_out, g_alpha = rest
 

time: 250 us -> 247 us (0.988)
  starting transfers between devices: 64.4 us -> 59.5 us
  waiting for transfers between devices: 53.1 us -> 55.6 us
    ppermute x52, starting transfers between devices: 64.4 us -> 59.5 us  [swap(): return lax.ppermute(x, axis, [(a, a ^ mask) for a in range(size)])]
    ppermute x52, waiting for transfers between devices: 53.1 us -> 55.6 us  [swap(): return lax.ppermute(x, axis, [(a, a ^ mask) for a in range(size)])]
  transfers between devices with their start and end apart: 52 -> 52, of which waited for: 17 -> 19; matrix products, arithmetic and copies ran while one was open for 3% -> 3% of each run, Pallas kernels for 33% -> 33%
where the time goes in v5:
time: 247 us; the launch traced here: 244 us
  Pallas kernels  116 us (47%)
  starting transfers between devices  59.5 us (24%)
  waiting for transfers between devices  55.6 us (23%)
  local copies, waits for them, and re-layouts  6.06 us (2%)
  other arithmetic  5.67 us (2%)
    pallas_call x20, Pallas kernels, run(): pl.pallas_call(kernel, grid_spec=pltpu.PrefetchScalarGridSpec(num_scalar_...  116 us
    ppermute x52, starting transfers between devices, swap(): return lax.ppermute(x, axis, [(a, a ^ mask) for a in range(size)])  59.5 us
    ppermute x52, waiting for transfers between devices, swap(): return lax.ppermute(x, axis, [(a, a ^ mask) for a in range(size)])  55.6 us
  transfers between devices with their start and end apart: 52, of which 19 were waited for; matrix products, arithmetic and copies ran while one was open for 3% of the time, Pallas kernels for 33%

profile of v5, /device:TPU:0, one launch (start us, length us, event | category | flops | bytes accessed | tf_op | source)
XLA Modules:
  0.0 244.0 jit_solution(8144736135457301461)
XLA Ops:
  1.3 2.9 %weight_pieces.1 = (bf16[48,512]{1,0:T(8,128)(2,1)}, bf16[144,512]{1,0:T(8,128)(2,1)}) custom-call(s32[2]{0:T(128)} %pad_add_fusion.place, f32[512,128]{1,0:T(8,128)} %refs_0_.3, f32[512,128]{1,0:T(8,128)} %refs_1_.5, f32[512,128]{1,0:T(8,128)} %refs_2_.3, f32[128,512]{1,0:T(8,128)} %refs_3_.3, f32[512,512]{1,0:T(8,128)} %we.1, f32[512,512]{1,0:T(8,128)} %wc.1), custom_call_target="tpu_custom_call" | custom-call | tf_op jit(solution)/shard_map/weight_pieces/pallas_call | solution.py:414
  4.2 5.0 %collective-permute-start.2 = (bf16[48,512]{1,0:T(8,128)(2,1)}, bf16[48,512]{1,0:T(8,128)(2,1)S(1)}, u32[]{:S(2)}, u32[]{:S(2)}) collective-permute-start(bf16[48,512]{1,0:T(8,128)(2,1)} %get-tuple-element.193), channel_id=1, source_target_pairs={{0,3},{1,2},{2,1},{3,0},{4,7},{5,6},{6,5},{7,4},{8,11},{9,10},{10,... | collective-permute-start | bytes 147464 | tf_op jit(solution)/shard_map/ppermute | solution.py:386
  9.8 3.8 %collective-permute-start.8 = (bf16[144,512]{1,0:T(8,128)(2,1)}, bf16[144,512]{1,0:T(8,128)(2,1)S(1)}, u32[]{:S(2)}, u32[]{:S(2)}) collective-permute-start(bf16[144,512]{1,0:T(8,128)(2,1)} %get-tuple-element.204), channel_id=1, source_target_pairs={{0,3},{1,2},{2,1},{3,0},{4,7},{5,6},{6,5},{7,4},{8,11},{9,10},{10,... | collective-permute-start | bytes 442376 | tf_op jit(solution)/shard_map/ppermute | solution.py:386
  17.2 3.4 %collective-permute-done.1 = bf16[48,512]{1,0:T(8,128)(2,1)S(1)} collective-permute-done((bf16[48,512]{1,0:T(8,128)(2,1)}, bf16[48,512]{1,0:T(8,128)(2,1)S(1)}, u32[]{:S(2)}, u32[]{:S(2)}) %collective-permute-start.1) | collective-permute-done | bytes 49184 | tf_op jit(solution)/shard_map/ppermute | solution.py:386
  20.6 2.5 %collective-permute-start.5 = (bf16[4,48,512]{2,1,0:T(8,128)(2,1)S(1)}, bf16[4,48,512]{2,1,0:T(8,128)(2,1)S(1)}, u32[]{:S(2)}, u32[]{:S(2)}) collective-permute-start(bf16[4,48,512]{2,1,0:T(8,128)(2,1)S(1)} %pad_maximum_fusion.4), channel_id=1, source_target_pairs={{0,24},{4,28},{8,16},{12,20},{16,8},{20,12},{24,0},{28,4},{1,25},{... | collective-permute-start | bytes 589832 | tf_op jit(solution)/shard_map/ppermute | solution.py:386
  33.3 2.1 collective-permute-start.14
  37.0 18.1 %attention_forward.1 = (bf16[4,4,1024,128]{3,2,1,0:T(8,128)(2,1)}, bf16[1024,512]{1,0:T(8,128)(2,1)}) custom-call(s32[2]{0:T(128)} %pad_add_fusion.place, s32[1,1024]{1,0:T(1,128)} %bitcast.56, bf16[4,1024,512]{2,1,0:T(8,128)(2,1)} %in_hbm.1, bf16[4,4,48,512]{3,2,1,0:T(8,128)(2,1)} %copy-done.19, bf16[4,4,48,512]{3,2,1,0:T(8,128)(2,1)} %copy-done.27), custom_call_target="tpu_custom_call" | custom-call | flops 5368709120 | bytes 11014144 | tf_op jit(solution)/shard_map/attention_forward/pallas_call | solution.py:414
  55.2 2.8 %buffer_pieces.1 = (f32[4,16,512]{2,1,0:T(8,128)}, f32[2,64,512]{2,1,0:T(8,128)}) custom-call(s32[2]{0:T(128)} %pad_add_fusion.place, f32[512,128]{1,0:T(8,128)} %q.2, f32[512,128]{1,0:T(8,128)} %k.2, f32[512,128]{1,0:T(8,128)} %v.2, f32[128,512]{1,0:T(8,128)} %o.2, f32[512,512]{1,0:T(8,128)} %e.2, f32[512,512]{1,0:T(8,128)} %c.2), custom_call_target="tpu_custom_call" | custom-call | tf_op jit(solution)/shard_map/buffer_pieces/pallas_call | solution.py:414
  59.2 3.3 %collective-permute-done.13.refs_4_ = bf16[256,512]{1,0:T(8,128)(2,1)S(1)} collective-permute-done((bf16[256,512]{1,0:T(8,128)(2,1)S(1)}, bf16[256,512]{1,0:T(8,128)(2,1)S(1)}, u32[]{:S(2)}, u32[]{:S(2)}) %collective-permute-start.13) | collective-permute-done | bytes 262176 | tf_op jit(solution)/shard_map/ppermute | solution.py:386
  68.0 28.0 %feed_forward.1 = (bf16[256,512]{1,0:T(8,128)(2,1)}, bf16[256,512]{1,0:T(8,128)(2,1)}, bf16[256,512]{1,0:T(8,128)(2,1)}, bf16[256,512]{1,0:T(8,128)(2,1)}, bf16[...) custom-call(s32[2]{0:T(128)} %pad_add_fusion.place, ...), custom_call_target="tpu_custom_call" | custom-call | flops 12884901888 | bytes 19947528 | tf_op jit(solution)/shard_map/feed_forward/pallas_call | solution.py:414
  108.1 26.5 %attention_backward.1 = (bf16[256,512]{1,0:T(8,128)(2,1)}, bf16[256,512]{1,0:T(8,128)(2,1)}, bf16[256,512]{1,0:T(8,128)(2,1)}, bf16[256,512]{1,0:T(8,128)(2,1)},...) custom-call(s32[2]{0:T(128)} %pad_add_fusion.place, s32[1,1024]{1,0:T(1,128)} %bitcast.61, ...), custom_call_target="tpu_custom_call" | custom-call | flops 11274289152 | bytes 17829888 | tf_op jit(solution)/shard_map/attention_backward/pallas_call | solution.py:414
  143.1 6.7 %collective-permute-done.32.refs_1_ = bf16[256,512]{1,0:T(8,128)(2,1)S(1)} collective-permute-done((bf16[256,512]{1,0:T(8,128)(2,1)S(1)}, bf16[256,512]{1,0:T(8,128)(2,1)S(1)}, u32[]{:S(2)}, u32[]{:S(2)}) %collective-permute-start.32) | collective-permute-done | bytes 262176 | tf_op jit(solution)/shard_map/ppermute | solution.py:386
  151.8 2.7 %collective-permute-done.30.refs_2_ = bf16[256,512]{1,0:T(8,128)(2,1)S(1)} collective-permute-done((bf16[256,512]{1,0:T(8,128)(2,1)S(1)}, bf16[256,512]{1,0:T(8,128)(2,1)S(1)}, u32[]{:S(2)}, u32[]{:S(2)}) %collective-permute-start.30) | collective-permute-done | bytes 262176 | tf_op jit(solution)/shard_map/ppermute | solution.py:386
  161.2 4.8 %collective-permute-done.34.refs_1_ = bf16[64,512]{1,0:T(8,128)(2,1)S(1)} collective-permute-done((bf16[64,512]{1,0:T(8,128)(2,1)S(1)}, bf16[64,512]{1,0:T(8,128)(2,1)S(1)}, u32[]{:S(2)}, u32[]{:S(2)}) %collective-permute-start.34) | collective-permute-done | bytes 65568 | tf_op jit(solution)/shard_map/ppermute | solution.py:386
  166.0 2.2 collective-permute-done.36.refs_3_
  173.0 9.7 %collective-permute-done.40.refs_2_ = bf16[256,512]{1,0:T(8,128)(2,1)S(1)} collective-permute-done((bf16[256,512]{1,0:T(8,128)(2,1)S(1)}, bf16[256,512]{1,0:T(8,128)(2,1)S(1)}, u32[]{:S(2)}, u32[]{:S(2)}) %collective-permute-start.40) | collective-permute-done | bytes 262176 | tf_op jit(solution)/shard_map/ppermute | solution.py:386
  186.3 2.4 collective-permute-start.45
  188.7 6.9 %newton_att.1 = (bf16[128,512]{1,0:T(8,128)(2,1)S(1)}, bf16[128,512]{1,0:T(8,128)(2,1)S(1)}, bf16[128,512]{1,0:T(8,128)(2,1)S(1)}, bf16[128,512]{1,0:T(8,128)(2,1)S(1)}) custom-call(s32[2]{0:T(128)S(1)} %copy-done.17, bf16[1280,512]{1,0:T(8,128)(2,1)S(1)} %constant_dynamic-update-slice_fusion.own, bf16[1280,512]{1,0:T(8,128)(2,1)S(1)} %collective-permute-done.41.other), custom_call_target="tpu_custom_call" | custom-call | flops 4026531840 | bytes 3145728 | tf_op jit(solution)/shard_map/newton_att/pallas_call | solution.py:414
  195.7 3.8 %collective-permute-done.42.refs_1_ = bf16[256,512]{1,0:T(8,128)(2,1)S(1)} collective-permute-done((bf16[256,512]{1,0:T(8,128)(2,1)S(1)}, bf16[256,512]{1,0:T(8,128)(2,1)S(1)}, u32[]{:S(2)}, u32[]{:S(2)}) %collective-permute-start.42) | collective-permute-done | bytes 262176 | tf_op jit(solution)/shard_map/ppermute | solution.py:386
  199.5 8.2 %collective-permute-start.47 = (bf16[128,512]{1,0:T(8,128)(2,1)S(1)}, bf16[128,512]{1,0:T(8,128)(2,1)S(1)}, u32[]{:S(2)}, u32[]{:S(2)}) collective-permute-start(bf16[128,512]{1,0:T(8,128)(2,1)S(1)} %get-tuple-element.328), channel_id=1, source_target_pairs={{0,1},{1,0},{2,3},{3,2},{4,5},{5,4},{6,7},{7,6},{8,9},{9,8},{10,11... | collective-permute-start | bytes 393224 | tf_op jit(solution)/shard_map/ppermute | solution.py:386
  207.7 2.4 collective-permute-start.49
  210.0 14.0 %newton_ffn.1 = (bf16[256,512]{1,0:T(8,128)(2,1)S(1)}, bf16[256,512]{1,0:T(8,128)(2,1)S(1)}) custom-call(s32[2]{0:T(128)S(1)} %copy-done.17, bf16[1280,512]{1,0:T(8,128)(2,1)S(1)} %constant_dynamic-update-slice_fusion.own, bf16[1280,512]{1,0:T(8,128)(2,1)S(1)} %collective-permute-done.41.other), custom_call_target="tpu_custom_call" | custom-call | flops 12079595520 | bytes 3145728 | tf_op jit(solution)/shard_map/newton_ffn/pallas_call | solution.py:414
  231.5 2.2 att_final.1
  233.8 5.8 %collective-permute-done.44.far = bf16[256,512]{1,0:T(8,128)(2,1)S(1)} collective-permute-done((bf16[256,512]{1,0:T(8,128)(2,1)S(1)}, bf16[256,512]{1,0:T(8,128)(2,1)S(1)}, u32[]{:S(2)}, u32[]{:S(2)}) %collective-permute-start.44) | collective-permute-done | bytes 262176 | tf_op jit(solution)/shard_map/ppermute | solution.py:386
  (218 shorter events, 72.0 us)
Async XLA Ops:
  9.8 13.8 %collective-permute-start.8 = (bf16[144,512]{1,0:T(8,128)(2,1)}, bf16[144,512]{1,0:T(8,128)(2,1)S(1)}, u32[]{:S(2)}, u32[]{:S(2)}) collective-permute-start(bf16[144,512]{1,0:T(8,128)(2,1)} %get-tuple-element.204), channel_id=1, source_target_pairs={{0,3},{1,2},{2,1},{3,0},{4,7},{5,6},{6,5},{7,4},{8,11},{9,10},{10,... | collective-permute-start | bytes 442376 | tf_op jit(solution)/shard_map/ppermute | solution.py:386
  13.6 13.1 %collective-permute-start.7 = (bf16[144,512]{1,0:T(8,128)(2,1)}, bf16[144,512]{1,0:T(8,128)(2,1)S(1)}, u32[]{:S(2)}, u32[]{:S(2)}) collective-permute-start(bf16[144,512]{1,0:T(8,128)(2,1)} %get-tuple-element.204), channel_id=1, source_target_pairs={{0,2},{1,3},{2,0},{3,1},{4,6},{5,7},{6,4},{7,5},{8,10},{9,11},{10,... | collective-permute-start | bytes 442376 | tf_op jit(solution)/shard_map/ppermute | solution.py:386
  29.7 28.3 %collective-permute-start.12 = (bf16[4,144,512]{2,1,0:T(8,128)(2,1)S(1)}, bf16[4,144,512]{2,1,0:T(8,128)(2,1)}, u32[]{:S(2)}, u32[]{:S(2)}) collective-permute-start(bf16[4,144,512]{2,1,0:T(8,128)(2,1)S(1)} %pad_maximum_fusion.1.refs_7_), channel_id=1, source_target_pairs={{0,24},{4,28},{8,16},{12,20},{16,8},{20,12},{24,0},{28,4},{1,25},{... | collective-permute-start | bytes 1769480 | tf_op jit(solution)/shard_map/ppermute | solution.py:386
  31.7 27.4 %collective-permute-start.11 = (bf16[4,144,512]{2,1,0:T(8,128)(2,1)S(1)}, bf16[4,144,512]{2,1,0:T(8,128)(2,1)}, u32[]{:S(2)}, u32[]{:S(2)}) collective-permute-start(bf16[4,144,512]{2,1,0:T(8,128)(2,1)S(1)} %pad_maximum_fusion.1.refs_7_), channel_id=1, source_target_pairs={{0,16},{4,20},{8,24},{12,28},{16,0},{20,4},{24,8},{28,12},{1,17},{... | collective-permute-start | bytes 1769480 | tf_op jit(solution)/shard_map/ppermute | solution.py:386
  32.8 26.4 %collective-permute-start.10 = (bf16[4,144,512]{2,1,0:T(8,128)(2,1)S(1)}, bf16[4,144,512]{2,1,0:T(8,128)(2,1)}, u32[]{:S(2)}, u32[]{:S(2)}) collective-permute-start(bf16[4,144,512]{2,1,0:T(8,128)(2,1)S(1)} %pad_maximum_fusion.1.refs_7_), channel_id=1, source_target_pairs={{0,8},{4,12},{8,0},{12,4},{16,24},{20,28},{24,16},{28,20},{1,9},{5... | collective-permute-start | bytes 1769480 | tf_op jit(solution)/shard_map/ppermute | solution.py:386
  33.3 21.8 %collective-permute-start.14 = (bf16[256,512]{1,0:T(8,128)(2,1)S(1)}, bf16[256,512]{1,0:T(8,128)(2,1)S(1)}, u32[]{:S(2)}, u32[]{:S(2)}) collective-permute-start(bf16[256,512]{1,0:T(8,128)(2,1)S(1)} %get-tuple-element.217), channel_id=1, source_target_pairs={{0,2},{1,3},{2,0},{3,1},{4,6},{5,7},{6,4},{7,5},{8,10},{9,11},{10,... | collective-permute-start | bytes 786440 | tf_op jit(solution)/shard_map/ppermute | solution.py:386
  35.4 22.6 %collective-permute-start.15 = (bf16[256,512]{1,0:T(8,128)(2,1)S(1)}, bf16[256,512]{1,0:T(8,128)(2,1)S(1)}, u32[]{:S(2)}, u32[]{:S(2)}) collective-permute-start(bf16[256,512]{1,0:T(8,128)(2,1)S(1)} %get-tuple-element.218), channel_id=1, source_target_pairs={{0,3},{1,2},{2,1},{3,0},{4,7},{5,6},{6,5},{7,4},{8,11},{9,10},{10,... | collective-permute-start | bytes 786440 | tf_op jit(solution)/shard_map/ppermute | solution.py:386
  99.2 35.4 %collective-permute-start.25 = (bf16[256,512]{1,0:T(8,128)(2,1)}, bf16[256,512]{1,0:T(8,128)(2,1)S(1)}, u32[]{:S(2)}, u32[]{:S(2)}) collective-permute-start(bf16[256,512]{1,0:T(8,128)(2,1)} %get-tuple-element.263), channel_id=1, source_target_pairs={{0,2},{1,3},{2,0},{3,1},{4,6},{5,7},{6,4},{7,5},{8,10},{9,11},{10,... | collective-permute-start | bytes 786440 | tf_op jit(solution)/shard_map/ppermute | solution.py:386
  100.3 34.4 %collective-permute-start.26 = (bf16[256,512]{1,0:T(8,128)(2,1)}, bf16[256,512]{1,0:T(8,128)(2,1)S(1)}, u32[]{:S(2)}, u32[]{:S(2)}) collective-permute-start(bf16[256,512]{1,0:T(8,128)(2,1)} %get-tuple-element.264), channel_id=1, source_target_pairs={{0,3},{1,2},{2,1},{3,0},{4,7},{5,6},{6,5},{7,4},{8,11},{9,10},{10,... | collective-permute-start | bytes 786440 | tf_op jit(solution)/shard_map/ppermute | solution.py:386
  104.5 30.1 %collective-permute-start.22 = (bf16[528,512]{1,0:T(8,128)(2,1)S(1)}, bf16[528,512]{1,0:T(8,128)(2,1)S(1)}, u32[]{:S(2)}, u32[]{:S(2)}) collective-permute-start(bf16[528,512]{1,0:T(8,128)(2,1)S(1)} %get-tuple-element.260), channel_id=1, source_target_pairs={{0,8},{4,12},{8,0},{12,4},{16,24},{20,28},{24,16},{28,20},{1,9},{5... | collective-permute-start | bytes 1622024 | tf_op jit(solution)/shard_map/ppermute | solution.py:386
  106.1 28.6 %collective-permute-start.23 = (bf16[528,512]{1,0:T(8,128)(2,1)S(1)}, bf16[528,512]{1,0:T(8,128)(2,1)S(1)}, u32[]{:S(2)}, u32[]{:S(2)}) collective-permute-start(bf16[528,512]{1,0:T(8,128)(2,1)S(1)} %get-tuple-element.261), channel_id=1, source_target_pairs={{0,16},{4,20},{8,24},{12,28},{16,0},{20,4},{24,8},{28,12},{1,17},{... | collective-permute-start | bytes 1622024 | tf_op jit(solution)/shard_map/ppermute | solution.py:386
  107.6 27.1 %collective-permute-start.24 = (bf16[528,512]{1,0:T(8,128)(2,1)S(1)}, bf16[528,512]{1,0:T(8,128)(2,1)S(1)}, u32[]{:S(2)}, u32[]{:S(2)}) collective-permute-start(bf16[528,512]{1,0:T(8,128)(2,1)S(1)} %get-tuple-element.262), channel_id=1, source_target_pairs={{0,24},{4,28},{8,16},{12,20},{16,8},{20,12},{24,0},{28,4},{1,25},{... | collective-permute-start | bytes 1622024 | tf_op jit(solution)/shard_map/ppermute | solution.py:386
  135.9 15.9 %collective-permute-start.27 = (bf16[272,512]{1,0:T(8,128)(2,1)S(1)}, bf16[272,512]{1,0:T(8,128)(2,1)S(1)}, u32[]{:S(2)}, u32[]{:S(2)}) collective-permute-start(bf16[272,512]{1,0:T(8,128)(2,1)S(1)} %get-tuple-element.274), channel_id=1, source_target_pairs={{0,2},{1,3},{2,0},{3,1},{4,6},{5,7},{6,4},{7,5},{8,10},{9,11},{10,... | collective-permute-start | bytes 835592 | tf_op jit(solution)/shard_map/ppermute | solution.py:386
  141.1 13.4 %collective-permute-start.30 = (bf16[256,512]{1,0:T(8,128)(2,1)S(1)}, bf16[256,512]{1,0:T(8,128)(2,1)S(1)}, u32[]{:S(2)}, u32[]{:S(2)}) collective-permute-start(bf16[256,512]{1,0:T(8,128)(2,1)S(1)} %get-tuple-element.279), channel_id=1, source_target_pairs={{0,16},{4,20},{8,24},{12,28},{16,0},{20,4},{24,8},{28,12},{1,17},{... | collective-permute-start | bytes 786440 | tf_op jit(solution)/shard_map/ppermute | solution.py:386
  155.2 13.0 %collective-permute-start.33 = (bf16[272,512]{1,0:T(8,128)(2,1)S(1)}, bf16[272,512]{1,0:T(8,128)(2,1)S(1)}, u32[]{:S(2)}, u32[]{:S(2)}) collective-permute-start(bf16[272,512]{1,0:T(8,128)(2,1)S(1)} %ffn_far_sum.1.keep), channel_id=1, source_target_pairs={{0,1},{1,0},{2,3},{3,2},{4,5},{5,4},{6,7},{7,6},{8,9},{9,8},{10,11... | collective-permute-start | bytes 835592 | tf_op jit(solution)/shard_map/ppermute | solution.py:386
  168.8 13.9 %collective-permute-start.39 = (bf16[320,512]{1,0:T(8,128)(2,1)S(1)}, bf16[320,512]{1,0:T(8,128)(2,1)S(1)}, u32[]{:S(2)}, u32[]{:S(2)}) collective-permute-start(bf16[320,512]{1,0:T(8,128)(2,1)S(1)} %get-tuple-element.303), channel_id=1, source_target_pairs={{0,24},{4,28},{8,16},{12,20},{16,8},{20,12},{24,0},{28,4},{1,25},{... | collective-permute-start | bytes 983048 | tf_op jit(solution)/shard_map/ppermute | solution.py:386
  170.3 14.0 %collective-permute-start.38 = (bf16[320,512]{1,0:T(8,128)(2,1)S(1)}, bf16[320,512]{1,0:T(8,128)(2,1)S(1)}, u32[]{:S(2)}, u32[]{:S(2)}) collective-permute-start(bf16[320,512]{1,0:T(8,128)(2,1)S(1)} %get-tuple-element.303), channel_id=1, source_target_pairs={{0,16},{4,20},{8,24},{12,28},{16,0},{20,4},{24,8},{28,12},{1,17},{... | collective-permute-start | bytes 983048 | tf_op jit(solution)/shard_map/ppermute | solution.py:386
  185.2 14.3 %collective-permute-start.42 = (bf16[256,512]{1,0:T(8,128)(2,1)S(1)}, bf16[256,512]{1,0:T(8,128)(2,1)S(1)}, u32[]{:S(2)}, u32[]{:S(2)}) collective-permute-start(bf16[256,512]{1,0:T(8,128)(2,1)S(1)} %copy-done.32), channel_id=1, source_target_pairs={{0,1},{1,0},{2,3},{3,2},{4,5},{5,4},{6,7},{7,6},{8,9},{9,8},{10,11... | collective-permute-start | bytes 786440 | tf_op jit(solution)/shard_map/ppermute | solution.py:386
  185.3 14.2 %collective-permute-start.43 = (bf16[256,512]{1,0:T(8,128)(2,1)S(1)}, bf16[256,512]{1,0:T(8,128)(2,1)S(1)}, u32[]{:S(2)}, u32[]{:S(2)}) collective-permute-start(bf16[256,512]{1,0:T(8,128)(2,1)S(1)} %copy-done.31), channel_id=1, source_target_pairs={{0,3},{1,2},{2,1},{3,0},{4,7},{5,6},{6,5},{7,4},{8,11},{9,10},{10,... | collective-permute-start | bytes 786440 | tf_op jit(solution)/shard_map/ppermute | solution.py:386
  186.3 37.9 %collective-permute-start.45 = (bf16[256,512]{1,0:T(8,128)(2,1)S(1)}, bf16[256,512]{1,0:T(8,128)(2,1)S(1)}, u32[]{:S(2)}, u32[]{:S(2)}) collective-permute-start(bf16[256,512]{1,0:T(8,128)(2,1)S(1)} %momentum_rows.1), channel_id=1, source_target_pairs={{0,2},{1,3},{2,0},{3,1},{4,6},{5,7},{6,4},{7,5},{8,10},{9,11},{10,... | collective-permute-start | bytes 786440 | tf_op jit(solution)/shard_map/ppermute | solution.py:386
  199.5 24.6 %collective-permute-start.47 = (bf16[128,512]{1,0:T(8,128)(2,1)S(1)}, bf16[128,512]{1,0:T(8,128)(2,1)S(1)}, u32[]{:S(2)}, u32[]{:S(2)}) collective-permute-start(bf16[128,512]{1,0:T(8,128)(2,1)S(1)} %get-tuple-element.328), channel_id=1, source_target_pairs={{0,1},{1,0},{2,3},{3,2},{4,5},{5,4},{6,7},{7,6},{8,9},{9,8},{10,11... | collective-permute-start | bytes 393224 | tf_op jit(solution)/shard_map/ppermute | solution.py:386
  207.7 16.4 %collective-permute-start.48 = (bf16[128,512]{1,0:T(8,128)(2,1)S(1)}, bf16[128,512]{1,0:T(8,128)(2,1)S(1)}, u32[]{:S(2)}, u32[]{:S(2)}) collective-permute-start(bf16[128,512]{1,0:T(8,128)(2,1)S(1)} %get-tuple-element.329), channel_id=1, source_target_pairs={{0,2},{1,3},{2,0},{3,1},{4,6},{5,7},{6,4},{7,5},{8,10},{9,11},{10,... | collective-permute-start | bytes 393224 | tf_op jit(solution)/shard_map/ppermute | solution.py:386
  207.7 16.4 %collective-permute-start.49 = (bf16[128,512]{1,0:T(8,128)(2,1)S(1)}, bf16[128,512]{1,0:T(8,128)(2,1)S(1)}, u32[]{:S(2)}, u32[]{:S(2)}) collective-permute-start(bf16[128,512]{1,0:T(8,128)(2,1)S(1)} %get-tuple-element.330), channel_id=1, source_target_pairs={{0,3},{1,2},{2,1},{3,0},{4,7},{5,6},{6,5},{7,4},{8,11},{9,10},{10,... | collective-permute-start | bytes 393224 | tf_op jit(solution)/shard_map/ppermute | solution.py:386
  224.8 14.8 %collective-permute-start.44 = (bf16[256,512]{1,0:T(8,128)(2,1)S(1)}, bf16[256,512]{1,0:T(8,128)(2,1)S(1)}, u32[]{:S(2)}, u32[]{:S(2)}) collective-permute-start(bf16[256,512]{1,0:T(8,128)(2,1)S(1)} %get-tuple-element.316), channel_id=1, source_target_pairs={{0,2},{1,3},{2,0},{3,1},{4,6},{5,7},{6,4},{7,5},{8,10},{9,11},{10,... | collective-permute-start | bytes 786440 | tf_op jit(solution)/shard_map/ppermute | solution.py:386
  (67 other events, 642.7 us)

commit v6 on v5

--- a/solution.py
+++ b/solution.py
@@ -540,9 +540,12 @@
     return in_lanes(HEAD_DIM * half, HEAD_DIM * (half + 1), x, spare_lanes(half, values, x))
 
 
-def two_parts(x):
-    high = x.astype(bf16)
-    return high, (x - high.astype(f32)).astype(bf16)
+def low_parts(x):
+    parts = []
+    for _ in range(3):
+        parts.append(x.astype(bf16))
+        x = x - parts[-1].astype(f32)
+    return parts
 
 
 def forward_kernel(place, last_ref, in_ref, *refs):
@@ -579,7 +582,7 @@
             out = mm(weight, v_ref[half, low:high, :], nn)
             total = out[:, spare : spare + 1]
             found.append(out * (1.0 / total))
-            parts = two_parts(-(peak + jnp.log(total)))
+            parts = low_parts(-(peak + jnp.log(total)))
             x_ref[0, half, first:high, :] = head_lanes(half, q_ref[half, first:high, :], parts)
         o_ref[first:high, :] = in_lanes(0, HEAD_DIM, found[0], found[1]).astype(bf16)
 
@@ -641,10 +644,10 @@
     one = jnp.asarray(1, bf16)
     product = g_ref[...].astype(f32) * o_ref[...].astype(f32)
     for half in range(2):
-        k_ref[half] = head_lanes(half, x_ref[0, 2], (one, one))
-        v_ref[half] = head_lanes(half, x_ref[0, 3], (one, one))
+        k_ref[half] = head_lanes(half, x_ref[0, 2], (one,) * 3)
+        v_ref[half] = head_lanes(half, x_ref[0, 3], (one,) * 3)
         delta = jnp.sum(head_lanes(half, product), axis=1, keepdims=True)
-        gs_ref[half] = head_lanes(half, g_ref[...], two_parts(-delta))
+        gs_ref[half] = head_lanes(half, g_ref[...], low_parts(-delta))
     for first, low, high in blocks:
         q_both = jnp.concatenate([head_lanes(half, x_ref[0, half, first:high, :]) for half in range(2)], 0)
         g_both = jnp.concatenate([head_lanes(half, g_ref[first:high, :]) for half in range(2)], 0)

time: 247 us -> 247 us (level)
  no operation moved by 1% of the time
where the time goes in v6:
time: 247 us; the launch traced here: 244 us
  Pallas kernels  116 us (47%)
  starting transfers between devices  59.5 us (24%)
  waiting for transfers between devices  55.6 us (23%)
  local copies, waits for them, and re-layouts  6.06 us (2%)
  other arithmetic  5.67 us (2%)
    pallas_call x20, Pallas kernels, run(): pl.pallas_call(kernel, grid_spec=pltpu.PrefetchScalarGridSpec(num_scalar_...  116 us
    ppermute x52, starting transfers between devices, swap(): return lax.ppermute(x, axis, [(a, a ^ mask) for a in range(size)])  59.5 us
    ppermute x52, waiting for transfers between devices, swap(): return lax.ppermute(x, axis, [(a, a ^ mask) for a in range(size)])  55.6 us
  transfers between devices with their start and end apart: 52, of which 19 were waited for; matrix products, arithmetic and copies ran while one was open for 3% of the time, Pallas kernels for 33%

profile of v6, /device:TPU:0, one launch (start us, length us, event | category | flops | bytes accessed | tf_op | source)
XLA Modules:
  0.0 244.1 jit_solution(8612520288974643758)
XLA Ops:
  1.3 2.9 %weight_pieces.1 = (bf16[48,512]{1,0:T(8,128)(2,1)}, bf16[144,512]{1,0:T(8,128)(2,1)}) custom-call(s32[2]{0:T(128)} %pad_add_fusion.place, f32[512,128]{1,0:T(8,128)} %refs_0_.3, f32[512,128]{1,0:T(8,128)} %refs_1_.5, f32[512,128]{1,0:T(8,128)} %refs_2_.3, f32[128,512]{1,0:T(8,128)} %refs_3_.3, f32[512,512]{1,0:T(8,128)} %we.1, f32[512,512]{1,0:T(8,128)} %wc.1), custom_call_target="tpu_custom_call" | custom-call | tf_op jit(solution)/shard_map/weight_pieces/pallas_call | solution.py:414
  4.2 5.0 %collective-permute-start.2 = (bf16[48,512]{1,0:T(8,128)(2,1)}, bf16[48,512]{1,0:T(8,128)(2,1)S(1)}, u32[]{:S(2)}, u32[]{:S(2)}) collective-permute-start(bf16[48,512]{1,0:T(8,128)(2,1)} %get-tuple-element.193), channel_id=1, source_target_pairs={{0,3},{1,2},{2,1},{3,0},{4,7},{5,6},{6,5},{7,4},{8,11},{9,10},{10,... | collective-permute-start | bytes 147464 | tf_op jit(solution)/shard_map/ppermute | solution.py:386
  9.8 3.8 %collective-permute-start.8 = (bf16[144,512]{1,0:T(8,128)(2,1)}, bf16[144,512]{1,0:T(8,128)(2,1)S(1)}, u32[]{:S(2)}, u32[]{:S(2)}) collective-permute-start(bf16[144,512]{1,0:T(8,128)(2,1)} %get-tuple-element.204), channel_id=1, source_target_pairs={{0,3},{1,2},{2,1},{3,0},{4,7},{5,6},{6,5},{7,4},{8,11},{9,10},{10,... | collective-permute-start | bytes 442376 | tf_op jit(solution)/shard_map/ppermute | solution.py:386
  17.2 3.4 %collective-permute-done.1 = bf16[48,512]{1,0:T(8,128)(2,1)S(1)} collective-permute-done((bf16[48,512]{1,0:T(8,128)(2,1)}, bf16[48,512]{1,0:T(8,128)(2,1)S(1)}, u32[]{:S(2)}, u32[]{:S(2)}) %collective-permute-start.1) | collective-permute-done | bytes 49184 | tf_op jit(solution)/shard_map/ppermute | solution.py:386
  20.6 2.5 %collective-permute-start.5 = (bf16[4,48,512]{2,1,0:T(8,128)(2,1)S(1)}, bf16[4,48,512]{2,1,0:T(8,128)(2,1)S(1)}, u32[]{:S(2)}, u32[]{:S(2)}) collective-permute-start(bf16[4,48,512]{2,1,0:T(8,128)(2,1)S(1)} %pad_maximum_fusion.4), channel_id=1, source_target_pairs={{0,24},{4,28},{8,16},{12,20},{16,8},{20,12},{24,0},{28,4},{1,25},{... | collective-permute-start | bytes 589832 | tf_op jit(solution)/shard_map/ppermute | solution.py:386
  33.3 2.1 collective-permute-start.14
  37.0 18.2 %attention_forward.1 = (bf16[4,4,1024,128]{3,2,1,0:T(8,128)(2,1)}, bf16[1024,512]{1,0:T(8,128)(2,1)}) custom-call(s32[2]{0:T(128)} %pad_add_fusion.place, s32[1,1024]{1,0:T(1,128)} %bitcast.56, bf16[4,1024,512]{2,1,0:T(8,128)(2,1)} %in_hbm.1, bf16[4,4,48,512]{3,2,1,0:T(8,128)(2,1)} %copy-done.19, bf16[4,4,48,512]{3,2,1,0:T(8,128)(2,1)} %copy-done.27), custom_call_target="tpu_custom_call" | custom-call | flops 5368709120 | bytes 11014144 | tf_op jit(solution)/shard_map/attention_forward/pallas_call | solution.py:414
  55.3 2.8 %buffer_pieces.1 = (f32[4,16,512]{2,1,0:T(8,128)}, f32[2,64,512]{2,1,0:T(8,128)}) custom-call(s32[2]{0:T(128)} %pad_add_fusion.place, f32[512,128]{1,0:T(8,128)} %q.2, f32[512,128]{1,0:T(8,128)} %k.2, f32[512,128]{1,0:T(8,128)} %v.2, f32[128,512]{1,0:T(8,128)} %o.2, f32[512,512]{1,0:T(8,128)} %e.2, f32[512,512]{1,0:T(8,128)} %c.2), custom_call_target="tpu_custom_call" | custom-call | tf_op jit(solution)/shard_map/buffer_pieces/pallas_call | solution.py:414
  59.2 3.4 %collective-permute-done.13.refs_4_ = bf16[256,512]{1,0:T(8,128)(2,1)S(1)} collective-permute-done((bf16[256,512]{1,0:T(8,128)(2,1)S(1)}, bf16[256,512]{1,0:T(8,128)(2,1)S(1)}, u32[]{:S(2)}, u32[]{:S(2)}) %collective-permute-start.13) | collective-permute-done | bytes 262176 | tf_op jit(solution)/shard_map/ppermute | solution.py:386
  68.1 28.0 %feed_forward.1 = (bf16[256,512]{1,0:T(8,128)(2,1)}, bf16[256,512]{1,0:T(8,128)(2,1)}, bf16[256,512]{1,0:T(8,128)(2,1)}, bf16[256,512]{1,0:T(8,128)(2,1)}, bf16[...) custom-call(s32[2]{0:T(128)} %pad_add_fusion.place, ...), custom_call_target="tpu_custom_call" | custom-call | flops 12884901888 | bytes 19947528 | tf_op jit(solution)/shard_map/feed_forward/pallas_call | solution.py:414
  108.2 26.6 %attention_backward.1 = (bf16[256,512]{1,0:T(8,128)(2,1)}, bf16[256,512]{1,0:T(8,128)(2,1)}, bf16[256,512]{1,0:T(8,128)(2,1)}, bf16[256,512]{1,0:T(8,128)(2,1)},...) custom-call(s32[2]{0:T(128)} %pad_add_fusion.place, s32[1,1024]{1,0:T(1,128)} %bitcast.61, ...), custom_call_target="tpu_custom_call" | custom-call | flops 11274289152 | bytes 17829888 | tf_op jit(solution)/shard_map/attention_backward/pallas_call | solution.py:414
  143.2 6.6 %collective-permute-done.32.refs_1_ = bf16[256,512]{1,0:T(8,128)(2,1)S(1)} collective-permute-done((bf16[256,512]{1,0:T(8,128)(2,1)S(1)}, bf16[256,512]{1,0:T(8,128)(2,1)S(1)}, u32[]{:S(2)}, u32[]{:S(2)}) %collective-permute-start.32) | collective-permute-done | bytes 262176 | tf_op jit(solution)/shard_map/ppermute | solution.py:386
  151.9 2.7 %collective-permute-done.30.refs_2_ = bf16[256,512]{1,0:T(8,128)(2,1)S(1)} collective-permute-done((bf16[256,512]{1,0:T(8,128)(2,1)S(1)}, bf16[256,512]{1,0:T(8,128)(2,1)S(1)}, u32[]{:S(2)}, u32[]{:S(2)}) %collective-permute-start.30) | collective-permute-done | bytes 262176 | tf_op jit(solution)/shard_map/ppermute | solution.py:386
  161.3 4.8 %collective-permute-done.34.refs_1_ = bf16[64,512]{1,0:T(8,128)(2,1)S(1)} collective-permute-done((bf16[64,512]{1,0:T(8,128)(2,1)S(1)}, bf16[64,512]{1,0:T(8,128)(2,1)S(1)}, u32[]{:S(2)}, u32[]{:S(2)}) %collective-permute-start.34) | collective-permute-done | bytes 65568 | tf_op jit(solution)/shard_map/ppermute | solution.py:386
  166.2 2.1 collective-permute-done.36.refs_3_
  173.2 9.7 %collective-permute-done.40.refs_2_ = bf16[256,512]{1,0:T(8,128)(2,1)S(1)} collective-permute-done((bf16[256,512]{1,0:T(8,128)(2,1)S(1)}, bf16[256,512]{1,0:T(8,128)(2,1)S(1)}, u32[]{:S(2)}, u32[]{:S(2)}) %collective-permute-start.40) | collective-permute-done | bytes 262176 | tf_op jit(solution)/shard_map/ppermute | solution.py:386
  186.5 2.4 collective-permute-start.45
  188.9 6.9 %newton_att.1 = (bf16[128,512]{1,0:T(8,128)(2,1)S(1)}, bf16[128,512]{1,0:T(8,128)(2,1)S(1)}, bf16[128,512]{1,0:T(8,128)(2,1)S(1)}, bf16[128,512]{1,0:T(8,128)(2,1)S(1)}) custom-call(s32[2]{0:T(128)S(1)} %copy-done.17, bf16[1280,512]{1,0:T(8,128)(2,1)S(1)} %constant_dynamic-update-slice_fusion.own, bf16[1280,512]{1,0:T(8,128)(2,1)S(1)} %collective-permute-done.41.other), custom_call_target="tpu_custom_call" | custom-call | flops 4026531840 | bytes 3145728 | tf_op jit(solution)/shard_map/newton_att/pallas_call | solution.py:414
  195.8 3.8 %collective-permute-done.42.refs_1_ = bf16[256,512]{1,0:T(8,128)(2,1)S(1)} collective-permute-done((bf16[256,512]{1,0:T(8,128)(2,1)S(1)}, bf16[256,512]{1,0:T(8,128)(2,1)S(1)}, u32[]{:S(2)}, u32[]{:S(2)}) %collective-permute-start.42) | collective-permute-done | bytes 262176 | tf_op jit(solution)/shard_map/ppermute | solution.py:386
  199.6 8.2 %collective-permute-start.47 = (bf16[128,512]{1,0:T(8,128)(2,1)S(1)}, bf16[128,512]{1,0:T(8,128)(2,1)S(1)}, u32[]{:S(2)}, u32[]{:S(2)}) collective-permute-start(bf16[128,512]{1,0:T(8,128)(2,1)S(1)} %get-tuple-element.328), channel_id=1, source_target_pairs={{0,1},{1,0},{2,3},{3,2},{4,5},{5,4},{6,7},{7,6},{8,9},{9,8},{10,11... | collective-permute-start | bytes 393224 | tf_op jit(solution)/shard_map/ppermute | solution.py:386
  207.8 2.4 collective-permute-start.49
  210.2 14.1 %newton_ffn.1 = (bf16[256,512]{1,0:T(8,128)(2,1)S(1)}, bf16[256,512]{1,0:T(8,128)(2,1)S(1)}) custom-call(s32[2]{0:T(128)S(1)} %copy-done.17, bf16[1280,512]{1,0:T(8,128)(2,1)S(1)} %constant_dynamic-update-slice_fusion.own, bf16[1280,512]{1,0:T(8,128)(2,1)S(1)} %collective-permute-done.41.other), custom_call_target="tpu_custom_call" | custom-call | flops 12079595520 | bytes 3145728 | tf_op jit(solution)/shard_map/newton_ffn/pallas_call | solution.py:414
  231.7 2.2 att_final.1
  233.9 5.8 %collective-permute-done.44.far = bf16[256,512]{1,0:T(8,128)(2,1)S(1)} collective-permute-done((bf16[256,512]{1,0:T(8,128)(2,1)S(1)}, bf16[256,512]{1,0:T(8,128)(2,1)S(1)}, u32[]{:S(2)}, u32[]{:S(2)}) %collective-permute-start.44) | collective-permute-done | bytes 262176 | tf_op jit(solution)/shard_map/ppermute | solution.py:386
  (218 shorter events, 72.0 us)
Async XLA Ops:
  9.8 13.8 %collective-permute-start.8 = (bf16[144,512]{1,0:T(8,128)(2,1)}, bf16[144,512]{1,0:T(8,128)(2,1)S(1)}, u32[]{:S(2)}, u32[]{:S(2)}) collective-permute-start(bf16[144,512]{1,0:T(8,128)(2,1)} %get-tuple-element.204), channel_id=1, source_target_pairs={{0,3},{1,2},{2,1},{3,0},{4,7},{5,6},{6,5},{7,4},{8,11},{9,10},{10,... | collective-permute-start | bytes 442376 | tf_op jit(solution)/shard_map/ppermute | solution.py:386
  13.6 13.1 %collective-permute-start.7 = (bf16[144,512]{1,0:T(8,128)(2,1)}, bf16[144,512]{1,0:T(8,128)(2,1)S(1)}, u32[]{:S(2)}, u32[]{:S(2)}) collective-permute-start(bf16[144,512]{1,0:T(8,128)(2,1)} %get-tuple-element.204), channel_id=1, source_target_pairs={{0,2},{1,3},{2,0},{3,1},{4,6},{5,7},{6,4},{7,5},{8,10},{9,11},{10,... | collective-permute-start | bytes 442376 | tf_op jit(solution)/shard_map/ppermute | solution.py:386
  29.7 28.4 %collective-permute-start.12 = (bf16[4,144,512]{2,1,0:T(8,128)(2,1)S(1)}, bf16[4,144,512]{2,1,0:T(8,128)(2,1)}, u32[]{:S(2)}, u32[]{:S(2)}) collective-permute-start(bf16[4,144,512]{2,1,0:T(8,128)(2,1)S(1)} %pad_maximum_fusion.1.refs_7_), channel_id=1, source_target_pairs={{0,24},{4,28},{8,16},{12,20},{16,8},{20,12},{24,0},{28,4},{1,25},{... | collective-permute-start | bytes 1769480 | tf_op jit(solution)/shard_map/ppermute | solution.py:386
  31.7 27.4 %collective-permute-start.11 = (bf16[4,144,512]{2,1,0:T(8,128)(2,1)S(1)}, bf16[4,144,512]{2,1,0:T(8,128)(2,1)}, u32[]{:S(2)}, u32[]{:S(2)}) collective-permute-start(bf16[4,144,512]{2,1,0:T(8,128)(2,1)S(1)} %pad_maximum_fusion.1.refs_7_), channel_id=1, source_target_pairs={{0,16},{4,20},{8,24},{12,28},{16,0},{20,4},{24,8},{28,12},{1,17},{... | collective-permute-start | bytes 1769480 | tf_op jit(solution)/shard_map/ppermute | solution.py:386
  32.8 26.4 %collective-permute-start.10 = (bf16[4,144,512]{2,1,0:T(8,128)(2,1)S(1)}, bf16[4,144,512]{2,1,0:T(8,128)(2,1)}, u32[]{:S(2)}, u32[]{:S(2)}) collective-permute-start(bf16[4,144,512]{2,1,0:T(8,128)(2,1)S(1)} %pad_maximum_fusion.1.refs_7_), channel_id=1, source_target_pairs={{0,8},{4,12},{8,0},{12,4},{16,24},{20,28},{24,16},{28,20},{1,9},{5... | collective-permute-start | bytes 1769480 | tf_op jit(solution)/shard_map/ppermute | solution.py:386
  33.3 21.9 %collective-permute-start.14 = (bf16[256,512]{1,0:T(8,128)(2,1)S(1)}, bf16[256,512]{1,0:T(8,128)(2,1)S(1)}, u32[]{:S(2)}, u32[]{:S(2)}) collective-permute-start(bf16[256,512]{1,0:T(8,128)(2,1)S(1)} %get-tuple-element.217), channel_id=1, source_target_pairs={{0,2},{1,3},{2,0},{3,1},{4,6},{5,7},{6,4},{7,5},{8,10},{9,11},{10,... | collective-permute-start | bytes 786440 | tf_op jit(solution)/shard_map/ppermute | solution.py:386
  35.4 22.7 %collective-permute-start.15 = (bf16[256,512]{1,0:T(8,128)(2,1)S(1)}, bf16[256,512]{1,0:T(8,128)(2,1)S(1)}, u32[]{:S(2)}, u32[]{:S(2)}) collective-permute-start(bf16[256,512]{1,0:T(8,128)(2,1)S(1)} %get-tuple-element.218), channel_id=1, source_target_pairs={{0,3},{1,2},{2,1},{3,0},{4,7},{5,6},{6,5},{7,4},{8,11},{9,10},{10,... | collective-permute-start | bytes 786440 | tf_op jit(solution)/shard_map/ppermute | solution.py:386
  99.3 35.5 %collective-permute-start.25 = (bf16[256,512]{1,0:T(8,128)(2,1)}, bf16[256,512]{1,0:T(8,128)(2,1)S(1)}, u32[]{:S(2)}, u32[]{:S(2)}) collective-permute-start(bf16[256,512]{1,0:T(8,128)(2,1)} %get-tuple-element.263), channel_id=1, source_target_pairs={{0,2},{1,3},{2,0},{3,1},{4,6},{5,7},{6,4},{7,5},{8,10},{9,11},{10,... | collective-permute-start | bytes 786440 | tf_op jit(solution)/shard_map/ppermute | solution.py:386
  100.4 34.4 %collective-permute-start.26 = (bf16[256,512]{1,0:T(8,128)(2,1)}, bf16[256,512]{1,0:T(8,128)(2,1)S(1)}, u32[]{:S(2)}, u32[]{:S(2)}) collective-permute-start(bf16[256,512]{1,0:T(8,128)(2,1)} %get-tuple-element.264), channel_id=1, source_target_pairs={{0,3},{1,2},{2,1},{3,0},{4,7},{5,6},{6,5},{7,4},{8,11},{9,10},{10,... | collective-permute-start | bytes 786440 | tf_op jit(solution)/shard_map/ppermute | solution.py:386
  104.6 30.2 %collective-permute-start.22 = (bf16[528,512]{1,0:T(8,128)(2,1)S(1)}, bf16[528,512]{1,0:T(8,128)(2,1)S(1)}, u32[]{:S(2)}, u32[]{:S(2)}) collective-permute-start(bf16[528,512]{1,0:T(8,128)(2,1)S(1)} %get-tuple-element.260), channel_id=1, source_target_pairs={{0,8},{4,12},{8,0},{12,4},{16,24},{20,28},{24,16},{28,20},{1,9},{5... | collective-permute-start | bytes 1622024 | tf_op jit(solution)/shard_map/ppermute | solution.py:386
  106.2 28.6 %collective-permute-start.23 = (bf16[528,512]{1,0:T(8,128)(2,1)S(1)}, bf16[528,512]{1,0:T(8,128)(2,1)S(1)}, u32[]{:S(2)}, u32[]{:S(2)}) collective-permute-start(bf16[528,512]{1,0:T(8,128)(2,1)S(1)} %get-tuple-element.261), channel_id=1, source_target_pairs={{0,16},{4,20},{8,24},{12,28},{16,0},{20,4},{24,8},{28,12},{1,17},{... | collective-permute-start | bytes 1622024 | tf_op jit(solution)/shard_map/ppermute | solution.py:386
  107.7 27.1 %collective-permute-start.24 = (bf16[528,512]{1,0:T(8,128)(2,1)S(1)}, bf16[528,512]{1,0:T(8,128)(2,1)S(1)}, u32[]{:S(2)}, u32[]{:S(2)}) collective-permute-start(bf16[528,512]{1,0:T(8,128)(2,1)S(1)} %get-tuple-element.262), channel_id=1, source_target_pairs={{0,24},{4,28},{8,16},{12,20},{16,8},{20,12},{24,0},{28,4},{1,25},{... | collective-permute-start | bytes 1622024 | tf_op jit(solution)/shard_map/ppermute | solution.py:386
  136.0 15.9 %collective-permute-start.27 = (bf16[272,512]{1,0:T(8,128)(2,1)S(1)}, bf16[272,512]{1,0:T(8,128)(2,1)S(1)}, u32[]{:S(2)}, u32[]{:S(2)}) collective-permute-start(bf16[272,512]{1,0:T(8,128)(2,1)S(1)} %get-tuple-element.274), channel_id=1, source_target_pairs={{0,2},{1,3},{2,0},{3,1},{4,6},{5,7},{6,4},{7,5},{8,10},{9,11},{10,... | collective-permute-start | bytes 835592 | tf_op jit(solution)/shard_map/ppermute | solution.py:386
  141.2 13.4 %collective-permute-start.30 = (bf16[256,512]{1,0:T(8,128)(2,1)S(1)}, bf16[256,512]{1,0:T(8,128)(2,1)S(1)}, u32[]{:S(2)}, u32[]{:S(2)}) collective-permute-start(bf16[256,512]{1,0:T(8,128)(2,1)S(1)} %get-tuple-element.279), channel_id=1, source_target_pairs={{0,16},{4,20},{8,24},{12,28},{16,0},{20,4},{24,8},{28,12},{1,17},{... | collective-permute-start | bytes 786440 | tf_op jit(solution)/shard_map/ppermute | solution.py:386
  155.3 13.0 %collective-permute-start.33 = (bf16[272,512]{1,0:T(8,128)(2,1)S(1)}, bf16[272,512]{1,0:T(8,128)(2,1)S(1)}, u32[]{:S(2)}, u32[]{:S(2)}) collective-permute-start(bf16[272,512]{1,0:T(8,128)(2,1)S(1)} %ffn_far_sum.1.keep), channel_id=1, source_target_pairs={{0,1},{1,0},{2,3},{3,2},{4,5},{5,4},{6,7},{7,6},{8,9},{9,8},{10,11... | collective-permute-start | bytes 835592 | tf_op jit(solution)/shard_map/ppermute | solution.py:386
  168.9 13.9 %collective-permute-start.39 = (bf16[320,512]{1,0:T(8,128)(2,1)S(1)}, bf16[320,512]{1,0:T(8,128)(2,1)S(1)}, u32[]{:S(2)}, u32[]{:S(2)}) collective-permute-start(bf16[320,512]{1,0:T(8,128)(2,1)S(1)} %get-tuple-element.303), channel_id=1, source_target_pairs={{0,24},{4,28},{8,16},{12,20},{16,8},{20,12},{24,0},{28,4},{1,25},{... | collective-permute-start | bytes 983048 | tf_op jit(solution)/shard_map/ppermute | solution.py:386
  170.4 14.0 %collective-permute-start.38 = (bf16[320,512]{1,0:T(8,128)(2,1)S(1)}, bf16[320,512]{1,0:T(8,128)(2,1)S(1)}, u32[]{:S(2)}, u32[]{:S(2)}) collective-permute-start(bf16[320,512]{1,0:T(8,128)(2,1)S(1)} %get-tuple-element.303), channel_id=1, source_target_pairs={{0,16},{4,20},{8,24},{12,28},{16,0},{20,4},{24,8},{28,12},{1,17},{... | collective-permute-start | bytes 983048 | tf_op jit(solution)/shard_map/ppermute | solution.py:386
  185.4 14.3 %collective-permute-start.42 = (bf16[256,512]{1,0:T(8,128)(2,1)S(1)}, bf16[256,512]{1,0:T(8,128)(2,1)S(1)}, u32[]{:S(2)}, u32[]{:S(2)}) collective-permute-start(bf16[256,512]{1,0:T(8,128)(2,1)S(1)} %copy-done.32), channel_id=1, source_target_pairs={{0,1},{1,0},{2,3},{3,2},{4,5},{5,4},{6,7},{7,6},{8,9},{9,8},{10,11... | collective-permute-start | bytes 786440 | tf_op jit(solution)/shard_map/ppermute | solution.py:386
  185.5 14.2 %collective-permute-start.43 = (bf16[256,512]{1,0:T(8,128)(2,1)S(1)}, bf16[256,512]{1,0:T(8,128)(2,1)S(1)}, u32[]{:S(2)}, u32[]{:S(2)}) collective-permute-start(bf16[256,512]{1,0:T(8,128)(2,1)S(1)} %copy-done.31), channel_id=1, source_target_pairs={{0,3},{1,2},{2,1},{3,0},{4,7},{5,6},{6,5},{7,4},{8,11},{9,10},{10,... | collective-permute-start | bytes 786440 | tf_op jit(solution)/shard_map/ppermute | solution.py:386
  186.5 37.9 %collective-permute-start.45 = (bf16[256,512]{1,0:T(8,128)(2,1)S(1)}, bf16[256,512]{1,0:T(8,128)(2,1)S(1)}, u32[]{:S(2)}, u32[]{:S(2)}) collective-permute-start(bf16[256,512]{1,0:T(8,128)(2,1)S(1)} %momentum_rows.1), channel_id=1, source_target_pairs={{0,2},{1,3},{2,0},{3,1},{4,6},{5,7},{6,4},{7,5},{8,10},{9,11},{10,... | collective-permute-start | bytes 786440 | tf_op jit(solution)/shard_map/ppermute | solution.py:386
  199.6 24.6 %collective-permute-start.47 = (bf16[128,512]{1,0:T(8,128)(2,1)S(1)}, bf16[128,512]{1,0:T(8,128)(2,1)S(1)}, u32[]{:S(2)}, u32[]{:S(2)}) collective-permute-start(bf16[128,512]{1,0:T(8,128)(2,1)S(1)} %get-tuple-element.328), channel_id=1, source_target_pairs={{0,1},{1,0},{2,3},{3,2},{4,5},{5,4},{6,7},{7,6},{8,9},{9,8},{10,11... | collective-permute-start | bytes 393224 | tf_op jit(solution)/shard_map/ppermute | solution.py:386
  207.8 16.4 %collective-permute-start.48 = (bf16[128,512]{1,0:T(8,128)(2,1)S(1)}, bf16[128,512]{1,0:T(8,128)(2,1)S(1)}, u32[]{:S(2)}, u32[]{:S(2)}) collective-permute-start(bf16[128,512]{1,0:T(8,128)(2,1)S(1)} %get-tuple-element.329), channel_id=1, source_target_pairs={{0,2},{1,3},{2,0},{3,1},{4,6},{5,7},{6,4},{7,5},{8,10},{9,11},{10,... | collective-permute-start | bytes 393224 | tf_op jit(solution)/shard_map/ppermute | solution.py:386
  207.8 16.5 %collective-permute-start.49 = (bf16[128,512]{1,0:T(8,128)(2,1)S(1)}, bf16[128,512]{1,0:T(8,128)(2,1)S(1)}, u32[]{:S(2)}, u32[]{:S(2)}) collective-permute-start(bf16[128,512]{1,0:T(8,128)(2,1)S(1)} %get-tuple-element.330), channel_id=1, source_target_pairs={{0,3},{1,2},{2,1},{3,0},{4,7},{5,6},{6,5},{7,4},{8,11},{9,10},{10,... | collective-permute-start | bytes 393224 | tf_op jit(solution)/shard_map/ppermute | solution.py:386
  224.9 14.8 %collective-permute-start.44 = (bf16[256,512]{1,0:T(8,128)(2,1)S(1)}, bf16[256,512]{1,0:T(8,128)(2,1)S(1)}, u32[]{:S(2)}, u32[]{:S(2)}) collective-permute-start(bf16[256,512]{1,0:T(8,128)(2,1)S(1)} %get-tuple-element.316), channel_id=1, source_target_pairs={{0,2},{1,3},{2,0},{3,1},{4,6},{5,7},{6,4},{7,5},{8,10},{9,11},{10,... | collective-permute-start | bytes 786440 | tf_op jit(solution)/shard_map/ppermute | solution.py:386
  (67 other events, 643.1 us)
